TPU v7x, 256 devices: a whole 4x4x8 slice. The times are simulated.
256 devices in a mesh: cache: 4 (over y), ctx: 32 (over z, x), head: 2 (over core).
Axes of the slice: x: 4, y: 4, z: 8, core: 2. Of those that a mesh axis runs over, the one named last changes fastest.
Arguments:
- conv_out: bfloat16 [8, 2048, 16384], P('cache', 'ctx', 'head'), may hold values from -6 to 6
- dt_low: bfloat16 [8, 2048, 512], P('cache', 'ctx'), may hold values from -6 to 6
- state_proj: float32 [8, 2048, 32], P('cache', 'ctx'), may hold values from -1.2 to 1.2
- dt_weight: bfloat16 [512, 16384], P('ctx', 'head'), may hold values from -0.25 to 0.25
- dt_bias: float32 [16384], P('head'), may hold values from -2.5 to -0.5
- decay_rate: float32 [16, 16384], P(None, 'head'), may hold values from 0.0003 to 0.15
- skip_gain: float32 [16384], P('head'), may hold values from 0.5 to 1.5
- cache_states: bfloat16 [256, 2, 16, 8192], P('cache', 'head', None, 'ctx'), may hold values from -10 to 10
- hit_owner: int32 [8, 1], replicated, may hold values from 0 to 3; in each aligned block of 2 rows (0 to 1, 2 to 3, ...) at most 2 rows name the same one
- hit_slot: int32 [8], replicated, may hold values from 0 to 63
- evict_order: int32 [4, 64], P('cache'), may hold values from 0 to 63, each once within a row
- new_lengths: int32 [8], replicated, may hold values from 1 to 2048, 10240 in all
Outputs:
- mixed_out: bfloat16 [8, 2048, 16384], P('cache', 'ctx', 'head')
- new_cache: bfloat16 [256, 2, 16, 8192], P('cache', 'head', None, 'ctx')
Inputs may be any that keep to these rules, and one draw needn't show every extreme that they name: `hit_owner`: among the 2 requests of one index of cache (aligned blocks of 2), no owner is named more than 2 times. `evict_order`: each row holds every slot number once. `new_lengths`: the longest request has exactly 2048 new positions.
All inputs are finite; a program needn't handle non-finite values.
Results may differ from a plain program's by a relative error of at most 0.0085.
Values may be sent and summed in bfloat16 or wider, within the bound.
No kernel may reach another device: no remote copies, remote signals or barrier semaphores. Data moves between devices by JAX's collectives and lax.ppermute only.
A program may use at most 192 MiB of HBM per device.

v0:
```python
import jax
import jax.numpy as jnp
from jax import lax
from jax.sharding import PartitionSpec as P


def entering(value, axis, join, neutral):
    count, mine = (lax.axis_size(axis), lax.axis_index(axis))
    pieces = jax.tree.map(lambda part: lax.all_gather(part, axis), value)
    running = jax.tree.map(
        lambda part, zero: jnp.full_like(part, 0) + jnp.asarray(zero, part.dtype), value, neutral
    )

    def turn(position, running):
        longer = join(running, jax.tree.map(lambda part: part[position], pieces))
        return jax.tree.map(lambda new, old: jnp.where(position < mine, new, old), longer, running)

    return lax.fori_loop(0, count - 1, turn, running)


def broadcast(value, axis, source):
    kept = jnp.where(lax.axis_index(axis) == source, value, 0).astype(value.dtype)
    return lax.psum(kept, axis)


def combine_pairs(first_part, second_part):
    return (first_part[0] * second_part[0], second_part[0] * first_part[1] + second_part[1])


def run_tokens(
    start_state, step_major, x_major, proj_major, live_major, decay_rate, skip_gain, emit_rows
):
    state_dim = decay_rate.shape[0]

    def advance(carried, inputs):
        step_now, token_x, proj_now, live_now = inputs
        wide_x = token_x.astype(jnp.float32)
        decay_now = jnp.exp(-step_now[:, None, :] * decay_rate[None, :, :])
        carried = (
            decay_now * carried + proj_now[:, :state_dim, None] * (step_now * wide_x)[:, None, :]
        )
        if emit_rows:
            output_row = (
                jnp.einsum(
                    "rn,rnc->rc", proj_now[:, state_dim:], carried, precision=lax.Precision.HIGHEST
                )
                + skip_gain[None, :] * wide_x
            )
            return (carried, jnp.where(live_now[:, None], output_row, 0.0).astype(jnp.bfloat16))
        return (carried, None)

    return lax.scan(advance, start_state, (step_major, x_major, proj_major, live_major), unroll=8)


def on_device(
    conv_out,
    dt_low,
    state_proj,
    dt_weight,
    dt_bias,
    decay_rate,
    skip_gain,
    cache_states,
    hit_owner,
    hit_slot,
    evict_order,
    new_lengths,
):
    groups = lax.axis_size("cache")
    group_here = lax.axis_index("cache")
    ctx_count = lax.axis_size("ctx")
    ctx_here = lax.axis_index("ctx")
    req_dev = conv_out.shape[0]
    tok_dev = conv_out.shape[1]
    state_dim = decay_rate.shape[0]
    piece_width = cache_states.shape[3]
    slot_count = cache_states.shape[0]
    most_per = max(2, req_dev // 2)
    owners = hit_owner[:, 0]
    request_count = owners.shape[0]
    request_ids = jnp.arange(request_count, dtype=jnp.int32)
    group_of = request_ids // req_dev
    same_owner = owners[:, None] == owners[None, :]
    earlier_req = request_ids[None, :] < request_ids[:, None]
    same_group = group_of[:, None] == group_of[None, :]
    global_rank = jnp.sum(same_owner & earlier_req, axis=1)
    local_rank = jnp.sum(same_owner & earlier_req & same_group, axis=1)
    group_ids = jnp.arange(groups, dtype=jnp.int32)
    rank_ids = jnp.arange(most_per, dtype=jnp.int32)
    slot_ids = jnp.arange(slot_count, dtype=jnp.int32)
    group_hot = (group_of[:, None] == group_ids[None, :]).astype(jnp.float32)
    rank_hot = (local_rank[:, None] == rank_ids[None, :]).astype(jnp.float32)
    owned_here = (owners == group_here).astype(jnp.float32)
    route_hot = jnp.einsum("rg,rm->rgm", group_hot * owned_here[:, None], rank_hot).reshape(
        request_count, groups * most_per
    )
    slot_hot = (hit_slot[:, None] == slot_ids[None, :]).astype(jnp.bfloat16)
    pick_read = jnp.dot(
        route_hot.T.astype(jnp.bfloat16), slot_hot, preferred_element_type=jnp.float32
    ).astype(jnp.bfloat16)
    stored = cache_states.reshape(slot_count, -1)
    outgoing = jnp.dot(pick_read, stored, preferred_element_type=jnp.float32).astype(jnp.bfloat16)
    outgoing = outgoing.reshape(groups, most_per, state_dim, piece_width)
    incoming = lax.all_to_all(outgoing, "cache", split_axis=0, concat_axis=0, tiled=True)
    first_req = group_here * req_dev
    my_owner = lax.dynamic_slice_in_dim(owners, first_req, req_dev)
    my_rank = lax.dynamic_slice_in_dim(local_rank, first_req, req_dev)
    my_lengths = lax.dynamic_slice_in_dim(new_lengths, first_req, req_dev)
    choose = (my_owner[:, None, None] == group_ids[None, :, None]) & (
        my_rank[:, None, None] == rank_ids[None, None, :]
    )
    choose = choose.reshape(req_dev, groups * most_per).astype(jnp.bfloat16)
    seed_piece = jnp.dot(
        choose, incoming.reshape(groups * most_per, -1), preferred_element_type=jnp.float32
    )
    seed_piece = seed_piece.astype(jnp.bfloat16).reshape(req_dev, state_dim, piece_width)
    weights, seed_full = (
        lax.all_gather(dt_weight, "ctx", axis=0, tiled=True),
        lax.all_gather(seed_piece, "ctx", axis=2, tiled=True),
    )
    positions = ctx_here * tok_dev + jnp.arange(tok_dev, dtype=jnp.int32)
    live_major = positions[:, None] < my_lengths[None, :]
    pre_rate = jnp.einsum("rtk,kc->trc", dt_low, weights, preferred_element_type=jnp.float32)
    step_major = jnp.where(
        live_major[:, :, None], jax.nn.softplus(pre_rate + dt_bias[None, None, :]), 0.0
    )
    x_major = jnp.swapaxes(conv_out, 0, 1)
    proj_major = jnp.swapaxes(state_proj, 0, 1)
    zero_state = jnp.zeros((req_dev, state_dim, conv_out.shape[2]), jnp.float32)
    local_end = run_tokens(
        zero_state, step_major, x_major, proj_major, live_major, decay_rate, skip_gain, False
    )[0]
    step_total = jnp.sum(step_major, axis=0)
    seed_wide = seed_full.astype(jnp.float32)
    block_decay = jnp.exp(-step_total[:, None, :] * decay_rate[None, :, :])
    prior_decay, prior_state = entering(
        (block_decay, local_end),
        "ctx",
        combine_pairs,
        (jnp.ones_like(local_end), jnp.zeros_like(local_end)),
    )
    carry_in = prior_decay * seed_wide + prior_state
    final_end, outputs = run_tokens(
        carry_in, step_major, x_major, proj_major, live_major, decay_rate, skip_gain, True
    )
    mixed_out = jnp.swapaxes(outputs, 0, 1)
    last_whole = broadcast(final_end.astype(jnp.bfloat16), "ctx", ctx_count - 1)
    new_piece = lax.dynamic_slice_in_dim(last_whole, ctx_here * piece_width, piece_width, 2)
    leaving = jnp.dot(choose.T, new_piece.reshape(req_dev, -1), preferred_element_type=jnp.float32)
    leaving = leaving.astype(jnp.bfloat16).reshape(groups, most_per, state_dim, piece_width)
    arrived = lax.all_to_all(leaving, "cache", split_axis=0, concat_axis=0, tiled=True)
    rank_full = (global_rank[:, None] == slot_ids[None, :]).astype(jnp.float32)
    order_hot = (evict_order[0][:, None] == slot_ids[None, :]).astype(jnp.float32)
    target_hot = jnp.dot(rank_full, order_hot)
    place_hot = jnp.dot(route_hot.T, target_hot)
    written = jnp.sum(place_hot, axis=0) > 0.5
    fresh_rows = jnp.dot(
        place_hot.T.astype(jnp.bfloat16),
        arrived.reshape(groups * most_per, -1),
        preferred_element_type=jnp.float32,
    ).astype(jnp.bfloat16)
    updated = jnp.where(written[:, None], fresh_rows, stored).reshape(cache_states.shape)
    return (mixed_out, updated)


def solution(mesh):
    in_specs = (
        P("cache", "ctx", "head"),
        P("cache", "ctx", None),
        P("cache", "ctx", None),
        P("ctx", "head"),
        P("head"),
        P(None, "head"),
        P("head"),
        P("cache", "head", None, "ctx"),
        P(),
        P(),
        P("cache", None),
        P(),
    )
    out_specs = (P("cache", "ctx", "head"), P("cache", "head", None, "ctx"))
    return jax.shard_map(
        on_device, mesh=mesh, in_specs=in_specs, out_specs=out_specs, check_vma=False
    )
```

profile of v0, /device:TPU:8, one launch (start us, length us, event | category | flops | bytes accessed | tf_op | source)
XLA Modules:
  0.0 1048.9 jit_solution(14456230331669557244)
XLA Ops:
  8.0 3.8 copy.27
  12.7 99.2 %all-gather.5.cloned.1.call-done = bf16[512,8192]{1,0:T(8,128)(2,1)} async-done(((bf16[16,8192]{1,0:T(8,128)(2,1)}), bf16[512,8192]{1,0:T(8,128)(2,1)}) %all-gather.5.cloned.1.call-update) | async-done | bytes 8388624 | tf_op jit(solution)/shard_map/all_gather | solution.py:118
  111.9 7.9 fusion.115
  119.8 5.2 copy.28
  125.0 57.3 %while.40 = (s32[]{:T(128)}, f32[2,16,8192]{2,1,0:T(8,128)}, f32[8,8,2,8192]{3,2,1,0:T(2,128)}, f32[16,8192]{1,0:T(8,128)S(1)}, f32[8,8,2,32]{3,2,1,0:T(2,128)},...) while((s32[]{:T(128)}, f32[2,16,8192]{2,1,0:T(8,128)}, ...), condition=%wide.region_2.3_spmd.clone, body=%wide.region_1.2_spmd.clone.sunk | while | flops 9043978 | bytes 5510443 | solution.py:52
  128.6 3.5 fusion.189
  135.6 3.6 fusion.189
  142.8 3.6 fusion.189
  150.0 3.6 fusion.189
  157.2 3.6 fusion.189
  164.4 3.6 fusion.189
  171.5 3.6 fusion.189
  178.7 3.6 fusion.189
  187.3 4.8 all-to-all-start
  192.7 3.6 all-to-all-done
  196.5 46.9 %all_gather.20 = bf16[2,16,8192]{2,1,0:T(8,128)(2,1)} all-gather(bf16[2,16,256]{2,1,0:T(8,128)(2,1)S(1)} %bitcast.490), channel_id=1, replica_groups=mesh['cache'=4,'ctx'=32,'head'=2] {'ctx'}, dimensions={2}, use_global_device_ids=true | all-gather | bytes 540672 | tf_op jit(solution)/shard_map/all_gather | solution.py:119
  243.4 174.4 %all-gather.9.cloned.1.call-done = f32[64,16,8192]{2,1,0:T(8,128)} async-done(((f32[2,16,8192]{2,1,0:T(8,128)}), f32[64,16,8192]{2,1,0:T(8,128)}) %all-gather.9.cloned.1.call-update) | async-done | bytes 33554448 | tf_op jit(solution)/shard_map/all_gather | solution.py:9
  417.8 233.0 %all-gather.7.cloned.1.call-done = f32[32,2,16,8192]{3,2,1,0:T(8,128)} async-done(((f32[1,2,16,8192]{3,2,1,0:T(8,128)}), f32[32,2,16,8192]{3,2,1,0:T(8,128)}) %all-gather.7.cloned.1.call-update) | async-done | bytes 33554448 | tf_op jit(solution)/shard_map/all_gather | solution.py:9
  650.8 71.6 %while.41 = (s32[]{:T(128)}, f32[2,16,8192]{2,1,0:T(8,128)S(1)}, f32[2,16,8192]{2,1,0:T(8,128)S(1)}, s32[]{:T(128)}, f32[32,2,16,8192]{3,2,1,0:T(8,128)}, /*index=5*/f32[32,2,16,8192]{3,2,1,0:T(8,128)}, s32[]{:T(128)}, s32[]{:T(128)}) while((s32[]{:T(128)}, f32[2,16,8192]{2,1,0:T(8,128)S(1)}, f32[2,16,8192]{2,1,0:T(8,128)S(1)}, ...), condition=%wide.region_4.5_spmd.clone, body=%wide.region_3.4_spmd.clone.sunk | while | flops 1835012 | bytes 6291565 | solution.py:18
  650.8 2.3 fusion.190
  653.1 2.3 fusion.190
  660.0 2.3 fusion.190
  667.0 2.3 fusion.190
  671.6 2.3 fusion.190
  678.5 2.3 fusion.190
  685.4 2.3 fusion.190
  690.1 2.3 fusion.190
  692.4 2.3 fusion.190
  724.9 160.1 %while.39 = (s32[]{:T(128)}, f32[2,16,8192]{2,1,0:T(8,128)S(1)}, bf16[8,8,2,8192]{3,1,0,2:T(8,128)(2,1)}, f32[8,8,2,8192]{3,2,1,0:T(2,128)}, f32[16,8192]{1,0:T(...) while((s32[]{:T(128)}, f32[2,16,8192]{2,1,0:T(8,128)S(1)}, ...), condition=%wide.region_7.8_spmd, body=%wide.region_6.7_spmd.sunk | while | flops 47185928 | bytes 22036412 | solution.py:52
  886.2 144.3 %all-reduce.2.cloned.1.call-done = bf16[2,16,8192]{2,1,0:T(8,128)(2,1)} async-done(((bf16[2,16,8192]{2,1,0:T(8,128)(2,1)}), bf16[2,16,8192]{2,1,0:T(8,128)(2,1)}) %all-reduce.2.cloned.1.call-update) | async-done | bytes 524304 | tf_op jit(solution)/shard_map/psum | solution.py:23
  1032.2 4.8 all-to-all-start.1
  1037.0 4.2 all-to-all-done.1
  (323 shorter events, 251.9 us)
Async XLA Ops:
  7.2 104.7 %copy-start = (bf16[2,64,512]{2,1,0:T(8,128)(2,1)S(1)}, bf16[2,64,512]{2,1,0:T(8,128)(2,1)}, u32[]{:S(2)}) copy-start(bf16[2,64,512]{2,1,0:T(8,128)(2,1)} %param.19) | copy-start | bytes 393220
  7.2 4.6 copy-start.6
  7.2 5.3 copy-start.12
  7.2 104.7 %copy-start.11 = (f32[8192]{0:T(1024)S(1)}, f32[8192]{0:T(1024)}, u32[]{:S(2)}) copy-start(f32[8192]{0:T(1024)} %param.22) | copy-start | bytes 98308
  7.2 104.6 %all-gather.5.cloned.1.call-start = ((), (), s32[]{:S(2)}) async-start(), calls=%async_computation.2 | async-start | bytes 8650752 | tf_op jit(solution)/shard_map/all_gather | solution.py:118
  7.9 409.9 %all-gather.9.cloned.1.call-start = ((), (), s32[]{:S(2)}) async-start(), calls=%async_computation.5 | async-start | bytes 34603008 | tf_op jit(solution)/shard_map/all_gather | solution.py:9
  12.6 107.2 %copy-start.8 = (s32[2]{0:T(128)}, s32[2]{0:T(128)S(1)}, u32[]{:S(2)}) copy-start(s32[2]{0:T(128)S(1)} %dynamic_slice.53) | copy-start | bytes 28
  119.8 5.2 copy-start.2
  182.3 10.2 copy-start.5
  182.3 3.7 copy-start.7
  182.3 4.0 copy-start.10
  182.4 10.1 copy-start.9
  182.4 468.4 %all-gather.7.cloned.1.call-start = ((), (), s32[]{:S(2)}) async-start(), calls=%async_computation.3 | async-start | bytes 34603008 | tf_op jit(solution)/shard_map/all_gather | solution.py:9
  187.3 9.0 all-to-all-start
  192.1 838.4 %all-reduce.2.cloned.1.call-start = ((), (), s32[]{:S(2)}) async-start(), calls=%async_computation.4 | async-start | bytes 1048576 | tf_op jit(solution)/shard_map/psum | solution.py:23
  650.8 74.1 %copy-start.3 = (f32[8192]{0:T(1024)S(1)}, f32[8192]{0:T(1024)}, u32[]{:S(2)}) copy-start(f32[8192]{0:T(1024)} %param.24) | copy-start | bytes 98308
  722.4 1.0 copy-start.4
  724.9 161.0 %copy-start.13 = (s32[1,64]{1,0:T(1,128)S(1)}, s32[1,64]{1,0:T(1,128)}, u32[]{:S(2)}) copy-start(s32[1,64]{1,0:T(1,128)} %param.28) | copy-start | bytes 772
  885.0 157.4 %copy-start.1 = (bf16[2,64,512]{2,1,0:T(8,128)(2,1)S(1)}, bf16[2,64,512]{2,1,0:T(8,128)(2,1)}, u32[]{:S(2)}) copy-start(bf16[2,64,512]{2,1,0:T(8,128)(2,1)} %param.19) | copy-start | bytes 393220
  1032.2 9.0 all-to-all-start.1
Sparse Core Ops, SparseCore 0:
  10.6 101.1 all-gather.4
  182.5 235.2 all-gather.8
  420.4 230.3 all-gather.6
  886.0 144.5 all-reduce.1
where the time goes:
time: 1060 us; the launch traced here: 1050 us
  waiting for transfers between devices  659 us (62%)
  other arithmetic  206 us (19%)
  matrix products  70.2 us (7%)
  blocking collectives  46.9 us (4%)
  local copies, waits for them, and re-layouts  40.7 us (4%)
  between operations  14 us (1%)
    all_gather x2, waiting for transfers between devices, entering(): pieces = jax.tree.map(lambda part: lax.all_gather(part, axis), value)  407 us
    psum x1, waiting for transfers between devices, broadcast(): return lax.psum(kept, axis)  144 us
    all_gather x1, waiting for transfers between devices, on_device(): lax.all_gather(dt_weight, 'ctx', axis=0, tiled=True)  99.2 us
    select_n x31, other arithmetic, turn(): jnp.where(position < mine, new, old)  70.9 us
    dot_general x64, matrix products, advance(): jnp.einsum('rn,rnc->rc', proj_now[:, state_dim:], carried, precision=lax....  61 us
    while x56, other arithmetic  48.4 us
    all_gather x1, blocking collectives, on_device(): lax.all_gather(seed_piece, 'ctx', axis=2, tiled=True)  46.9 us
    add x16, other arithmetic, advance(): decay_now * carried  43.1 us
  transfers between devices with their start and end apart: 6, of which 6 were waited for; matrix products, arithmetic and copies ran while one was open for 1% of the time, Pallas kernels for 0%

commit v1 on v0

v1 whole, which is shorter than its diff:
```python
import math

import jax
import jax.numpy as jnp
from jax import lax
from jax.experimental import pallas as pl
from jax.experimental.pallas import tpu as pltpu
from jax.sharding import Mesh, PartitionSpec as P

HI, LO = 4, 8
LANES, ROWS = 128, 8
LOG2E = math.log2(math.e)


def scan_kernel(
    place_ref, proj_ref, x_ref, dt_ref, w_ref, bias_ref, decay_ref, skip_ref, start_ref,
    y_ref, total_ref, end_ref, step_scr, x_scr,
):
    parts, reqs, toks, chans = x_ref.shape
    states = decay_ref.shape[0]
    rows = reqs * toks
    nbc = proj_ref.shape[0] // (parts * rows)

    def project(part, carry):
        wide_x = x_ref[part].reshape(rows, chans).astype(jnp.float32)
        pre = jnp.dot(
            dt_ref[part].reshape(rows, -1), w_ref[...], preferred_element_type=jnp.float32
        )
        pre = pre + bias_ref[...]
        row = lax.broadcasted_iota(jnp.int32, (rows, 1), 0)
        position = place_ref[0] + part * toks + jnp.where(row < toks, row, row - toks)
        limit = jnp.where(row < toks, place_ref[1], place_ref[2])
        step = jnp.maximum(pre, 0.0) + jnp.log1p(jnp.exp(-jnp.abs(pre)))
        step = jnp.where(position < limit, step, 0.0)
        for k in range(ROWS):
            at = pl.ds(part * (rows * ROWS) + k, rows, stride=ROWS)
            step_scr[at, :] = step[:, k * LANES : (k + 1) * LANES]
            x_scr[at, :] = wide_x[:, k * LANES : (k + 1) * LANES]
        return carry

    lax.fori_loop(0, parts, project, 0)

    skip = skip_ref[...]
    for req in range(reqs):

        def per_part(part, carried, req=req):
            def per_tok(tok, carried):
                total, held = carried
                row = (part * reqs + req) * toks + tok
                at = pl.ds(pl.multiple_of(row * ROWS, ROWS), ROWS)
                step = step_scr[at, :]
                wide_x = x_scr[at, :]
                driven = step * wide_x
                total = total + step
                out = skip * wide_x
                new = []
                for n in range(states):
                    decay = jnp.exp2(step * decay_ref[n])
                    state = decay * held[n] + proj_ref[row * nbc + n] * driven
                    out = out + proj_ref[row * nbc + states + n] * state
                    new.append(state)
                total_ref[at, :] = total
                y_ref[at, :] = out
                return total, tuple(new)

            return lax.fori_loop(0, toks, per_tok, carried, unroll=4)

        held = tuple(start_ref[req, n] for n in range(states))
        total, held = lax.fori_loop(0, parts, per_part, (jnp.zeros((ROWS, LANES), jnp.float32), held))
        for n in range(states):
            end_ref[req, n] = held[n]
        end_ref[req, states] = total


def correct_kernel(
    place_ref, proj_ref, y_ref, total_ref, decay_ref, carry_ref, out_ref, y_scr,
):
    parts, reqs, toks, chans = out_ref.shape
    states = decay_ref.shape[0]
    rows = reqs * toks
    nbc = proj_ref.shape[0] // (parts * rows)

    def per_part(part, done):
        for req in range(reqs):
            carry = [carry_ref[req, n] for n in range(states)]

            def per_tok(tok, done, req=req, carry=carry):
                row = (part * reqs + req) * toks + tok
                at = pl.ds(pl.multiple_of(row * ROWS, ROWS), ROWS)
                total = total_ref[at, :]
                out = y_ref[at, :]
                for n in range(states):
                    out = out + proj_ref[row * nbc + states + n] * (
                        jnp.exp2(total * decay_ref[n]) * carry[n]
                    )
                y_scr[pl.ds(pl.multiple_of((req * toks + tok) * ROWS, ROWS), ROWS), :] = out
                return done

            lax.fori_loop(0, toks, per_tok, 0, unroll=4)
            tok = lax.broadcasted_iota(jnp.int32, (toks, 1), 0)
            live = place_ref[0] + part * toks + tok < place_ref[1 + req]
            for k in range(ROWS):
                block = y_scr[pl.ds(req * toks * ROWS + k, toks, stride=ROWS), :]
                out_ref[part, req, :, k * LANES : (k + 1) * LANES] = jnp.where(
                    live, block, 0.0
                ).astype(jnp.bfloat16)
        return done

    lax.fori_loop(0, parts, per_part, 0)


def shifts(count, by):
    return [(i, (i + by) % count) for i in range(count)]


def halves(array):
    top = lax.reduce_precision(array, 8, 7)
    return top.astype(jnp.bfloat16), (array - top).astype(jnp.bfloat16)


def on_device(
    conv_out, dt_low, state_proj, dt_weight, dt_bias, decay_rate, skip_gain,
    cache_states, hit_owner, hit_slot, evict_order, new_lengths,
):
    groups = lax.axis_size("cache")
    group = lax.axis_index("cache")
    hi = lax.axis_index("hi")
    lo = lax.axis_index("lo")
    reqs, toks, width = conv_out.shape
    rank = dt_low.shape[2]
    states = decay_rate.shape[0]
    nbc = state_proj.shape[2]
    slots, piece = cache_states.shape[0], cache_states.shape[3]
    chans = width // LO
    owners = hit_owner[:, 0]
    count = owners.shape[0]
    stored = cache_states.reshape(slots, states, piece)

    mine = dt_weight.shape[0] // groups
    quarter = lax.dynamic_slice_in_dim(dt_weight, group * mine, mine, 0)
    quarter = quarter.reshape(mine, HI, LO, piece).transpose(2, 0, 1, 3).reshape(LO, mine, chans)
    quarter = jnp.broadcast_to(quarter[None], (HI, LO, mine, chans)).reshape(HI * LO, mine, chans)
    quarter = lax.all_to_all(quarter, ("hi", "lo"), split_axis=0, concat_axis=0, tiled=True)
    quarter = quarter.reshape(rank // groups, chans)
    pieces = [quarter] + [
        lax.ppermute(quarter, "cache", shifts(groups, by)) for by in range(1, groups)
    ]

    slot_rows = jnp.where(owners == group, hit_slot, 0)
    picked = jnp.stack(
        [lax.dynamic_index_in_dim(stored, slot_rows[r], 0, keepdims=False) for r in range(count)]
    )
    picked = jnp.where((owners == group)[:, None, None], picked, 0).astype(jnp.bfloat16)
    picked = lax.all_to_all(picked, "cache", split_axis=0, concat_axis=0, tiled=True)
    seed = jnp.sum(
        picked.reshape(groups, reqs, states, piece).astype(jnp.float32), axis=0
    ).astype(jnp.bfloat16)
    seeds = [seed] + [lax.ppermute(seed, "hi", [(by, 0)]) for by in range(1, HI)]
    start = jnp.stack(seeds, axis=2).reshape(reqs, states, ROWS, LANES).astype(jnp.float32)
    start = jnp.where(hi == 0, start, 0.0)

    sent_x = conv_out.reshape(reqs, toks, HI, LO, piece).transpose(3, 0, 1, 2, 4)
    sent_x = sent_x.reshape(LO, reqs, toks, chans)
    dt_sorted = dt_low.reshape(reqs, toks, HI * LO, groups, mine).transpose(0, 1, 3, 2, 4)
    dt_sorted = dt_sorted.reshape(reqs, toks, rank)
    coarse, fine = halves(state_proj)
    shared = jnp.concatenate(
        [dt_sorted, coarse, fine, jnp.zeros((reqs, toks, LANES - 2 * nbc), jnp.bfloat16)], axis=2
    )
    shared = jnp.broadcast_to(shared[None], (LO,) + shared.shape)
    got = lax.all_to_all(
        jnp.concatenate([sent_x, shared], axis=3), "lo", split_axis=0, concat_axis=0, tiled=True
    )
    x_here = got[..., :chans]
    dt_here = got[..., chans : chans + rank]
    proj = got[..., chans + rank : chans + rank + nbc].astype(jnp.float32) + got[
        ..., chans + rank + nbc : chans + rank + 2 * nbc
    ].astype(jnp.float32)
    proj = proj.reshape(-1)

    weights = jnp.zeros((groups, rank // groups, chans), jnp.bfloat16)
    for by in range(groups):
        weights = lax.dynamic_update_slice_in_dim(
            weights, pieces[by][None], lax.rem(group - by + groups, groups), 0
        )
    weights = weights.reshape(rank, chans)

    def own_channels(array):
        lead = array.shape[:-1]
        array = array.reshape(lead + (HI, LO, piece))
        return lax.dynamic_index_in_dim(array, lo, len(lead) + 1, keepdims=False)

    bias = own_channels(dt_bias).reshape(1, chans)
    decay = own_channels(decay_rate).reshape(states, ROWS, LANES) * (-LOG2E)
    skip = own_channels(skip_gain).reshape(ROWS, LANES)
    lengths = lax.dynamic_slice_in_dim(new_lengths, group * reqs, reqs)
    place = jnp.concatenate([(hi * (LO * toks))[None].astype(jnp.int32), lengths])

    all_rows = LO * reqs * toks * ROWS
    smem = pl.BlockSpec(memory_space=pltpu.SMEM)
    vmem = pl.BlockSpec(memory_space=pltpu.VMEM)
    rows_f32 = jax.ShapeDtypeStruct((all_rows, LANES), jnp.float32)
    y, total, end = pl.pallas_call(
        scan_kernel,
        out_shape=(
            rows_f32,
            rows_f32,
            jax.ShapeDtypeStruct((reqs, states + 1, ROWS, LANES), jnp.float32),
        ),
        in_specs=[smem, smem] + [vmem] * 7,
        out_specs=(vmem, vmem, vmem),
        scratch_shapes=[
            pltpu.VMEM((all_rows, LANES), jnp.float32),
            pltpu.VMEM((all_rows, LANES), jnp.float32),
        ],
        compiler_params=pltpu.CompilerParams(vmem_limit_bytes=48 << 20),
        name="scan",
    )(place, proj, x_here, dt_here, weights, bias, decay, skip, start)

    end_state, end_total = end[:, :states], end[:, states:]
    total_top, total_low = halves(end_total)
    leaving = jnp.concatenate([end_state.astype(jnp.bfloat16), total_top, total_low], axis=1)
    arrived = [
        lax.ppermute(leaving, "hi", [(i, i + by) for i in range(HI - by)]) for by in range(1, HI)
    ]
    carry = jnp.zeros((reqs, states, ROWS, LANES), jnp.float32)
    for block in reversed(arrived):
        block = block.astype(jnp.float32)
        block_total = block[:, states : states + 1] + block[:, states + 1 :]
        carry = block[:, :states] + jnp.exp2(block_total * decay[None]) * carry

    out = pl.pallas_call(
        correct_kernel,
        out_shape=jax.ShapeDtypeStruct((LO, reqs, toks, chans), jnp.bfloat16),
        in_specs=[smem, smem] + [vmem] * 4,
        out_specs=vmem,
        scratch_shapes=[pltpu.VMEM((reqs * toks * ROWS, LANES), jnp.float32)],
        compiler_params=pltpu.CompilerParams(vmem_limit_bytes=48 << 20),
        name="correct",
    )(place, proj, y, total, decay, carry)

    final = (end_state + jnp.exp2(end_total * decay[None]) * carry).astype(jnp.bfloat16)
    final = final.reshape(reqs, states, HI, piece)
    held = final[:, :, HI - 1]
    for to in range(HI - 1):
        moved = lax.ppermute(final[:, :, to], "hi", [(HI - 1, to)])
        held = jnp.where(hi == to, moved, held)
    fresh = [held] + [lax.ppermute(held, "cache", shifts(groups, by)) for by in range(1, groups)]
    fresh = jnp.stack(fresh)
    source_group = lax.rem(group - jnp.arange(groups, dtype=jnp.int32) + groups, groups)
    request = (source_group[:, None] * reqs + jnp.arange(reqs, dtype=jnp.int32)[None, :]).reshape(-1)
    ids = jnp.arange(count, dtype=jnp.int32)
    ranks = jnp.sum((owners[:, None] == owners[None, :]) & (ids[None, :] < ids[:, None]), axis=1)
    target = evict_order[0][ranks]
    slot_ids = jnp.arange(slots, dtype=jnp.int32)
    fresh = fresh.reshape(count, states, piece)
    hits = (target[request][:, None] == slot_ids[None, :]) & (owners[request] == group)[:, None]
    rows = jnp.dot(
        hits.T.astype(jnp.bfloat16), fresh.reshape(count, -1), preferred_element_type=jnp.float32
    ).astype(jnp.bfloat16)
    updated = jnp.where(jnp.any(hits, axis=0)[:, None], rows, stored.reshape(slots, -1))

    back = lax.all_to_all(out, "lo", split_axis=0, concat_axis=0, tiled=True)
    back = back.reshape(LO, reqs, toks, HI, piece).transpose(1, 2, 3, 0, 4)
    return back.reshape(conv_out.shape), updated.reshape(cache_states.shape)


def solution(mesh):
    fine = Mesh(mesh.devices.reshape(mesh.shape["cache"], HI, LO, mesh.shape["head"]),
                ("cache", "hi", "lo", "head"))
    ctx = ("hi", "lo")
    in_specs = (
        P("cache", ctx, "head"),
        P("cache", ctx, None),
        P("cache", ctx, None),
        P(ctx, "head"),
        P("head"),
        P(None, "head"),
        P("head"),
        P("cache", "head", None, ctx),
        P(),
        P(),
        P("cache", None),
        P(),
    )
    out_specs = (P("cache", ctx, "head"), P("cache", "head", None, ctx))
    return jax.shard_map(
        on_device, mesh=fine, in_specs=in_specs, out_specs=out_specs, check_vma=False
    )
```

time: 1060 us -> 229 us (0.22)
  waiting for transfers between devices: 659 us -> 73.3 us
  other arithmetic: 206 us -> 6.45 us
  matrix products: 70.2 us -> 0.4 us
  Pallas kernels: 0 us -> 55.3 us
  blocking collectives: 46.9 us -> 0 us
  starting transfers between devices: 9.93 us -> 42.8 us
    all_gather x3 -> x0, waiting for transfers between devices: 507 us -> none  [the longest x2 407 us: entering(): pieces = jax.tree.map(lambda part: lax.all_gather(part, axis), value)]
    psum x1 -> x0, waiting for transfers between devices: 144 us -> none  [broadcast(): return lax.psum(kept, axis)]
    select_n x33 -> x5, other arithmetic: 71.8 us -> 1.57 us  [the longest x1 0.83 us: on_device(): slot_rows = jnp.where(owners == group, hit_slot, 0)]
    dot_general x70 -> x1, matrix products: 70.2 us -> 0.4 us  [on_device(): jnp.dot(hits.T.astype(jnp.bfloat16), fresh.reshape(count, -1), preferred_...]
    ppermute x0 -> x15, waiting for transfers between devices: none -> 68.2 us  [the longest x3 33.2 us: on_device(): lax.ppermute(seed, 'hi', [(by, 0)])]
    pallas_call x0 -> x2, Pallas kernels: none -> 55.3 us  [the longest x1 33.6 us: on_device(): pl.pallas_call(scan_kernel, out_shape=(rows_f32, rows_f32, jax.ShapeDtype...]
    while x56 -> x0, other arithmetic: 48.4 us -> none
    all_gather x1 -> x0, blocking collectives: 46.9 us -> none  [on_device(): lax.all_gather(seed_piece, 'ctx', axis=2, tiled=True)]
  transfers between devices with their start and end apart: 6 -> 19, of which waited for: 6 -> 11; matrix products, arithmetic and copies ran while one was open for 1% -> 7% of each run, Pallas kernels for 0% -> 0%
where the time goes in v1:
time: 229 us; the launch traced here: 226 us
  waiting for transfers between devices  73.3 us (32%)
  Pallas kernels  55.3 us (24%)
  starting transfers between devices  42.8 us (19%)
  local copies, waits for them, and re-layouts  31.2 us (14%)
  between operations  16.3 us (7%)
  other arithmetic  6.45 us (3%)
    pallas_call x1, Pallas kernels, on_device(): pl.pallas_call(scan_kernel, out_shape=(rows_f32, rows_f32, jax.ShapeDtype...  33.6 us
    ppermute x3, waiting for transfers between devices, on_device(): lax.ppermute(seed, 'hi', [(by, 0)])  33.2 us
    pallas_call x1, Pallas kernels, on_device(): pl.pallas_call(correct_kernel, out_shape=jax.ShapeDtypeStruct((LO, reqs,...  21.6 us
    ppermute x3, waiting for transfers between devices, on_device(): moved = lax.ppermute(final[:, :, to], 'hi', [(HI - 1, to)])  21.1 us
    all_to_all x1, starting transfers between devices, on_device(): lax.all_to_all(quarter, ('hi', 'lo'), split_axis=0, concat_axis=0, tiled=...  10.8 us
    ppermute x3, waiting for transfers between devices, on_device(): lax.ppermute(quarter, 'cache', shifts(groups, by))  8.92 us
    unnamed x35, local copies, waits for them, and re-layouts  7.91 us
    ppermute x3, starting transfers between devices, on_device(): lax.ppermute(leaving, 'hi', [(i, i + by) for i in range(HI - by)])  5.55 us
  transfers between devices with their start and end apart: 19, of which 11 were waited for; matrix products, arithmetic and copies ran while one was open for 7% of the time, Pallas kernels for 0%

profile of v1, /device:TPU:8, one launch (start us, length us, event | category | flops | bytes accessed | tf_op | source)
XLA Modules:
  0.0 225.7 jit_solution(12106264277041152744)
XLA Ops:
  23.6 5.4 %all-to-all-start.2 = ((bf16[8,16,256]{2,1,0:T(8,128)(2,1)}), bf16[8,16,256]{2,1,0:T(8,128)(2,1)S(1)}, u32[]{:S(2)}, u32[]{:S(2)}) async-start(bf16[8,16,256]{2,1,0:T(8,128)(2,1)} %broadcast_select_fusion), calls=%async_computation.2 | async-start | bytes 131072 | tf_op jit(solution)/shard_map/all_to_all | solution.py:154
  31.2 2.0 all-to-all-done.2
  34.0 10.8 %all-to-all-start.1 = ((bf16[32,4,1024]{2,1,0:T(4,128)(2,1)}), bf16[32,4,1024]{2,1,0:T(4,128)(2,1)S(1)}, u32[]{:S(2)}, u32[]{:S(2)}) async-start(bf16[32,4,1024]{2,1,0:T(4,128)(2,1)} %bitcast.7), calls=%async_computation.1 | async-start | bytes 524288 | tf_op jit(solution)/shard_map/all_to_all | solution.py:143
  45.7 2.3 %copy.90 = bf16[2,64,4,8,256]{4,2,1,0,3:T(4,128)(2,1)} copy(bf16[2,64,4,8,256]{4,3,2,1,0:T(8,128)(2,1)S(1)} %bitcast.133) | data formatting | bytes 4194304 | tf_op jit(solution)/shard_map/reshape | solution.py:162
  48.0 3.2 %reshape.156 = bf16[8,2,64,1024]{3,2,1,0:T(8,128)(2,1)S(1)} reshape(bf16[8,2,64,4,256]{4,3,2,1,0:T(4,128)(2,1)} %bitcast.131) | data formatting | bytes 4194304 | tf_op jit(solution)/shard_map/reshape | solution.py:163
  51.4 2.1 pad_maximum_fusion
  53.5 3.0 %all-to-all-done.1 = bf16[32,4,1024]{2,1,0:T(4,128)(2,1)S(1)} async-done(((bf16[32,4,1024]{2,1,0:T(4,128)(2,1)}), bf16[32,4,1024]{2,1,0:T(4,128)(2,1)S(1)}, u32[]{:S(2)}, u32[]{:S(2)}) %all-to-all-start.1) | async-done | bytes 262176 | tf_op jit(solution)/shard_map/all_to_all | solution.py:143
  56.5 4.5 %all-to-all-start = ((bf16[8,2,64,1664]{3,2,1,0:T(8,128)(2,1)}), bf16[8,2,64,1664]{3,2,1,0:T(8,128)(2,1)}, u32[]{:S(2)}, u32[]{:S(2)}) async-start(bf16[8,2,64,1664]{3,2,1,0:T(8,128)(2,1)} %pad_maximum_fusion), calls=%async_computation | async-start | bytes 6815744 | tf_op jit(solution)/shard_map/all_to_all | solution.py:171
  61.4 1.3 collective-permute-start.3
  62.7 1.3 collective-permute-start.4
  64.0 1.3 collective-permute-start.5
  66.3 1.7 collective-permute-done.3
  68.1 31.5 %collective-permute-done.4 = bf16[2,16,256]{2,1,0:T(8,128)(2,1)S(1)} collective-permute-done((bf16[2,16,256]{2,1,0:T(8,128)(2,1)S(1)}, bf16[2,16,256]{2,1,0:T(8,128)(2,1)S(1)}, u32[]{:S(2)}, u32[]{:S(2)}) %collective-permute-start.4) | collective-permute-done | bytes 16416 | tf_op jit(solution)/shard_map/ppermute | solution.py:158
  99.8 1.5 collective-permute-start.1
  102.9 6.6 %collective-permute-done.1 = bf16[128,1024]{1,0:T(8,128)(2,1)S(1)} collective-permute-done((bf16[128,1024]{1,0:T(8,128)(2,1)S(1)}, bf16[128,1024]{1,0:T(8,128)(2,1)S(1)}, u32[]{:S(2)}, u32[]{:S(2)}) %collective-permute-start.1) | collective-permute-done | bytes 262176 | tf_op jit(solution)/shard_map/ppermute | solution.py:146
  109.5 2.3 %collective-permute-done.2 = bf16[128,1024]{1,0:T(8,128)(2,1)S(1)} collective-permute-done((bf16[128,1024]{1,0:T(8,128)(2,1)S(1)}, bf16[128,1024]{1,0:T(8,128)(2,1)S(1)}, u32[]{:S(2)}, u32[]{:S(2)}) %collective-permute-start.2) | collective-permute-done | bytes 262176 | tf_op jit(solution)/shard_map/ppermute | solution.py:146
  113.2 1.8 slice.116.x_ref
  115.0 1.3 slice.117.dt_ref
  116.3 33.6 %scan.1 = (f32[8192,128]{1,0:T(8,128)}, f32[8192,128]{1,0:T(8,128)}, f32[2,17,8,128]{3,2,1,0:T(8,128)S(1)}) custom-call(s32[3]{0:T(128)S(1)} %pad_add_fusion.place_ref, f32[32768]{0:T(1024)S(1)} %reshape.159.proj_ref, bf16[8,2,64,1024]{3,2,1,0:T(8,128)(2,1)S(1)} %slice.116.x_ref, bf16[8,2,64,512]{3,2,1,0:T(8,128)(2,1)S(1)} %slice.117.dt_ref, ...), custom_call_target="tpu_custom_call" | custom-call | tf_op jit(solution)/shard_map/scan/pallas_call | solution.py:203
  150.0 1.3 collective-permute-start.8
  151.3 1.3 collective-permute-start.7
  152.6 3.0 %collective-permute-start.6 = (bf16[2,18,8,128]{3,2,1,0:T(8,128)(2,1)S(1)}, bf16[2,18,8,128]{3,2,1,0:T(8,128)(2,1)S(1)}, u32[]{:S(2)}, u32[]{:S(2)}) collective-permute-start(bf16[2,18,8,128]{3,2,1,0:T(8,128)(2,1)S(1)} %pad_maximum_fusion.1), channel_id=1, source_target_pairs={{0,16},{16,32},{32,48},{1,17},{17,33},{33,49},{2,18},{18,34},{34,5... | collective-permute-start | bytes 221192 | tf_op jit(solution)/shard_map/ppermute | solution.py:224
  155.8 1.7 collective-permute-done.6
  157.7 21.6 %correct.1 = bf16[8,2,64,1024]{3,2,1,0:T(8,128)(2,1)} custom-call(s32[3]{0:T(128)S(1)} %pad_add_fusion.place_ref, f32[32768]{0:T(1024)S(1)} %reshape.159.proj_ref, f32[8192,128]{1,0:T(8,128)} %get-tuple-element.5.y_ref, f32[8192,128]{1,0:T(8,128)} %get-tuple-element.6.total_ref, f32[16,8,128]{2,1,0:T(8,128)S(1)} %mul.96.decay_ref, ...), custom_call_target="tpu_custom_call" | custom-call | tf_op jit(solution)/shard_map/correct/pallas_call | solution.py:232
  179.3 4.4 %all-to-all-start.3 = ((bf16[8,2,64,1024]{3,2,1,0:T(8,128)(2,1)}), bf16[8,2,64,1024]{3,2,1,0:T(8,128)(2,1)S(1)}, u32[]{:S(2)}, u32[]{:S(2)}) async-start(bf16[8,2,64,1024]{3,2,1,0:T(8,128)(2,1)} %correct.1), calls=%async_computation.3 | async-start | bytes 4194304 | tf_op jit(solution)/shard_map/all_to_all | solution.py:263
  188.9 21.1 %collective-permute-done.11 = bf16[2,16,256]{2,1,0:T(8,128)(2,1)S(1)} collective-permute-done((bf16[2,16,256]{2,1,0:T(8,128)(2,1)S(1)}, bf16[2,16,256]{2,1,0:T(8,128)(2,1)S(1)}, u32[]{:S(2)}, u32[]{:S(2)}) %collective-permute-start.11) | collective-permute-done | bytes 16416 | tf_op jit(solution)/shard_map/ppermute | solution.py:246
  210.2 1.9 collective-permute-start.14
  212.4 1.4 collective-permute-done.12
  213.8 1.6 collective-permute-done.13
  216.8 2.7 %reshape.170 = bf16[8,2,64,4,256]{4,3,2,1,0:T(4,128)(2,1)} reshape(bf16[8,2,64,1024]{3,2,1,0:T(8,128)(2,1)S(1)} %all-to-all-done.3) | data formatting | bytes 4194304 | tf_op jit(solution)/shard_map/reshape | solution.py:264
  219.5 3.8 %copy.60 = bf16[2,64,4,8,256]{4,3,2,1,0:T(8,128)(2,1)S(1)} copy(bf16[2,64,4,8,256]{4,2,1,0,3:T(4,128)(2,1)} %bitcast.132) | data formatting | bytes 4194304 | tf_op jit(solution)/shard_map/transpose | solution.py:264
  223.4 2.3 %reshape.171 = bf16[2,64,8192]{2,1,0:T(8,128)(2,1)} reshape(bf16[2,64,4,8,256]{4,3,2,1,0:T(8,128)(2,1)S(1)} %copy.60) | data formatting | bytes 4194304 | tf_op jit(solution)/shard_map/reshape | solution.py:265
  (113 shorter events, 23.6 us)
Async XLA Ops:
  0.6 28.4 %copy-start = (bf16[16,8192]{1,0:T(8,128)(2,1)S(1)}, bf16[16,8192]{1,0:T(8,128)(2,1)}, u32[]{:S(2)}) copy-start(bf16[16,8192]{1,0:T(8,128)(2,1)} %param.15) | copy-start | bytes 786436
  0.6 44.5 %copy-start.3 = (bf16[2,64,8192]{2,1,0:T(8,128)(2,1)S(1)}, bf16[2,64,8192]{2,1,0:T(8,128)(2,1)}, u32[]{:S(2)}) copy-start(bf16[2,64,8192]{2,1,0:T(8,128)(2,1)} %param.12) | copy-start | bytes 6291460
  23.6 9.6 %all-to-all-start.2 = ((bf16[8,16,256]{2,1,0:T(8,128)(2,1)}), bf16[8,16,256]{2,1,0:T(8,128)(2,1)S(1)}, u32[]{:S(2)}, u32[]{:S(2)}) async-start(bf16[8,16,256]{2,1,0:T(8,128)(2,1)} %broadcast_select_fusion), calls=%async_computation.2 | async-start | bytes 131072 | tf_op jit(solution)/shard_map/all_to_all | solution.py:154
  34.0 22.5 %all-to-all-start.1 = ((bf16[32,4,1024]{2,1,0:T(4,128)(2,1)}), bf16[32,4,1024]{2,1,0:T(4,128)(2,1)S(1)}, u32[]{:S(2)}, u32[]{:S(2)}) async-start(bf16[32,4,1024]{2,1,0:T(4,128)(2,1)} %bitcast.7), calls=%async_computation.1 | async-start | bytes 524288 | tf_op jit(solution)/shard_map/all_to_all | solution.py:143
  53.5 7.5 %copy-start.5 = (f32[16,8192]{1,0:T(8,128)S(1)}, f32[16,8192]{1,0:T(8,128)}, u32[]{:S(2)}) copy-start(f32[16,8192]{1,0:T(8,128)} %param.17) | copy-start | bytes 1572868
  53.5 7.7 %copy-start.6 = (f32[8192]{0:T(1024)S(1)}, f32[8192]{0:T(1024)}, u32[]{:S(2)}) copy-start(f32[8192]{0:T(1024)} %param.16) | copy-start | bytes 98308
  53.5 7.7 %copy-start.7 = (f32[8192]{0:T(1024)S(1)}, f32[8192]{0:T(1024)}, u32[]{:S(2)}) copy-start(f32[8192]{0:T(1024)} %param.18) | copy-start | bytes 98308
  53.5 7.7 %copy-start.8 = (s32[8]{0:T(128)S(1)}, s32[8]{0:T(128)}, u32[]{:S(2)}) copy-start(s32[8]{0:T(128)} %param.23) | copy-start | bytes 100
  56.5 55.4 %all-to-all-start = ((bf16[8,2,64,1664]{3,2,1,0:T(8,128)(2,1)}), bf16[8,2,64,1664]{3,2,1,0:T(8,128)(2,1)}, u32[]{:S(2)}, u32[]{:S(2)}) async-start(bf16[8,2,64,1664]{3,2,1,0:T(8,128)(2,1)} %pad_maximum_fusion), calls=%async_computation | async-start | bytes 6815744 | tf_op jit(solution)/shard_map/all_to_all | solution.py:171
  61.4 6.6 %collective-permute-start.3 = (bf16[2,16,256]{2,1,0:T(8,128)(2,1)S(1)}, bf16[2,16,256]{2,1,0:T(8,128)(2,1)S(1)}, u32[]{:S(2)}, u32[]{:S(2)}) collective-permute-start(bf16[2,16,256]{2,1,0:T(8,128)(2,1)S(1)} %reduce_sum.23), channel_id=1, source_target_pairs={{16,0},{17,1},{18,2},{19,3},{20,4},{21,5},{22,6},{23,7},{24,8},{25... | collective-permute-start | bytes 49160 | tf_op jit(solution)/shard_map/ppermute | solution.py:158
  62.7 36.9 %collective-permute-start.4 = (bf16[2,16,256]{2,1,0:T(8,128)(2,1)S(1)}, bf16[2,16,256]{2,1,0:T(8,128)(2,1)S(1)}, u32[]{:S(2)}, u32[]{:S(2)}) collective-permute-start(bf16[2,16,256]{2,1,0:T(8,128)(2,1)S(1)} %reduce_sum.23), channel_id=1, source_target_pairs={{32,0},{33,1},{34,2},{35,3},{36,4},{37,5},{38,6},{39,7},{40,8},{41... | collective-permute-start | bytes 49160 | tf_op jit(solution)/shard_map/ppermute | solution.py:158
  64.0 35.6 %collective-permute-start.5 = (bf16[2,16,256]{2,1,0:T(8,128)(2,1)S(1)}, bf16[2,16,256]{2,1,0:T(8,128)(2,1)S(1)}, u32[]{:S(2)}, u32[]{:S(2)}) collective-permute-start(bf16[2,16,256]{2,1,0:T(8,128)(2,1)S(1)} %reduce_sum.23), channel_id=1, source_target_pairs={{48,0},{49,1},{50,2},{51,3},{52,4},{53,5},{54,6},{55,7},{56,8},{57... | collective-permute-start | bytes 49160 | tf_op jit(solution)/shard_map/ppermute | solution.py:158
  65.4 37.4 %collective-permute-start = (bf16[128,1024]{1,0:T(8,128)(2,1)S(1)}, bf16[128,1024]{1,0:T(8,128)(2,1)S(1)}, u32[]{:S(2)}, u32[]{:S(2)}) collective-permute-start(bf16[128,1024]{1,0:T(8,128)(2,1)S(1)} %reshape.162), channel_id=1, source_target_pairs={{0,64},{64,128},{128,192},{192,0},{1,65},{65,129},{129,193},{193,1... | collective-permute-start | bytes 786440 | tf_op jit(solution)/shard_map/ppermute | solution.py:146
  99.8 9.7 %collective-permute-start.1 = (bf16[128,1024]{1,0:T(8,128)(2,1)S(1)}, bf16[128,1024]{1,0:T(8,128)(2,1)S(1)}, u32[]{:S(2)}, u32[]{:S(2)}) collective-permute-start(bf16[128,1024]{1,0:T(8,128)(2,1)S(1)} %reshape.162), channel_id=1, source_target_pairs={{0,128},{64,192},{128,0},{192,64},{1,129},{65,193},{129,1},{193,65... | collective-permute-start | bytes 786440 | tf_op jit(solution)/shard_map/ppermute | solution.py:146
  101.3 10.5 %collective-permute-start.2 = (bf16[128,1024]{1,0:T(8,128)(2,1)S(1)}, bf16[128,1024]{1,0:T(8,128)(2,1)S(1)}, u32[]{:S(2)}, u32[]{:S(2)}) collective-permute-start(bf16[128,1024]{1,0:T(8,128)(2,1)S(1)} %reshape.162), channel_id=1, source_target_pairs={{0,192},{64,0},{128,64},{192,128},{1,193},{65,1},{129,65},{193,129... | collective-permute-start | bytes 786440 | tf_op jit(solution)/shard_map/ppermute | solution.py:146
  150.0 5.8 %collective-permute-start.8 = (bf16[2,18,8,128]{3,2,1,0:T(8,128)(2,1)S(1)}, bf16[2,18,8,128]{3,2,1,0:T(8,128)(2,1)S(1)}, u32[]{:S(2)}, u32[]{:S(2)}) collective-permute-start(bf16[2,18,8,128]{3,2,1,0:T(8,128)(2,1)S(1)} %pad_maximum_fusion.1), channel_id=1, source_target_pairs={{0,48},{1,49},{2,50},{3,51},{4,52},{5,53},{6,54},{7,55},{8,56},{9,... | collective-permute-start | bytes 221192 | tf_op jit(solution)/shard_map/ppermute | solution.py:224
  151.3 4.5 %collective-permute-start.7 = (bf16[2,18,8,128]{3,2,1,0:T(8,128)(2,1)S(1)}, bf16[2,18,8,128]{3,2,1,0:T(8,128)(2,1)S(1)}, u32[]{:S(2)}, u32[]{:S(2)}) collective-permute-start(bf16[2,18,8,128]{3,2,1,0:T(8,128)(2,1)S(1)} %pad_maximum_fusion.1), channel_id=1, source_target_pairs={{0,32},{16,48},{1,33},{17,49},{2,34},{18,50},{3,35},{19,51},{4,36}... | collective-permute-start | bytes 221192 | tf_op jit(solution)/shard_map/ppermute | solution.py:224
  152.6 4.9 %collective-permute-start.6 = (bf16[2,18,8,128]{3,2,1,0:T(8,128)(2,1)S(1)}, bf16[2,18,8,128]{3,2,1,0:T(8,128)(2,1)S(1)}, u32[]{:S(2)}, u32[]{:S(2)}) collective-permute-start(bf16[2,18,8,128]{3,2,1,0:T(8,128)(2,1)S(1)} %pad_maximum_fusion.1), channel_id=1, source_target_pairs={{0,16},{16,32},{32,48},{1,17},{17,33},{33,49},{2,18},{18,34},{34,5... | collective-permute-start | bytes 221192 | tf_op jit(solution)/shard_map/ppermute | solution.py:224
  179.3 4.6 %copy-start.1 = (s32[8,1]{0,1:T(1,128)S(1)}, s32[8,1]{0,1:T(1,128)}, u32[]{:S(2)}) copy-start(s32[8,1]{0,1:T(1,128)} %param.20) | copy-start | bytes 100
  179.3 8.3 %copy-start.2 = (s32[1,64]{1,0:T(1,128)S(1)}, s32[1,64]{1,0:T(1,128)}, u32[]{:S(2)}) copy-start(s32[1,64]{1,0:T(1,128)} %param.22) | copy-start | bytes 772
  179.3 37.5 %all-to-all-start.3 = ((bf16[8,2,64,1024]{3,2,1,0:T(8,128)(2,1)}), bf16[8,2,64,1024]{3,2,1,0:T(8,128)(2,1)S(1)}, u32[]{:S(2)}, u32[]{:S(2)}) async-start(bf16[8,2,64,1024]{3,2,1,0:T(8,128)(2,1)} %correct.1), calls=%async_computation.3 | async-start | bytes 4194304 | tf_op jit(solution)/shard_map/all_to_all | solution.py:263
  183.7 28.5 %copy-start.4 = (bf16[64,1,16,256]{3,2,1,0:T(8,128)(2,1)S(1)}, bf16[64,1,16,256]{3,2,1,0:T(8,128)(2,1)}, u32[]{:S(2)}) copy-start(bf16[64,1,16,256]{3,2,1,0:T(8,128)(2,1)} %param.19) | copy-start | bytes 1572868
  184.9 4.0 %collective-permute-start.10 = (bf16[2,16,256]{2,1,0:T(8,128)(2,1)S(1)}, bf16[2,16,256]{2,1,0:T(8,128)(2,1)S(1)}, u32[]{:S(2)}, u32[]{:S(2)}) collective-permute-start(bf16[2,16,256]{2,1,0:T(8,128)(2,1)S(1)} %bitcast.153), channel_id=1, source_target_pairs={{48,16},{49,17},{50,18},{51,19},{52,20},{53,21},{54,22},{55,23},{5... | collective-permute-start | bytes 49160 | tf_op jit(solution)/shard_map/ppermute | solution.py:246
  185.6 24.4 %collective-permute-start.11 = (bf16[2,16,256]{2,1,0:T(8,128)(2,1)S(1)}, bf16[2,16,256]{2,1,0:T(8,128)(2,1)S(1)}, u32[]{:S(2)}, u32[]{:S(2)}) collective-permute-start(bf16[2,16,256]{2,1,0:T(8,128)(2,1)S(1)} %bitcast.154), channel_id=1, source_target_pairs={{48,0},{49,1},{50,2},{51,3},{52,4},{53,5},{54,6},{55,7},{56,8},{57... | collective-permute-start | bytes 49160 | tf_op jit(solution)/shard_map/ppermute | solution.py:246
  186.9 23.1 %collective-permute-start.9 = (bf16[2,16,256]{2,1,0:T(8,128)(2,1)S(1)}, bf16[2,16,256]{2,1,0:T(8,128)(2,1)S(1)}, u32[]{:S(2)}, u32[]{:S(2)}) collective-permute-start(bf16[2,16,256]{2,1,0:T(8,128)(2,1)S(1)} %bitcast.155), channel_id=1, source_target_pairs={{48,32},{49,33},{50,34},{51,35},{52,36},{53,37},{54,38},{55,39},{5... | collective-permute-start | bytes 49160 | tf_op jit(solution)/shard_map/ppermute | solution.py:246
  210.0 3.8 %collective-permute-start.12 = (bf16[2,16,256]{2,1,0:T(8,128)(2,1)S(1)}, bf16[2,16,256]{2,1,0:T(8,128)(2,1)S(1)}, u32[]{:S(2)}, u32[]{:S(2)}) collective-permute-start(bf16[2,16,256]{2,1,0:T(8,128)(2,1)S(1)} %fusion.8), channel_id=1, source_target_pairs={{0,64},{64,128},{128,192},{192,0},{1,65},{65,129},{129,193},{193,1... | collective-permute-start | bytes 49160 | tf_op jit(solution)/shard_map/ppermute | solution.py:248
  210.1 5.4 %collective-permute-start.13 = (bf16[2,16,256]{2,1,0:T(8,128)(2,1)S(1)}, bf16[2,16,256]{2,1,0:T(8,128)(2,1)S(1)}, u32[]{:S(2)}, u32[]{:S(2)}) collective-permute-start(bf16[2,16,256]{2,1,0:T(8,128)(2,1)S(1)} %fusion.8), channel_id=1, source_target_pairs={{0,128},{64,192},{128,0},{192,64},{1,129},{65,193},{129,1},{193,65... | collective-permute-start | bytes 49160 | tf_op jit(solution)/shard_map/ppermute | solution.py:248
  210.2 5.3 %collective-permute-start.14 = (bf16[2,16,256]{2,1,0:T(8,128)(2,1)S(1)}, bf16[2,16,256]{2,1,0:T(8,128)(2,1)S(1)}, u32[]{:S(2)}, u32[]{:S(2)}) collective-permute-start(bf16[2,16,256]{2,1,0:T(8,128)(2,1)S(1)} %fusion.8), channel_id=1, source_target_pairs={{0,192},{64,0},{128,64},{192,128},{1,193},{65,1},{129,65},{193,129... | collective-permute-start | bytes 49160 | tf_op jit(solution)/shard_map/ppermute | solution.py:248

commit v2 on v0

v2 whole, which is shorter than its diff:
```python
import functools
import math

import jax
import jax.numpy as jnp
from jax import lax
from jax.experimental import pallas as pl
from jax.experimental.pallas import tpu as pltpu
from jax.sharding import Mesh, PartitionSpec as P

HI, LO = 4, 8
LANES, ROWS = 128, 8
LOG2E = math.log2(math.e)


def params(mib):
    return pltpu.CompilerParams(vmem_limit_bytes=mib << 20)


def cost(us):
    return pl.CostEstimate(flops=0, bytes_accessed=int(us * 3.6e6), transcendentals=0)


def spread_kernel(group_ref, w_ref, out_ref):
    width = w_ref.shape[1] // LO
    for lo in range(LO):
        block = w_ref[:, lo * width : (lo + 1) * width]
        for hi in range(HI):
            out_ref[hi * LO + lo] = block


def pack_kernel(x_ref, dt_ref, proj_ref, out_ref):
    piece = x_ref.shape[2] // (HI * LO)
    chans, rank, nbc = piece * HI, dt_ref.shape[2], proj_ref.shape[2]
    proj = proj_ref[0]
    top = proj.astype(jnp.bfloat16)
    low = (proj - top.astype(jnp.float32)).astype(jnp.bfloat16)
    pad = jnp.zeros((proj.shape[0], LANES - 2 * nbc), jnp.bfloat16)
    tail = jnp.concatenate([top, low, pad], axis=1)
    for lo in range(LO):
        for hi in range(HI):
            at = (hi * LO + lo) * piece
            out_ref[lo, :, hi * piece : (hi + 1) * piece] = x_ref[0, :, at : at + piece]
        out_ref[lo, :, chans : chans + rank] = dt_ref[0]
        out_ref[lo, :, chans + rank :] = tail


def unpack_kernel(back_ref, *refs):
    out_ref = refs[-1]
    piece = back_ref.shape[2] // HI
    for lo in range(LO):
        for hi in range(HI):
            at = (hi * LO + lo) * piece
            out_ref[0, :, at : at + piece] = back_ref[lo, :, hi * piece : (hi + 1) * piece]


def replicate(tail, first, count, scr, offset, rows, total_rows):
    depth = lax.broadcasted_iota(jnp.int32, (LANES, 2 * LANES), 0)
    side = lax.broadcasted_iota(jnp.int32, (LANES, 2 * LANES), 1) // LANES
    for n in range(0, count, 2):
        column = first + n + side
        pick = ((depth == column) | (depth == 32 + column)).astype(jnp.float32).astype(jnp.bfloat16)
        wide = jnp.dot(tail, pick, preferred_element_type=jnp.float32)
        scr[pl.ds(n * total_rows + offset, rows), :] = wide[:, :LANES]
        scr[pl.ds((n + 1) * total_rows + offset, rows), :] = wide[:, LANES:]


def to_rows(scr, refs, count):
    for p, ref in enumerate(refs):
        for j in range(2):
            value = ref[:, j * LANES : (j + 1) * LANES]
            scr[pl.ds(2 * p + j, count, stride=ROWS), :] = value


def scan_kernel(req, place_ref, lengths_ref, got_ref, *refs):
    w_refs, decay_refs, bias_refs, skip_refs = (refs[i * HI : (i + 1) * HI] for i in range(4))
    refs = refs[4 * HI :]
    before_refs, refs = refs[:-9], refs[-9:]
    if before_refs:
        seed_ref, leave_ref, *before_refs = before_refs[-2], before_refs[-1], *before_refs[:-2]
    y_ref, total_ref, end_ref, step_scr, x_scr, bc_scr, decay_scr, skip_scr, held_scr = refs
    parts, toks, _ = got_ref.shape
    rank, width = w_refs[0].shape
    chans = HI * width
    states = decay_refs[0].shape[0]
    rows = parts * toks
    hi, group = place_ref[0], place_ref[2]
    step_id = pl.program_id(0)

    @pl.when(step_id == 0)
    def _():
        to_rows(decay_scr, decay_refs, states)
        decay_scr[...] = decay_scr[...] * (-LOG2E)
        for p in range(HI):
            for j in range(2):
                skip_scr[2 * p + j : 2 * p + j + 1, :] = skip_refs[p][
                    :, j * LANES : (j + 1) * LANES
                ]
        held_scr[...] = jnp.zeros_like(held_scr)

    wide_x = got_ref[:, :, :chans].reshape(rows, chans).astype(jnp.float32)
    dt = got_ref[:, :, chans : chans + rank].reshape(rows, rank)
    tail = got_ref[:, :, chans + rank :].reshape(rows, LANES)
    position = (hi * pl.num_programs(0) + step_id) * rows + lax.broadcasted_iota(
        jnp.int32, (rows, 1), 0
    )
    live = position < lengths_ref[group * 2 + req]
    for by in range(HI):
        block = lax.rem(group - by + HI, HI)
        bias = bias_refs[0][...]
        for p in range(1, HI):
            bias = jnp.where(block == p, bias_refs[p][...], bias)
        pre = jnp.dot(dt, w_refs[by][...], preferred_element_type=jnp.float32) + bias
        step = jnp.maximum(pre, 0.0) + jnp.log1p(jnp.exp(-jnp.abs(pre)))
        step = jnp.where(live, step, 0.0)
        for j in range(2):
            step_scr[pl.ds(2 * block + j, rows, stride=ROWS), :] = step[
                :, j * LANES : (j + 1) * LANES
            ]
    for k in range(ROWS):
        x_scr[pl.ds(k, rows, stride=ROWS), :] = wide_x[:, k * LANES : (k + 1) * LANES]
    replicate(tail, 0, 2 * states, bc_scr, 0, rows, rows)
    skip = skip_scr[...]

    def per_tok(tok, carried):
        total, held = carried
        at = pl.ds(pl.multiple_of(tok * ROWS, ROWS), ROWS)
        step = step_scr[at, :]
        wide_x = x_scr[at, :]
        driven = step * wide_x
        total = total + step
        out = skip * wide_x
        new = []
        for n in range(states):
            enter = bc_scr[pl.ds(n * rows + tok, 1), :]
            leave = bc_scr[pl.ds((states + n) * rows + tok, 1), :]
            state = jnp.exp2(step * decay_scr[n * ROWS : (n + 1) * ROWS, :]) * held[n]
            state = state + enter * driven
            out = out + leave * state
            new.append(state)
        total_ref[at, :] = total
        y_ref[at, :] = out
        return total, tuple(new)

    held = tuple(held_scr[n * ROWS : (n + 1) * ROWS, :] for n in range(states))
    total, held = lax.fori_loop(
        0, rows, per_tok, (held_scr[states * ROWS :, :], held), unroll=8
    )
    for n in range(states):
        held_scr[n * ROWS : (n + 1) * ROWS, :] = held[n]
    held_scr[states * ROWS :, :] = total

    @pl.when(step_id == pl.num_programs(0) - 1)
    def _():
        end_ref[...] = held_scr[...]
        if before_refs:
            leave_ref[...] = sent_rows(list(before_refs) + [held_scr], seed_ref)


def sent_rows(ends, seed_ref):
    blocks = []
    for ref in ends:
        end = ref[...]
        total = end[-ROWS:]
        top = total.astype(jnp.bfloat16).astype(jnp.float32)
        blocks += [end[:-ROWS], top, total - top]
    for req in range(len(ends)):
        for j in range(2):
            blocks.append(seed_ref[req, :, j * LANES : (j + 1) * LANES].astype(jnp.float32))
    return jnp.concatenate(blocks, axis=0).astype(jnp.bfloat16)


def join_kernel(place_ref, *refs):
    own_ref, arrived_refs, refs = refs[0], refs[1:HI], refs[HI:]
    reqs = len(refs) - 3 - 2 * HI
    end_refs, refs = refs[:reqs], refs[reqs:]
    decay_refs, carry_ref, final_refs = refs[:HI], refs[HI], refs[HI + 1 : 2 * HI + 1]
    decay_scr, state_scr = refs[2 * HI + 1 :]
    states = decay_refs[0].shape[0]
    hi = place_ref[0]
    to_rows(decay_scr, decay_refs, states)
    per_req = (states + 2) * ROWS
    blocks = [ref[...].astype(jnp.float32) for ref in (own_ref, *arrived_refs)]
    for req in range(reqs):
        for by, block in enumerate(blocks):
            slot = lax.rem(hi - by + HI, HI)
            for j in range(2):
                at = reqs * per_req + (2 * req + j) * states
                state_scr[pl.ds(2 * slot + j, states, stride=ROWS), :] = block[at : at + states]
        for n in range(states):
            rows = slice(n * ROWS, (n + 1) * ROWS)
            decay = decay_scr[rows, :] * (-LOG2E)
            carry = state_scr[rows, :]
            for by in range(HI - 1, 0, -1):
                block = blocks[by][req * per_req : (req + 1) * per_req]
                total = block[states * ROWS : (states + 1) * ROWS] + block[(states + 1) * ROWS :]
                longer = block[rows] + jnp.exp2(total * decay) * carry
                carry = jnp.where(hi >= by, longer, carry)
            carry_ref[req, n] = carry
            total = end_refs[req][states * ROWS :, :]
            state_scr[rows, :] = end_refs[req][rows, :] + jnp.exp2(total * decay) * carry
        for p in range(HI):
            for j in range(2):
                value = state_scr[pl.ds(2 * p + j, states, stride=ROWS), :]
                final_refs[p][req, :, j * LANES : (j + 1) * LANES] = value.astype(jnp.bfloat16)


def correct_kernel(req, place_ref, lengths_ref, tail_ref, y_ref, total_ref, carry_ref, *refs):
    decay_refs, (out_ref, y_scr, c_scr, decay_scr) = refs[:HI], refs[HI:]
    parts, toks, _ = out_ref.shape
    states = decay_refs[0].shape[0]
    rows = parts * toks
    step_id = pl.program_id(0)

    @pl.when(step_id == 0)
    def _():
        to_rows(decay_scr, decay_refs, states)
        decay_scr[...] = decay_scr[...] * (-LOG2E)

    replicate(tail_ref[...].reshape(rows, LANES), states, states, c_scr, 0, rows, rows)
    carry = tuple(carry_ref[0, n] for n in range(states))

    def per_tok(tok, carry):
        at = pl.ds(pl.multiple_of(tok * ROWS, ROWS), ROWS)
        total = total_ref[at, :]
        out = y_ref[at, :]
        for n in range(states):
            leave = c_scr[pl.ds(n * rows + tok, 1), :]
            decay = decay_scr[n * ROWS : (n + 1) * ROWS, :]
            out = out + leave * (jnp.exp2(total * decay) * carry[n])
        y_scr[at, :] = out
        return carry

    lax.fori_loop(0, rows, per_tok, carry, unroll=8)
    position = (place_ref[0] * pl.num_programs(0) + step_id) * rows + lax.broadcasted_iota(
        jnp.int32, (rows, 1), 0
    )
    live = position < lengths_ref[place_ref[2] * 2 + req]
    for k in range(ROWS):
        block = jnp.where(live, y_scr[pl.ds(k, rows, stride=ROWS), :], 0.0)
        out_ref[:, :, k * LANES : (k + 1) * LANES] = block.astype(jnp.bfloat16).reshape(
            parts, toks, LANES
        )


def shifts(count, by):
    return [(i, (i + by) % count) for i in range(count)]


def on_device(
    conv_out, dt_low, state_proj, dt_weight, dt_bias, decay_rate, skip_gain,
    cache_states, hit_owner, hit_slot, evict_order, new_lengths,
):
    groups = lax.axis_size("cache")
    group = lax.axis_index("cache")
    hi = lax.axis_index("hi")
    lo = lax.axis_index("lo")
    reqs, toks, width = conv_out.shape
    rank = dt_low.shape[2]
    states = decay_rate.shape[0]
    slots, piece = cache_states.shape[0], cache_states.shape[3]
    chans = width // LO
    length = LO * toks
    owners = hit_owner[:, 0]
    count = owners.shape[0]
    sent_width = chans + rank + LANES

    def exchange(array, axis):
        return lax.all_to_all(array, axis, split_axis=0, concat_axis=0, tiled=True)

    mine = dt_weight.shape[0]
    quarter = pl.pallas_call(
        spread_kernel,
        grid_spec=pltpu.PrefetchScalarGridSpec(
            num_scalar_prefetch=1,
            grid=(1,),
            in_specs=[pl.BlockSpec((mine, width // groups), lambda i, at: (0, at[0]))],
            out_specs=pl.BlockSpec((HI * LO, mine, piece), lambda i, at: (0, 0, 0)),
        ),
        out_shape=jax.ShapeDtypeStruct((HI * LO, mine, piece), jnp.bfloat16),
        compiler_params=params(60),
        name="spread",
    )(group[None].astype(jnp.int32), dt_weight)
    quarter = exchange(quarter, ("hi", "lo")).reshape(rank, piece)

    stored = cache_states.reshape(slots, -1)
    slot_ids = jnp.arange(slots, dtype=jnp.int32)
    wanted = (hit_slot[:, None] == slot_ids[None, :]) & (owners == group)[:, None]
    picked = jnp.dot(
        wanted.astype(jnp.bfloat16), stored, preferred_element_type=jnp.float32
    ).astype(jnp.bfloat16)
    picked = picked.reshape(groups, reqs, states, piece)
    seed = lax.dynamic_index_in_dim(picked, group, 0, keepdims=False).astype(jnp.float32)
    for by in range(1, groups):
        leaving = lax.dynamic_index_in_dim(picked, lax.rem(group + by, groups), 0, keepdims=False)
        seed = seed + lax.ppermute(leaving, "cache", shifts(groups, by)).astype(jnp.float32)
    seed = seed.astype(jnp.bfloat16)

    sent = [
        pl.pallas_call(
            pack_kernel,
            grid=(1,),
            in_specs=[
                pl.BlockSpec((1, toks, n), lambda i, req=req: (req, 0, 0))
                for n in (width, rank, state_proj.shape[2])
            ],
            out_specs=pl.BlockSpec((LO, toks, sent_width), lambda i: (0, 0, 0)),
            out_shape=jax.ShapeDtypeStruct((LO, toks, sent_width), jnp.bfloat16),
            compiler_params=params(60),
            name="pack",
        )(conv_out, dt_low, state_proj)
        for req in range(reqs)
    ]
    first_sent, seed = lax.optimization_barrier((sent[0], seed))
    pieces = [quarter] + [
        lax.ppermute(quarter, "cache", shifts(groups, by)) for by in range(1, groups)
    ]
    got = [exchange(first_sent, "lo")]
    for req in range(1, reqs):
        next_sent, got[-1], pieces = lax.optimization_barrier((sent[req], got[-1], pieces))
        got.append(exchange(next_sent, "lo"))

    place = jnp.stack([hi, lo, group]).astype(jnp.int32)
    steps = 4
    parts = LO // steps
    rows = parts * toks
    rows_f32 = jax.ShapeDtypeStruct((length * ROWS, LANES), jnp.float32)
    rows_spec = pl.BlockSpec((rows * ROWS, LANES), lambda i, *at: (i, 0))
    bias, skip = dt_bias.reshape(1, width), skip_gain.reshape(1, width)

    def whole(*shape):
        return pl.BlockSpec(shape, lambda i, *at: (0,) * len(shape))

    def own(lead):
        return [
            pl.BlockSpec((lead, piece), lambda i, at, *_, p=p: (0, p * LO + at[1]))
            for p in range(HI)
        ]

    def scratch(*lengths):
        return [pltpu.VMEM((n, LANES), jnp.float32) for n in lengths]

    end_rows = (states + 1) * ROWS
    leave_rows = reqs * ((states + 2) * ROWS + 2 * states)
    y, total, end = [], [], []
    for req in range(reqs):
        last = req == reqs - 1
        one_y, one_total, one_end, *leaving = pl.pallas_call(
            functools.partial(scan_kernel, req),
            grid_spec=pltpu.PrefetchScalarGridSpec(
                num_scalar_prefetch=2,
                grid=(steps,),
                in_specs=[pl.BlockSpec((parts, toks, sent_width), lambda i, *at: (i, 0, 0))]
                + [whole(rank, piece)] * HI
                + own(states)
                + own(1) * 2
                + ([whole(end_rows, LANES)] * req + [whole(reqs, states, piece)] if last else []),
                out_specs=([whole(leave_rows, LANES)] if last else [])
                + [rows_spec, rows_spec, whole(end_rows, LANES)],
                scratch_shapes=scratch(
                    rows * ROWS, rows * ROWS, 2 * states * rows, states * ROWS, ROWS, end_rows
                ),
            ),
            out_shape=(
                [jax.ShapeDtypeStruct((leave_rows, LANES), jnp.bfloat16)] if last else []
            )
            + [rows_f32, rows_f32, jax.ShapeDtypeStruct((end_rows, LANES), jnp.float32)],
            compiler_params=params(60),
            cost_estimate=cost(15),
            name="scan",
        )(
            place, new_lengths, got[req], *pieces, *[decay_rate] * HI, *[bias] * HI,
            *[skip] * HI, *(end + [seed] if last else []),
        )
        if last:
            leaving, one_y, one_total, one_end = one_y, one_total, one_end, leaving[0]
        y.append(one_y)
        total.append(one_total)
        end.append(one_end)

    arrived = [lax.ppermute(leaving, "hi", shifts(HI, by)) for by in range(1, HI)]
    carry, *finals = pl.pallas_call(
        join_kernel,
        grid_spec=pltpu.PrefetchScalarGridSpec(
            num_scalar_prefetch=1,
            grid=(1,),
            in_specs=[whole(leave_rows, LANES)] * HI + [whole(end_rows, LANES)] * reqs + own(states),
            out_specs=[whole(reqs, states, ROWS, LANES)] + [whole(reqs, states, piece)] * HI,
            scratch_shapes=scratch(states * ROWS, states * ROWS),
        ),
        out_shape=[jax.ShapeDtypeStruct((reqs, states, ROWS, LANES), jnp.float32)]
        + [jax.ShapeDtypeStruct((reqs, states, piece), jnp.bfloat16)] * HI,
        compiler_params=params(60),
        name="join",
    )(place, leaving, *arrived, *end, *[decay_rate] * HI)

    back = []
    for req in range(reqs):
        out = pl.pallas_call(
            functools.partial(correct_kernel, req),
            grid_spec=pltpu.PrefetchScalarGridSpec(
                num_scalar_prefetch=2,
                grid=(steps,),
                in_specs=[
                    pl.BlockSpec(
                        (parts, toks, LANES), lambda i, *at: (i, 0, sent_width // LANES - 1)
                    ),
                    rows_spec,
                    rows_spec,
                    pl.BlockSpec((1, states, ROWS, LANES), lambda i, *at, req=req: (req, 0, 0, 0)),
                ]
                + own(states),
                out_specs=pl.BlockSpec((parts, toks, chans), lambda i, *at: (i, 0, 0)),
                scratch_shapes=scratch(rows * ROWS, states * rows, states * ROWS),
            ),
            out_shape=jax.ShapeDtypeStruct((LO, toks, chans), jnp.bfloat16),
            compiler_params=params(60),
            cost_estimate=cost(9),
            name="correct",
        )(place, new_lengths, got[req], y[req], total[req], carry, *[decay_rate] * HI)
        if req == reqs - 1:
            held = finals[HI - 1]
            for to in range(HI - 1):
                moved = lax.ppermute(finals[to], "hi", [(HI - 1, to)])
                held = jnp.where(hi == to, moved, held)
            out, held = lax.optimization_barrier((out, held))
        back.append(exchange(out, "lo"))

    fresh = [held] + [lax.ppermute(held, "cache", shifts(groups, by)) for by in range(1, groups)]
    fresh = jnp.stack(fresh).reshape(count, -1)
    source_group = lax.rem(group - jnp.arange(groups, dtype=jnp.int32) + groups, groups)
    request = (source_group[:, None] * reqs + jnp.arange(reqs, dtype=jnp.int32)[None, :]).reshape(-1)
    ids = jnp.arange(count, dtype=jnp.int32)
    ranks = jnp.sum((owners[:, None] == owners[None, :]) & (ids[None, :] < ids[:, None]), axis=1)
    target = evict_order[0][ranks]
    hits = (target[request][:, None] == slot_ids[None, :]) & (owners[request] == group)[:, None]
    rows = jnp.dot(
        hits.T.astype(jnp.bfloat16), fresh, preferred_element_type=jnp.float32
    ).astype(jnp.bfloat16)
    updated = jnp.where(jnp.any(hits, axis=0)[:, None], rows, stored)

    mixed = None
    for req in range(reqs):
        mixed = pl.pallas_call(
            unpack_kernel,
            grid=(1,),
            out_shape=jax.ShapeDtypeStruct(conv_out.shape, jnp.bfloat16),
            in_specs=[pl.BlockSpec((LO, toks, chans), lambda i: (0, 0, 0))]
            + ([] if mixed is None else [pl.BlockSpec(memory_space=pl.ANY)]),
            out_specs=pl.BlockSpec((1, toks, width), lambda i, req=req: (req, 0, 0)),
            input_output_aliases={} if mixed is None else {1: 0},
            compiler_params=params(16),
            name="unpack",
        )(*([back[req]] if mixed is None else [back[req], mixed]))
    return mixed, updated.reshape(cache_states.shape)


def solution(mesh):
    fine = Mesh(mesh.devices.reshape(mesh.shape["cache"], HI, LO, mesh.shape["head"]),
                ("cache", "hi", "lo", "head"))
    ctx = ("hi", "lo")
    in_specs = (
        P("cache", ctx, "head"),
        P("cache", ctx, None),
        P("cache", ctx, None),
        P(ctx, "head"),
        P("head"),
        P(None, "head"),
        P("head"),
        P("cache", "head", None, ctx),
        P(),
        P(),
        P("cache", None),
        P(),
    )
    out_specs = (P("cache", ctx, "head"), P("cache", "head", None, ctx))
    return jax.shard_map(
        on_device, mesh=fine, in_specs=in_specs, out_specs=out_specs, check_vma=False
    )
```

time: 1060 us -> 167 us (0.16)
  waiting for transfers between devices: 659 us -> 31.6 us
  other arithmetic: 206 us -> 2.27 us
  matrix products: 70.2 us -> 0.64 us
  Pallas kernels: 0 us -> 68.1 us
  blocking collectives: 46.9 us -> 0 us
  starting transfers between devices: 9.93 us -> 52.9 us
  local copies, waits for them, and re-layouts: 40.7 us -> 8.27 us
  between operations: 14 us -> 0.93 us
    all_gather x3 -> x0, waiting for transfers between devices: 507 us -> none  [the longest x2 407 us: entering(): pieces = jax.tree.map(lambda part: lax.all_gather(part, axis), value)]
    psum x1 -> x0, waiting for transfers between devices: 144 us -> none  [broadcast(): return lax.psum(kept, axis)]
    select_n x33 -> x2, other arithmetic: 71.8 us -> 0.01 us  [the longest x1 0.01 us: on_device(): target = evict_order[0][ranks]]
    dot_general x70 -> x2, matrix products: 70.2 us -> 0.64 us  [the longest x1 0.4 us: on_device(): jnp.dot(hits.T.astype(jnp.bfloat16), fresh, preferred_element_type=jnp.fl...]
    pallas_call x0 -> x10, Pallas kernels: none -> 68.1 us  [the longest x2 33.5 us: on_device(): pl.pallas_call(functools.partial(scan_kernel, req), grid_spec=pltpu.Prefe...]
    while x56 -> x0, other arithmetic: 48.4 us -> none
    all_gather x1 -> x0, blocking collectives: 46.9 us -> none  [on_device(): lax.all_gather(seed_piece, 'ctx', axis=2, tiled=True)]
    add x19 -> x1, other arithmetic: 44.6 us -> 0.07 us  [on_device(): source_group[:, None] * reqs + jnp.arange(reqs, dtype=jnp.int32)[None, :]]
  transfers between devices with their start and end apart: 6 -> 20, of which waited for: 6 -> 12; matrix products, arithmetic and copies ran while one was open for 1% -> 5% of each run, Pallas kernels for 0% -> 21%
where the time goes in v2:
time: 167 us; the launch traced here: 165 us
  Pallas kernels  68.1 us (41%)
  starting transfers between devices  52.9 us (32%)
  waiting for transfers between devices  31.6 us (19%)
  local copies, waits for them, and re-layouts  8.27 us (5%)
  other arithmetic  2.27 us (1%)
    pallas_call x2, Pallas kernels, on_device(): pl.pallas_call(functools.partial(scan_kernel, req), grid_spec=pltpu.Prefe...  33.5 us
    all_to_all x5, starting transfers between devices, exchange(): return lax.all_to_all(array, axis, split_axis=0, concat_axis=0, tiled=True)  27.9 us
    pallas_call x2, Pallas kernels, on_device(): pl.pallas_call(functools.partial(correct_kernel, req), grid_spec=pltpu.Pr...  23 us
    all_to_all x5, waiting for transfers between devices, exchange(): return lax.all_to_all(array, axis, split_axis=0, concat_axis=0, tiled=True)  14.7 us
    ppermute x3, starting transfers between devices, on_device(): lax.ppermute(leaving, 'hi', shifts(HI, by))  8.71 us
    ppermute x3, waiting for transfers between devices, on_device(): lax.ppermute(leaving, 'hi', shifts(HI, by))  6.71 us
    unnamed x43, local copies, waits for them, and re-layouts  6.24 us
    ppermute x3, waiting for transfers between devices, on_device(): lax.ppermute(quarter, 'cache', shifts(groups, by))  5.89 us
  transfers between devices with their start and end apart: 20, of which 12 were waited for; matrix products, arithmetic and copies ran while one was open for 5% of the time, Pallas kernels for 21%

profile of v2, /device:TPU:8, one launch (start us, length us, event | category | flops | bytes accessed | tf_op | source)
XLA Modules:
  0.0 164.8 jit_solution(646735267835143440)
XLA Ops:
  0.7 1.6 spread.1
  2.2 11.3 %all-to-all-start.1 = ((bf16[32,16,256]{2,1,0:T(8,128)(2,1)}), bf16[32,16,256]{2,1,0:T(8,128)(2,1)S(1)}, u32[]{:S(2)}, u32[]{:S(2)}) async-start(bf16[32,16,256]{2,1,0:T(8,128)(2,1)} %spread.1), calls=%async_computation.1 | async-start | bytes 524288 | tf_op jit(solution)/shard_map/all_to_all | solution.py:269
  16.6 1.7 %collective-permute-start = (bf16[2,16,256]{2,1,0:T(8,128)(2,1)S(1)}, bf16[2,16,256]{2,1,0:T(8,128)(2,1)S(1)}, u32[]{:S(2)}, u32[]{:S(2)}) collective-permute-start(bf16[2,16,256]{2,1,0:T(8,128)(2,1)S(1)} %get-tuple-element.52), channel_id=1, source_target_pairs={{0,64},{64,128},{128,192},{192,0},{1,65},{65,129},{129,193},{193,1... | collective-permute-start | bytes 49160 | tf_op jit(solution)/shard_map/ppermute | solution.py:296
  19.2 2.4 %collective-permute-start.2 = (bf16[2,16,256]{2,1,0:T(8,128)(2,1)S(1)}, bf16[2,16,256]{2,1,0:T(8,128)(2,1)S(1)}, u32[]{:S(2)}, u32[]{:S(2)}) collective-permute-start(bf16[2,16,256]{2,1,0:T(8,128)(2,1)S(1)} %get-tuple-element.53), channel_id=1, source_target_pairs={{0,192},{64,0},{128,64},{192,128},{1,193},{65,1},{129,65},{193,129... | collective-permute-start | bytes 49160 | tf_op jit(solution)/shard_map/ppermute | solution.py:296
  22.3 2.6 %pack.3 = bf16[8,64,1664]{2,1,0:T(8,128)(2,1)} custom-call(bf16[2,64,8192]{2,1,0:T(8,128)(2,1)} %x_ref.3, bf16[2,64,512]{2,1,0:T(8,128)(2,1)} %dt_ref.3, f32[2,64,32]{2,1,0:T(8,128)} %copy.21.proj_ref), custom_call_target="tpu_custom_call" | custom-call | tf_op jit(solution)/shard_map/pack/pallas_call | solution.py:300
  26.2 4.7 %all-to-all-start = ((bf16[8,64,1664]{2,1,0:T(8,128)(2,1)}), bf16[8,64,1664]{2,1,0:T(8,128)(2,1)S(1)}, u32[]{:S(2)}, u32[]{:S(2)}) async-start(bf16[8,64,1664]{2,1,0:T(8,128)(2,1)} %pack.3), calls=%async_computation | async-start | bytes 3407872 | tf_op jit(solution)/shard_map/all_to_all | solution.py:269
  31.5 2.9 %collective-permute-start.4 = (bf16[512,256]{1,0:T(8,128)(2,1)S(1)}, bf16[512,256]{1,0:T(8,128)(2,1)S(1)}, u32[]{:S(2)}, u32[]{:S(2)}) collective-permute-start(bf16[512,256]{1,0:T(8,128)(2,1)S(1)} %bitcast.52), channel_id=1, source_target_pairs={{0,128},{64,192},{128,0},{192,64},{1,129},{65,193},{129,1},{193,65... | collective-permute-start | bytes 786440 | tf_op jit(solution)/shard_map/ppermute | solution.py:316
  35.4 2.6 %pack.2 = bf16[8,64,1664]{2,1,0:T(8,128)(2,1)} custom-call(bf16[2,64,8192]{2,1,0:T(8,128)(2,1)} %x_ref.3, bf16[2,64,512]{2,1,0:T(8,128)(2,1)} %dt_ref.3, f32[2,64,32]{2,1,0:T(8,128)} %copy.21.proj_ref), custom_call_target="tpu_custom_call" | custom-call | tf_op jit(solution)/shard_map/pack/pallas_call | solution.py:300
  38.0 2.1 %collective-permute-done.3.refs_1_ = bf16[512,256]{1,0:T(8,128)(2,1)S(1)} collective-permute-done((bf16[512,256]{1,0:T(8,128)(2,1)S(1)}, bf16[512,256]{1,0:T(8,128)(2,1)S(1)}, u32[]{:S(2)}, u32[]{:S(2)}) %collective-permute-start.3) | collective-permute-done | bytes 262176 | tf_op jit(solution)/shard_map/ppermute | solution.py:316
  40.1 1.7 %collective-permute-done.4.refs_2_ = bf16[512,256]{1,0:T(8,128)(2,1)S(1)} collective-permute-done((bf16[512,256]{1,0:T(8,128)(2,1)S(1)}, bf16[512,256]{1,0:T(8,128)(2,1)S(1)}, u32[]{:S(2)}, u32[]{:S(2)}) %collective-permute-start.4) | collective-permute-done | bytes 262176 | tf_op jit(solution)/shard_map/ppermute | solution.py:316
  42.6 2.0 %collective-permute-done.5.refs_3_ = bf16[512,256]{1,0:T(8,128)(2,1)S(1)} collective-permute-done((bf16[512,256]{1,0:T(8,128)(2,1)S(1)}, bf16[512,256]{1,0:T(8,128)(2,1)S(1)}, u32[]{:S(2)}, u32[]{:S(2)}) %collective-permute-start.5) | collective-permute-done | bytes 262176 | tf_op jit(solution)/shard_map/ppermute | solution.py:316
  44.6 6.8 %all-to-all-done.got_ref.tail_ref = bf16[8,64,1664]{2,1,0:T(8,128)(2,1)S(1)} async-done(((bf16[8,64,1664]{2,1,0:T(8,128)(2,1)}), bf16[8,64,1664]{2,1,0:T(8,128)(2,1)S(1)}, u32[]{:S(2)}, u32[]{:S(2)}) %all-to-all-start) | async-done | bytes 1703968 | tf_op jit(solution)/shard_map/all_to_all | solution.py:269
  51.4 3.6 %all-to-all-start.2 = ((bf16[8,64,1664]{2,1,0:T(8,128)(2,1)}), bf16[8,64,1664]{2,1,0:T(8,128)(2,1)S(1)}, u32[]{:S(2)}, u32[]{:S(2)}) async-start(bf16[8,64,1664]{2,1,0:T(8,128)(2,1)} %pack.2), calls=%async_computation.2 | async-start | bytes 3407872 | tf_op jit(solution)/shard_map/all_to_all | solution.py:269
  55.6 16.7 %scan.2 = (f32[4096,128]{1,0:T(8,128)}, f32[4096,128]{1,0:T(8,128)}, f32[136,128]{1,0:T(8,128)}) custom-call(s32[3]{0:T(128)} %pad_add_fusion.place_ref, s32[8]{0:T(128)} %lengths_ref.7, bf16[8,64,1664]{2,1,0:T(8,128)(2,1)} %copy-done.2, bf16[512,256]{1,0:T(8,128)(2,1)} %bitcast.54, bf16[512,256]{1,0:T(8,128)(2,1)} %copy-done.7, bf16[512,256]{1,0:T(8,128)(2,1)} %copy-done.8, ...), custom_call_target="tpu_custom_call" | custom-call | bytes 54000000 | tf_op jit(solution)/shard_map/scan/pallas_call | solution.py:348
  72.3 4.7 %all-to-all-done.2.got_ref.tail_ref = bf16[8,64,1664]{2,1,0:T(8,128)(2,1)S(1)} async-done(((bf16[8,64,1664]{2,1,0:T(8,128)(2,1)}), bf16[8,64,1664]{2,1,0:T(8,128)(2,1)S(1)}, u32[]{:S(2)}, u32[]{:S(2)}) %all-to-all-start.2) | async-done | bytes 1703968 | tf_op jit(solution)/shard_map/all_to_all | solution.py:269
  78.2 16.8 %scan.3 = (bf16[352,128]{1,0:T(8,128)(2,1)}, f32[4096,128]{1,0:T(8,128)}, f32[4096,128]{1,0:T(8,128)}, f32[136,128]{1,0:T(8,128)}) custom-call(s32[3]{0:T(128)} %pad_add_fusion.place_ref, s32[8]{0:T(128)} %lengths_ref.7, bf16[8,64,1664]{2,1,0:T(8,128)(2,1)} %copy-done.3, bf16[512,256]{1,0:T(8,128)(2,1)} %bitcast.55, bf16[512,256]{1,0:T(8,128)(2,1)} %copy-done.7, ...), custom_call_target="tpu_custom_call" | custom-call | bytes 54000000 | tf_op jit(solution)/shard_map/scan/pallas_call | solution.py:348
  95.1 2.4 %collective-permute-start.6 = (bf16[352,128]{1,0:T(8,128)(2,1)}, bf16[352,128]{1,0:T(8,128)(2,1)S(1)}, u32[]{:S(2)}, u32[]{:S(2)}) collective-permute-start(bf16[352,128]{1,0:T(8,128)(2,1)} %get-tuple-element.35.refs_0_), channel_id=1, source_target_pairs={{0,16},{16,32},{32,48},{48,0},{1,17},{17,33},{33,49},{49,1},{2,18}... | collective-permute-start | bytes 270344 | tf_op jit(solution)/shard_map/ppermute | solution.py:381
  97.5 2.7 %collective-permute-start.7 = (bf16[352,128]{1,0:T(8,128)(2,1)}, bf16[352,128]{1,0:T(8,128)(2,1)S(1)}, u32[]{:S(2)}, u32[]{:S(2)}) collective-permute-start(bf16[352,128]{1,0:T(8,128)(2,1)} %get-tuple-element.35.refs_0_), channel_id=1, source_target_pairs={{0,32},{16,48},{32,0},{48,16},{1,33},{17,49},{33,1},{49,17},{2,34}... | collective-permute-start | bytes 270344 | tf_op jit(solution)/shard_map/ppermute | solution.py:381
  100.2 3.5 %collective-permute-start.8 = (bf16[352,128]{1,0:T(8,128)(2,1)}, bf16[352,128]{1,0:T(8,128)(2,1)S(1)}, u32[]{:S(2)}, u32[]{:S(2)}) collective-permute-start(bf16[352,128]{1,0:T(8,128)(2,1)} %get-tuple-element.35.refs_0_), channel_id=1, source_target_pairs={{0,48},{16,0},{32,16},{48,32},{1,49},{17,1},{33,17},{49,33},{2,50}... | collective-permute-start | bytes 270344 | tf_op jit(solution)/shard_map/ppermute | solution.py:381
  103.8 2.9 %collective-permute-done.7.refs_2_ = bf16[352,128]{1,0:T(8,128)(2,1)S(1)} collective-permute-done((bf16[352,128]{1,0:T(8,128)(2,1)}, bf16[352,128]{1,0:T(8,128)(2,1)S(1)}, u32[]{:S(2)}, u32[]{:S(2)}) %collective-permute-start.7) | collective-permute-done | bytes 90144 | tf_op jit(solution)/shard_map/ppermute | solution.py:381
  106.7 3.8 %collective-permute-done.8.refs_3_ = bf16[352,128]{1,0:T(8,128)(2,1)S(1)} collective-permute-done((bf16[352,128]{1,0:T(8,128)(2,1)}, bf16[352,128]{1,0:T(8,128)(2,1)S(1)}, u32[]{:S(2)}, u32[]{:S(2)}) %collective-permute-start.8) | collective-permute-done | bytes 90144 | tf_op jit(solution)/shard_map/ppermute | solution.py:381
  111.1 2.6 %join.1 = (f32[2,16,8,128]{3,2,1,0:T(8,128)}, bf16[2,16,256]{2,1,0:T(8,128)(2,1)}, bf16[2,16,256]{2,1,0:T(8,128)(2,1)}, bf16[2,16,256]{2,1,0:T(8,128)(2,1)}, bf16[2,16,256]{2,1,0:T(8,128)(2,1)}) custom-call(s32[3]{0:T(128)} %pad_add_fusion.place_ref, bf16[352,128]{1,0:T(8,128)(2,1)} %get-tuple-element.35.refs_0_, bf16[352,128]{1,0:T(8,128)(2,1)} %copy-done.10, ...), custom_call_target="tpu_custom_call" | custom-call | tf_op jit(solution)/shard_map/join/pallas_call | solution.py:382
  113.7 11.5 %correct.3 = bf16[8,64,1024]{2,1,0:T(8,128)(2,1)} custom-call(s32[3]{0:T(128)} %pad_add_fusion.place_ref, s32[8]{0:T(128)} %lengths_ref.7, bf16[8,64,1664]{2,1,0:T(8,128)(2,1)} %copy-done.2, f32[4096,128]{1,0:T(8,128)} %get-tuple-element.43.y_ref, f32[4096,128]{1,0:T(8,128)} %get-tuple-element.44.total_ref, f32[2,16,8,128]{3,2,1,0:T(8,128)} %get-tuple-element.37.carry_ref, ...), custom_call_target="tpu_custom_call" | custom-call | bytes 32400000 | tf_op jit(solution)/shard_map/correct/pallas_call | solution.py:399
  125.3 3.7 %all-to-all-start.4 = ((bf16[8,64,1024]{2,1,0:T(8,128)(2,1)}), bf16[8,64,1024]{2,1,0:T(8,128)(2,1)S(1)}, u32[]{:S(2)}, u32[]{:S(2)}) async-start(bf16[8,64,1024]{2,1,0:T(8,128)(2,1)} %correct.3), calls=%async_computation.4 | async-start | bytes 2097152 | tf_op jit(solution)/shard_map/all_to_all | solution.py:269
  129.7 1.3 collective-permute-start.11
  131.8 11.5 %correct.2 = bf16[8,64,1024]{2,1,0:T(8,128)(2,1)} custom-call(s32[3]{0:T(128)} %pad_add_fusion.place_ref, s32[8]{0:T(128)} %lengths_ref.7, bf16[8,64,1664]{2,1,0:T(8,128)(2,1)} %copy-done.3, f32[4096,128]{1,0:T(8,128)} %get-tuple-element.33.y_ref, f32[4096,128]{1,0:T(8,128)} %get-tuple-element.34.total_ref, f32[2,16,8,128]{3,2,1,0:T(8,128)} %get-tuple-element.37.carry_ref, ...), custom_call_target="tpu_custom_call" | custom-call | bytes 32400000 | tf_op jit(solution)/shard_map/correct/pallas_call | solution.py:399
  143.4 1.2 collective-permute-done.11
  144.6 4.5 %all-to-all-start.3 = ((bf16[8,64,1024]{2,1,0:T(8,128)(2,1)}), bf16[8,64,1024]{2,1,0:T(8,128)(2,1)S(1)}, u32[]{:S(2)}, u32[]{:S(2)}) async-start(bf16[8,64,1024]{2,1,0:T(8,128)(2,1)} %correct.2), calls=%async_computation.3 | async-start | bytes 2097152 | tf_op jit(solution)/shard_map/all_to_all | solution.py:269
  151.7 3.3 %collective-permute-start.13 = (bf16[2,16,256]{2,1,0:T(8,128)(2,1)S(1)}, bf16[2,16,256]{2,1,0:T(8,128)(2,1)S(1)}, u32[]{:S(2)}, u32[]{:S(2)}) collective-permute-start(bf16[2,16,256]{2,1,0:T(8,128)(2,1)S(1)} %select_select_fusion), channel_id=1, source_target_pairs={{0,128},{64,192},{128,0},{192,64},{1,129},{65,193},{129,1},{193,65... | collective-permute-start | bytes 49160 | tf_op jit(solution)/shard_map/ppermute | solution.py:429
  155.7 1.3 collective-permute-done.13
  156.9 1.8 %collective-permute-done.14 = bf16[2,16,256]{2,1,0:T(8,128)(2,1)S(1)} collective-permute-done((bf16[2,16,256]{2,1,0:T(8,128)(2,1)S(1)}, bf16[2,16,256]{2,1,0:T(8,128)(2,1)S(1)}, u32[]{:S(2)}, u32[]{:S(2)}) %collective-permute-start.14) | collective-permute-done | bytes 16416 | tf_op jit(solution)/shard_map/ppermute | solution.py:429
  161.2 2.5 %all-to-all-done.3.back_ref = bf16[8,64,1024]{2,1,0:T(8,128)(2,1)S(1)} async-done(((bf16[8,64,1024]{2,1,0:T(8,128)(2,1)}), bf16[8,64,1024]{2,1,0:T(8,128)(2,1)S(1)}, u32[]{:S(2)}, u32[]{:S(2)}) %all-to-all-start.3) | async-done | bytes 1048608 | tf_op jit(solution)/shard_map/all_to_all | solution.py:269
  (81 shorter events, 18.9 us)
Async XLA Ops:
  0.6 149.6 %copy-start = (s32[1,64]{1,0:T(1,128)S(1)}, s32[1,64]{1,0:T(1,128)}, u32[]{:S(2)}) copy-start(s32[1,64]{1,0:T(1,128)} %param.22) | copy-start | bytes 772
  0.6 15.6 %copy-start.15 = (s32[8]{0:T(128)S(1)}, s32[8]{0:T(128)}, u32[]{:S(2)}) copy-start(s32[8]{0:T(128)} %param.21) | copy-start | bytes 100
  0.7 20.9 %copy-start.13 = (f32[2,64,32]{1,2,0:T(8,128)S(1)}, f32[2,64,32]{1,2,0:T(8,128)}, u32[]{:S(2)}) copy-start(f32[2,64,32]{1,2,0:T(8,128)} %param.14) | copy-start | bytes 49156
  2.2 24.0 %all-to-all-start.1 = ((bf16[32,16,256]{2,1,0:T(8,128)(2,1)}), bf16[32,16,256]{2,1,0:T(8,128)(2,1)S(1)}, u32[]{:S(2)}, u32[]{:S(2)}) async-start(bf16[32,16,256]{2,1,0:T(8,128)(2,1)} %spread.1), calls=%async_computation.1 | async-start | bytes 524288 | tf_op jit(solution)/shard_map/all_to_all | solution.py:269
  16.6 8.3 %collective-permute-start = (bf16[2,16,256]{2,1,0:T(8,128)(2,1)S(1)}, bf16[2,16,256]{2,1,0:T(8,128)(2,1)S(1)}, u32[]{:S(2)}, u32[]{:S(2)}) collective-permute-start(bf16[2,16,256]{2,1,0:T(8,128)(2,1)S(1)} %get-tuple-element.52), channel_id=1, source_target_pairs={{0,64},{64,128},{128,192},{192,0},{1,65},{65,129},{129,193},{193,1... | collective-permute-start | bytes 49160 | tf_op jit(solution)/shard_map/ppermute | solution.py:296
  18.2 6.6 %collective-permute-start.1 = (bf16[2,16,256]{2,1,0:T(8,128)(2,1)S(1)}, bf16[2,16,256]{2,1,0:T(8,128)(2,1)S(1)}, u32[]{:S(2)}, u32[]{:S(2)}) collective-permute-start(bf16[2,16,256]{2,1,0:T(8,128)(2,1)S(1)} %get-tuple-element.54), channel_id=1, source_target_pairs={{0,128},{64,192},{128,0},{192,64},{1,129},{65,193},{129,1},{193,65... | collective-permute-start | bytes 49160 | tf_op jit(solution)/shard_map/ppermute | solution.py:296
  19.2 5.7 %collective-permute-start.2 = (bf16[2,16,256]{2,1,0:T(8,128)(2,1)S(1)}, bf16[2,16,256]{2,1,0:T(8,128)(2,1)S(1)}, u32[]{:S(2)}, u32[]{:S(2)}) collective-permute-start(bf16[2,16,256]{2,1,0:T(8,128)(2,1)S(1)} %get-tuple-element.53), channel_id=1, source_target_pairs={{0,192},{64,0},{128,64},{192,128},{1,193},{65,1},{129,65},{193,129... | collective-permute-start | bytes 49160 | tf_op jit(solution)/shard_map/ppermute | solution.py:296
  26.2 11.8 %copy-start.6 = (bf16[32,16,256]{2,1,0:T(8,128)(2,1)}, bf16[32,16,256]{2,1,0:T(8,128)(2,1)S(1)}, u32[]{:S(2)}) copy-start(bf16[32,16,256]{2,1,0:T(8,128)(2,1)S(1)} %all-to-all-done.1) | copy-start | bytes 786436
  26.2 25.1 %all-to-all-start = ((bf16[8,64,1664]{2,1,0:T(8,128)(2,1)}), bf16[8,64,1664]{2,1,0:T(8,128)(2,1)S(1)}, u32[]{:S(2)}, u32[]{:S(2)}) async-start(bf16[8,64,1664]{2,1,0:T(8,128)(2,1)} %pack.3), calls=%async_computation | async-start | bytes 3407872 | tf_op jit(solution)/shard_map/all_to_all | solution.py:269
  31.0 9.2 %collective-permute-start.3 = (bf16[512,256]{1,0:T(8,128)(2,1)S(1)}, bf16[512,256]{1,0:T(8,128)(2,1)S(1)}, u32[]{:S(2)}, u32[]{:S(2)}) collective-permute-start(bf16[512,256]{1,0:T(8,128)(2,1)S(1)} %bitcast.51), channel_id=1, source_target_pairs={{0,64},{64,128},{128,192},{192,0},{1,65},{65,129},{129,193},{193,1... | collective-permute-start | bytes 786440 | tf_op jit(solution)/shard_map/ppermute | solution.py:316
  31.5 10.4 %collective-permute-start.4 = (bf16[512,256]{1,0:T(8,128)(2,1)S(1)}, bf16[512,256]{1,0:T(8,128)(2,1)S(1)}, u32[]{:S(2)}, u32[]{:S(2)}) collective-permute-start(bf16[512,256]{1,0:T(8,128)(2,1)S(1)} %bitcast.52), channel_id=1, source_target_pairs={{0,128},{64,192},{128,0},{192,64},{1,129},{65,193},{129,1},{193,65... | collective-permute-start | bytes 786440 | tf_op jit(solution)/shard_map/ppermute | solution.py:316
  34.4 10.2 %collective-permute-start.5 = (bf16[512,256]{1,0:T(8,128)(2,1)S(1)}, bf16[512,256]{1,0:T(8,128)(2,1)S(1)}, u32[]{:S(2)}, u32[]{:S(2)}) collective-permute-start(bf16[512,256]{1,0:T(8,128)(2,1)S(1)} %bitcast.53), channel_id=1, source_target_pairs={{0,192},{64,0},{128,64},{192,128},{1,193},{65,1},{129,65},{193,129... | collective-permute-start | bytes 786440 | tf_op jit(solution)/shard_map/ppermute | solution.py:316
  44.6 6.8 %copy-start.9 = (bf16[512,256]{1,0:T(8,128)(2,1)}, bf16[512,256]{1,0:T(8,128)(2,1)S(1)}, u32[]{:S(2)}) copy-start(bf16[512,256]{1,0:T(8,128)(2,1)S(1)} %collective-permute-done.5.refs_3_) | copy-start | bytes 786436
  51.4 4.2 %copy-start.2 = (bf16[8,64,1664]{2,1,0:T(8,128)(2,1)}, bf16[8,64,1664]{2,1,0:T(8,128)(2,1)S(1)}, u32[]{:S(2)}) copy-start(bf16[8,64,1664]{2,1,0:T(8,128)(2,1)S(1)} %all-to-all-done.got_ref.tail_ref) | copy-start | bytes 5111812
  51.4 25.6 %all-to-all-start.2 = ((bf16[8,64,1664]{2,1,0:T(8,128)(2,1)}), bf16[8,64,1664]{2,1,0:T(8,128)(2,1)S(1)}, u32[]{:S(2)}, u32[]{:S(2)}) async-start(bf16[8,64,1664]{2,1,0:T(8,128)(2,1)} %pack.2), calls=%async_computation.2 | async-start | bytes 3407872 | tf_op jit(solution)/shard_map/all_to_all | solution.py:269
  95.1 8.7 %collective-permute-start.6 = (bf16[352,128]{1,0:T(8,128)(2,1)}, bf16[352,128]{1,0:T(8,128)(2,1)S(1)}, u32[]{:S(2)}, u32[]{:S(2)}) collective-permute-start(bf16[352,128]{1,0:T(8,128)(2,1)} %get-tuple-element.35.refs_0_), channel_id=1, source_target_pairs={{0,16},{16,32},{32,48},{48,0},{1,17},{17,33},{33,49},{49,1},{2,18}... | collective-permute-start | bytes 270344 | tf_op jit(solution)/shard_map/ppermute | solution.py:381
  97.5 9.2 %collective-permute-start.7 = (bf16[352,128]{1,0:T(8,128)(2,1)}, bf16[352,128]{1,0:T(8,128)(2,1)S(1)}, u32[]{:S(2)}, u32[]{:S(2)}) collective-permute-start(bf16[352,128]{1,0:T(8,128)(2,1)} %get-tuple-element.35.refs_0_), channel_id=1, source_target_pairs={{0,32},{16,48},{32,0},{48,16},{1,33},{17,49},{33,1},{49,17},{2,34}... | collective-permute-start | bytes 270344 | tf_op jit(solution)/shard_map/ppermute | solution.py:381
  100.2 10.2 %collective-permute-start.8 = (bf16[352,128]{1,0:T(8,128)(2,1)}, bf16[352,128]{1,0:T(8,128)(2,1)S(1)}, u32[]{:S(2)}, u32[]{:S(2)}) collective-permute-start(bf16[352,128]{1,0:T(8,128)(2,1)} %get-tuple-element.35.refs_0_), channel_id=1, source_target_pairs={{0,48},{16,0},{32,16},{48,32},{1,49},{17,1},{33,17},{49,33},{2,50}... | collective-permute-start | bytes 270344 | tf_op jit(solution)/shard_map/ppermute | solution.py:381
  103.8 6.7 %copy-start.10 = (bf16[352,128]{1,0:T(8,128)(2,1)}, bf16[352,128]{1,0:T(8,128)(2,1)S(1)}, u32[]{:S(2)}) copy-start(bf16[352,128]{1,0:T(8,128)(2,1)S(1)} %collective-permute-done.6.refs_1_) | copy-start | bytes 270340
  125.2 4.4 %copy-start.17 = (bf16[2,16,256]{2,1,0:T(8,128)(2,1)S(1)}, bf16[2,16,256]{2,1,0:T(8,128)(2,1)}, u32[]{:S(2)}) copy-start(bf16[2,16,256]{2,1,0:T(8,128)(2,1)} %get-tuple-element.40) | copy-start | bytes 49156
  125.3 5.7 %copy-start.16 = (bf16[2,16,256]{2,1,0:T(8,128)(2,1)S(1)}, bf16[2,16,256]{2,1,0:T(8,128)(2,1)}, u32[]{:S(2)}) copy-start(bf16[2,16,256]{2,1,0:T(8,128)(2,1)} %get-tuple-element.38) | copy-start | bytes 49156
  125.3 19.4 %all-to-all-start.4 = ((bf16[8,64,1024]{2,1,0:T(8,128)(2,1)}), bf16[8,64,1024]{2,1,0:T(8,128)(2,1)S(1)}, u32[]{:S(2)}, u32[]{:S(2)}) async-start(bf16[8,64,1024]{2,1,0:T(8,128)(2,1)} %correct.3), calls=%async_computation.4 | async-start | bytes 2097152 | tf_op jit(solution)/shard_map/all_to_all | solution.py:269
  129.0 14.4 %collective-permute-start.10 = (bf16[2,16,256]{2,1,0:T(8,128)(2,1)S(1)}, bf16[2,16,256]{2,1,0:T(8,128)(2,1)S(1)}, u32[]{:S(2)}, u32[]{:S(2)}) collective-permute-start(bf16[2,16,256]{2,1,0:T(8,128)(2,1)S(1)} %copy-done.18), channel_id=1, source_target_pairs={{48,16},{49,17},{50,18},{51,19},{52,20},{53,21},{54,22},{55,23},{5... | collective-permute-start | bytes 49160 | tf_op jit(solution)/shard_map/ppermute | solution.py:424
  129.7 14.9 %collective-permute-start.11 = (bf16[2,16,256]{2,1,0:T(8,128)(2,1)S(1)}, bf16[2,16,256]{2,1,0:T(8,128)(2,1)S(1)}, u32[]{:S(2)}, u32[]{:S(2)}) collective-permute-start(bf16[2,16,256]{2,1,0:T(8,128)(2,1)S(1)} %copy-done.17), channel_id=1, source_target_pairs={{48,0},{49,1},{50,2},{51,3},{52,4},{53,5},{54,6},{55,7},{56,8},{57... | collective-permute-start | bytes 49160 | tf_op jit(solution)/shard_map/ppermute | solution.py:424
  131.0 13.6 %collective-permute-start.9 = (bf16[2,16,256]{2,1,0:T(8,128)(2,1)S(1)}, bf16[2,16,256]{2,1,0:T(8,128)(2,1)S(1)}, u32[]{:S(2)}, u32[]{:S(2)}) collective-permute-start(bf16[2,16,256]{2,1,0:T(8,128)(2,1)S(1)} %copy-done.16), channel_id=1, source_target_pairs={{48,32},{49,33},{50,34},{51,35},{52,36},{53,37},{54,38},{55,39},{5... | collective-permute-start | bytes 49160 | tf_op jit(solution)/shard_map/ppermute | solution.py:424
  131.8 12.8 %copy-start.14 = (bf16[2,16,256]{2,1,0:T(8,128)(2,1)S(1)}, bf16[2,16,256]{2,1,0:T(8,128)(2,1)}, u32[]{:S(2)}) copy-start(bf16[2,16,256]{2,1,0:T(8,128)(2,1)} %get-tuple-element.41) | copy-start | bytes 49156
  143.3 6.0 %copy-start.1 = (s32[8,1]{0,1:T(1,128)S(1)}, s32[8,1]{0,1:T(1,128)}, u32[]{:S(2)}) copy-start(s32[8,1]{0,1:T(1,128)} %param.20) | copy-start | bytes 100
  143.3 15.5 %copy-start.5 = (bf16[8,8,16,256]{3,1,2,0:T(8,128)(2,1)S(1)}, bf16[8,8,16,256]{3,1,2,0:T(8,128)(2,1)}, u32[]{:S(2)}) copy-start(bf16[8,8,16,256]{3,1,2,0:T(8,128)(2,1)} %copy-done.4) | copy-start | bytes 1572868
  144.6 19.1 %all-to-all-start.3 = ((bf16[8,64,1024]{2,1,0:T(8,128)(2,1)}), bf16[8,64,1024]{2,1,0:T(8,128)(2,1)S(1)}, u32[]{:S(2)}, u32[]{:S(2)}) async-start(bf16[8,64,1024]{2,1,0:T(8,128)(2,1)} %correct.2), calls=%async_computation.3 | async-start | bytes 2097152 | tf_op jit(solution)/shard_map/all_to_all | solution.py:269
  151.5 4.1 %collective-permute-start.12 = (bf16[2,16,256]{2,1,0:T(8,128)(2,1)S(1)}, bf16[2,16,256]{2,1,0:T(8,128)(2,1)S(1)}, u32[]{:S(2)}, u32[]{:S(2)}) collective-permute-start(bf16[2,16,256]{2,1,0:T(8,128)(2,1)S(1)} %select_select_fusion), channel_id=1, source_target_pairs={{0,64},{64,128},{128,192},{192,0},{1,65},{65,129},{129,193},{193,1... | collective-permute-start | bytes 49160 | tf_op jit(solution)/shard_map/ppermute | solution.py:429
  151.7 5.3 %collective-permute-start.13 = (bf16[2,16,256]{2,1,0:T(8,128)(2,1)S(1)}, bf16[2,16,256]{2,1,0:T(8,128)(2,1)S(1)}, u32[]{:S(2)}, u32[]{:S(2)}) collective-permute-start(bf16[2,16,256]{2,1,0:T(8,128)(2,1)S(1)} %select_select_fusion), channel_id=1, source_target_pairs={{0,128},{64,192},{128,0},{192,64},{1,129},{65,193},{129,1},{193,65... | collective-permute-start | bytes 49160 | tf_op jit(solution)/shard_map/ppermute | solution.py:429
  155.0 3.7 %collective-permute-start.14 = (bf16[2,16,256]{2,1,0:T(8,128)(2,1)S(1)}, bf16[2,16,256]{2,1,0:T(8,128)(2,1)S(1)}, u32[]{:S(2)}, u32[]{:S(2)}) collective-permute-start(bf16[2,16,256]{2,1,0:T(8,128)(2,1)S(1)} %select_select_fusion), channel_id=1, source_target_pairs={{0,192},{64,0},{128,64},{192,128},{1,193},{65,1},{129,65},{193,129... | collective-permute-start | bytes 49160 | tf_op jit(solution)/shard_map/ppermute | solution.py:429
  (7 other events, 12.6 us)

commit v3 on v2

--- a/solution.py
+++ b/solution.py
@@ -21,7 +21,7 @@
     return pl.CostEstimate(flops=0, bytes_accessed=int(us * 3.6e6), transcendentals=0)
 
 
-def spread_kernel(group_ref, w_ref, out_ref):
+def spread_kernel(place_ref, w_ref, out_ref):
     width = w_ref.shape[1] // LO
     for lo in range(LO):
         block = w_ref[:, lo * width : (lo + 1) * width]
@@ -29,23 +29,18 @@
             out_ref[hi * LO + lo] = block
 
 
-def pack_kernel(x_ref, dt_ref, proj_ref, out_ref):
+def pack_kernel(place_ref, x_ref, *refs):
+    out_ref = refs[-1]
     piece = x_ref.shape[2] // (HI * LO)
-    chans, rank, nbc = piece * HI, dt_ref.shape[2], proj_ref.shape[2]
-    proj = proj_ref[0]
-    top = proj.astype(jnp.bfloat16)
-    low = (proj - top.astype(jnp.float32)).astype(jnp.bfloat16)
-    pad = jnp.zeros((proj.shape[0], LANES - 2 * nbc), jnp.bfloat16)
-    tail = jnp.concatenate([top, low, pad], axis=1)
     for lo in range(LO):
         for hi in range(HI):
             at = (hi * LO + lo) * piece
             out_ref[lo, :, hi * piece : (hi + 1) * piece] = x_ref[0, :, at : at + piece]
-        out_ref[lo, :, chans : chans + rank] = dt_ref[0]
-        out_ref[lo, :, chans + rank :] = tail
-
-
-def unpack_kernel(back_ref, *refs):
+        for ref in refs[:-1]:
+            out_ref[lo, :, HI * piece :] = ref[...]
+
+
+def unpack_kernel(place_ref, back_ref, *refs):
     out_ref = refs[-1]
     piece = back_ref.shape[2] // HI
     for lo in range(LO):
@@ -65,6 +60,10 @@
         scr[pl.ds((n + 1) * total_rows + offset, rows), :] = wide[:, LANES:]
 
 
+def request_of(place_ref, turn, group):
+    return group * 2 + lax.rem(place_ref[3] + turn, 2)
+
+
 def to_rows(scr, refs, count):
     for p, ref in enumerate(refs):
         for j in range(2):
@@ -72,12 +71,14 @@
             scr[pl.ds(2 * p + j, count, stride=ROWS), :] = value
 
 
-def scan_kernel(req, place_ref, lengths_ref, got_ref, *refs):
+def scan_kernel(turn, place_ref, lengths_ref, got_ref, *refs):
+    share_ref, refs = (got_ref, refs) if turn == 0 else (refs[0], refs[1:])
     w_refs, decay_refs, bias_refs, skip_refs = (refs[i * HI : (i + 1) * HI] for i in range(4))
     refs = refs[4 * HI :]
     before_refs, refs = refs[:-9], refs[-9:]
     if before_refs:
-        seed_ref, leave_ref, *before_refs = before_refs[-2], before_refs[-1], *before_refs[:-2]
+        leave_ref, seed_refs = before_refs[-1], before_refs[-1 - HI : -1]
+        before_refs = before_refs[: -1 - HI]
     y_ref, total_ref, end_ref, step_scr, x_scr, bc_scr, decay_scr, skip_scr, held_scr = refs
     parts, toks, _ = got_ref.shape
     rank, width = w_refs[0].shape
@@ -98,13 +99,14 @@
                 ]
         held_scr[...] = jnp.zeros_like(held_scr)
 
+    first = chans if turn == 0 else 0
     wide_x = got_ref[:, :, :chans].reshape(rows, chans).astype(jnp.float32)
-    dt = got_ref[:, :, chans : chans + rank].reshape(rows, rank)
-    tail = got_ref[:, :, chans + rank :].reshape(rows, LANES)
+    dt = share_ref[:, :, first : first + rank].reshape(rows, rank)
+    tail = share_ref[:, :, first + rank :].reshape(rows, LANES)
     position = (hi * pl.num_programs(0) + step_id) * rows + lax.broadcasted_iota(
         jnp.int32, (rows, 1), 0
     )
-    live = position < lengths_ref[group * 2 + req]
+    live = position < lengths_ref[request_of(place_ref, turn, group)]
     for by in range(HI):
         block = lax.rem(group - by + HI, HI)
         bias = bias_refs[0][...]
@@ -144,7 +146,7 @@
 
     held = tuple(held_scr[n * ROWS : (n + 1) * ROWS, :] for n in range(states))
     total, held = lax.fori_loop(
-        0, rows, per_tok, (held_scr[states * ROWS :, :], held), unroll=8
+        0, rows, per_tok, (held_scr[states * ROWS :, :], held), unroll=16
     )
     for n in range(states):
         held_scr[n * ROWS : (n + 1) * ROWS, :] = held[n]
@@ -154,19 +156,25 @@
     def _():
         end_ref[...] = held_scr[...]
         if before_refs:
-            leave_ref[...] = sent_rows(list(before_refs) + [held_scr], seed_ref)
-
-
-def sent_rows(ends, seed_ref):
+            leave_ref[...] = sent_rows(
+                place_ref, list(before_refs) + [held_scr], seed_refs
+            )
+
+
+def sent_rows(place_ref, ends, seed_refs):
     blocks = []
     for ref in ends:
         end = ref[...]
         total = end[-ROWS:]
         top = total.astype(jnp.bfloat16).astype(jnp.float32)
         blocks += [end[:-ROWS], top, total - top]
-    for req in range(len(ends)):
+    seed = sum(ref[...].astype(jnp.float32) for ref in seed_refs)
+    states = seed.shape[0] // len(ends)
+    seeds = [seed[req * states : (req + 1) * states] for req in range(len(ends))]
+    for turn in range(len(ends)):
+        mine = jnp.where(request_of(place_ref, turn, 0) == 0, seeds[0], seeds[1])
         for j in range(2):
-            blocks.append(seed_ref[req, :, j * LANES : (j + 1) * LANES].astype(jnp.float32))
+            blocks.append(mine[:, j * LANES : (j + 1) * LANES])
     return jnp.concatenate(blocks, axis=0).astype(jnp.bfloat16)
 
 
@@ -205,8 +213,8 @@
                 final_refs[p][req, :, j * LANES : (j + 1) * LANES] = value.astype(jnp.bfloat16)
 
 
-def correct_kernel(req, place_ref, lengths_ref, tail_ref, y_ref, total_ref, carry_ref, *refs):
-    decay_refs, (out_ref, y_scr, c_scr, decay_scr) = refs[:HI], refs[HI:]
+def correct_kernel(turn, place_ref, lengths_ref, y_ref, total_ref, carry_ref, *refs):
+    decay_refs, (tail_ref, out_ref, y_scr, c_scr, decay_scr) = refs[:HI], refs[HI:]
     parts, toks, _ = out_ref.shape
     states = decay_refs[0].shape[0]
     rows = parts * toks
@@ -231,11 +239,11 @@
         y_scr[at, :] = out
         return carry
 
-    lax.fori_loop(0, rows, per_tok, carry, unroll=8)
+    lax.fori_loop(0, rows, per_tok, carry, unroll=16)
     position = (place_ref[0] * pl.num_programs(0) + step_id) * rows + lax.broadcasted_iota(
         jnp.int32, (rows, 1), 0
     )
-    live = position < lengths_ref[place_ref[2] * 2 + req]
+    live = position < lengths_ref[request_of(place_ref, turn, place_ref[2])]
     for k in range(ROWS):
         block = jnp.where(live, y_scr[pl.ds(k, rows, stride=ROWS), :], 0.0)
         out_ref[:, :, k * LANES : (k + 1) * LANES] = block.astype(jnp.bfloat16).reshape(
@@ -261,9 +269,10 @@
     slots, piece = cache_states.shape[0], cache_states.shape[3]
     chans = width // LO
     length = LO * toks
+    place = jnp.stack([hi, lo, group, lax.axis_index("head")]).astype(jnp.int32)
     owners = hit_owner[:, 0]
     count = owners.shape[0]
-    sent_width = chans + rank + LANES
+    share_width = rank + LANES
 
     def exchange(array, axis):
         return lax.all_to_all(array, axis, split_axis=0, concat_axis=0, tiled=True)
@@ -274,13 +283,13 @@
         grid_spec=pltpu.PrefetchScalarGridSpec(
             num_scalar_prefetch=1,
             grid=(1,),
-            in_specs=[pl.BlockSpec((mine, width // groups), lambda i, at: (0, at[0]))],
+            in_specs=[pl.BlockSpec((mine, width // groups), lambda i, at: (0, at[2]))],
             out_specs=pl.BlockSpec((HI * LO, mine, piece), lambda i, at: (0, 0, 0)),
         ),
         out_shape=jax.ShapeDtypeStruct((HI * LO, mine, piece), jnp.bfloat16),
         compiler_params=params(60),
         name="spread",
-    )(group[None].astype(jnp.int32), dt_weight)
+    )(place, dt_weight)
     quarter = exchange(quarter, ("hi", "lo")).reshape(rank, piece)
 
     stored = cache_states.reshape(slots, -1)
@@ -290,37 +299,56 @@
         wanted.astype(jnp.bfloat16), stored, preferred_element_type=jnp.float32
     ).astype(jnp.bfloat16)
     picked = picked.reshape(groups, reqs, states, piece)
-    seed = lax.dynamic_index_in_dim(picked, group, 0, keepdims=False).astype(jnp.float32)
-    for by in range(1, groups):
-        leaving = lax.dynamic_index_in_dim(picked, lax.rem(group + by, groups), 0, keepdims=False)
-        seed = seed + lax.ppermute(leaving, "cache", shifts(groups, by)).astype(jnp.float32)
-    seed = seed.astype(jnp.bfloat16)
-
+    def of_turn(turn):
+        return lambda i, at, *_: (lax.rem(at[3] + turn, 2), 0, 0)
+
+    proj = lax.dynamic_index_in_dim(state_proj, place[3], 0, keepdims=False)
+    top = lax.reduce_precision(proj, 8, 7)
+    share = jnp.concatenate(
+        [
+            lax.dynamic_index_in_dim(dt_low, place[3], 0, keepdims=False),
+            top.astype(jnp.bfloat16),
+            (proj - top).astype(jnp.bfloat16),
+            jnp.zeros((toks, LANES - 2 * proj.shape[1]), jnp.bfloat16),
+        ],
+        axis=1,
+    )
+    sent_width = chans + share_width
     sent = [
         pl.pallas_call(
             pack_kernel,
-            grid=(1,),
-            in_specs=[
-                pl.BlockSpec((1, toks, n), lambda i, req=req: (req, 0, 0))
-                for n in (width, rank, state_proj.shape[2])
-            ],
-            out_specs=pl.BlockSpec((LO, toks, sent_width), lambda i: (0, 0, 0)),
-            out_shape=jax.ShapeDtypeStruct((LO, toks, sent_width), jnp.bfloat16),
+            grid_spec=pltpu.PrefetchScalarGridSpec(
+                num_scalar_prefetch=1,
+                grid=(1,),
+                in_specs=[pl.BlockSpec((1, toks, width), of_turn(turn))]
+                + [pl.BlockSpec((toks, share_width), lambda i, at: (0, 0))] * (turn == 0),
+                out_specs=pl.BlockSpec((LO, toks, columns), lambda i, at: (0, 0, 0)),
+            ),
+            out_shape=jax.ShapeDtypeStruct((LO, toks, columns), jnp.bfloat16),
             compiler_params=params(60),
             name="pack",
-        )(conv_out, dt_low, state_proj)
-        for req in range(reqs)
+        )(place, conv_out, *[share] * (turn == 0))
+        for turn, columns in enumerate((sent_width, chans))
     ]
-    first_sent, seed = lax.optimization_barrier((sent[0], seed))
+    first_sent, picked = lax.optimization_barrier((sent[0], picked))
+
+    def wanted_by(member):
+        return lax.dynamic_index_in_dim(picked, member, 0, keepdims=False).reshape(-1, piece)
+
     pieces = [quarter] + [
-        lax.ppermute(quarter, "cache", shifts(groups, by)) for by in range(1, groups)
+        lax.ppermute(
+            jnp.concatenate([quarter, wanted_by(lax.rem(group + by, groups))]),
+            "cache",
+            shifts(groups, by),
+        )
+        for by in range(1, groups)
     ]
-    got = [exchange(first_sent, "lo")]
-    for req in range(1, reqs):
-        next_sent, got[-1], pieces = lax.optimization_barrier((sent[req], got[-1], pieces))
-        got.append(exchange(next_sent, "lo"))
-
-    place = jnp.stack([hi, lo, group]).astype(jnp.int32)
+    own_seed = wanted_by(group)
+    first_got = exchange(first_sent, "lo")
+    second_sent, first_got, pieces = lax.optimization_barrier((sent[1], first_got, pieces))
+    got = [first_got, exchange(second_sent, "lo")]
+    second_share = lax.ppermute(first_got[:, :, chans:], "head", [(0, 1), (1, 0)])
+
     steps = 4
     parts = LO // steps
     rows = parts * toks
@@ -350,11 +378,18 @@
             grid_spec=pltpu.PrefetchScalarGridSpec(
                 num_scalar_prefetch=2,
                 grid=(steps,),
-                in_specs=[pl.BlockSpec((parts, toks, sent_width), lambda i, *at: (i, 0, 0))]
+                in_specs=[
+                    pl.BlockSpec((parts, toks, columns), lambda i, *at: (i, 0, 0))
+                    for columns in ((chans, share_width) if req else (sent_width,))
+                ]
                 + [whole(rank, piece)] * HI
                 + own(states)
                 + own(1) * 2
-                + ([whole(end_rows, LANES)] * req + [whole(reqs, states, piece)] if last else []),
+                + ([whole(end_rows, LANES)] * req
+                   + [whole(reqs * states, piece)]
+                   + [pl.BlockSpec((reqs * states, piece), lambda i, *at: (rank // (reqs * states), 0))]
+                   * (groups - 1)
+                   if last else []),
                 out_specs=([whole(leave_rows, LANES)] if last else [])
                 + [rows_spec, rows_spec, whole(end_rows, LANES)],
                 scratch_shapes=scratch(
@@ -369,8 +404,8 @@
             cost_estimate=cost(15),
             name="scan",
         )(
-            place, new_lengths, got[req], *pieces, *[decay_rate] * HI, *[bias] * HI,
-            *[skip] * HI, *(end + [seed] if last else []),
+            place, new_lengths, got[req], *([second_share] if req else []), *pieces, *[decay_rate] * HI, *[bias] * HI,
+            *[skip] * HI, *(end + [own_seed, *pieces[1:]] if last else []),
         )
         if last:
             leaving, one_y, one_total, one_end = one_y, one_total, one_end, leaving[0]
@@ -390,7 +425,7 @@
         ),
         out_shape=[jax.ShapeDtypeStruct((reqs, states, ROWS, LANES), jnp.float32)]
         + [jax.ShapeDtypeStruct((reqs, states, piece), jnp.bfloat16)] * HI,
-        compiler_params=params(60),
+        compiler_params=params(8),
         name="join",
     )(place, leaving, *arrived, *end, *[decay_rate] * HI)
 
@@ -402,14 +437,19 @@
                 num_scalar_prefetch=2,
                 grid=(steps,),
                 in_specs=[
-                    pl.BlockSpec(
-                        (parts, toks, LANES), lambda i, *at: (i, 0, sent_width // LANES - 1)
-                    ),
                     rows_spec,
                     rows_spec,
                     pl.BlockSpec((1, states, ROWS, LANES), lambda i, *at, req=req: (req, 0, 0, 0)),
                 ]
-                + own(states),
+                + own(states)
+                + [
+                    pl.BlockSpec(
+                        (parts, toks, LANES),
+                        lambda i, *at, at_lane=rank + (0 if req else chans): (
+                            i, 0, at_lane // LANES
+                        ),
+                    )
+                ],
                 out_specs=pl.BlockSpec((parts, toks, chans), lambda i, *at: (i, 0, 0)),
                 scratch_shapes=scratch(rows * ROWS, states * rows, states * ROWS),
             ),
@@ -417,7 +457,10 @@
             compiler_params=params(60),
             cost_estimate=cost(9),
             name="correct",
-        )(place, new_lengths, got[req], y[req], total[req], carry, *[decay_rate] * HI)
+        )(
+            place, new_lengths, y[req], total[req], carry, *[decay_rate] * HI,
+            second_share if req else first_got,
+        )
         if req == reqs - 1:
             held = finals[HI - 1]
             for to in range(HI - 1):
@@ -429,7 +472,8 @@
     fresh = [held] + [lax.ppermute(held, "cache", shifts(groups, by)) for by in range(1, groups)]
     fresh = jnp.stack(fresh).reshape(count, -1)
     source_group = lax.rem(group - jnp.arange(groups, dtype=jnp.int32) + groups, groups)
-    request = (source_group[:, None] * reqs + jnp.arange(reqs, dtype=jnp.int32)[None, :]).reshape(-1)
+    turns = lax.rem(jnp.arange(reqs, dtype=jnp.int32) + place[3], reqs)
+    request = (source_group[:, None] * reqs + turns[None, :]).reshape(-1)
     ids = jnp.arange(count, dtype=jnp.int32)
     ranks = jnp.sum((owners[:, None] == owners[None, :]) & (ids[None, :] < ids[:, None]), axis=1)
     target = evict_order[0][ranks]
@@ -443,15 +487,18 @@
     for req in range(reqs):
         mixed = pl.pallas_call(
             unpack_kernel,
-            grid=(1,),
+            grid_spec=pltpu.PrefetchScalarGridSpec(
+                num_scalar_prefetch=1,
+                grid=(1,),
+                in_specs=[pl.BlockSpec((LO, toks, chans), lambda i, at: (0, 0, 0))]
+                + ([] if mixed is None else [pl.BlockSpec(memory_space=pl.ANY)]),
+                out_specs=pl.BlockSpec((1, toks, width), of_turn(req)),
+            ),
             out_shape=jax.ShapeDtypeStruct(conv_out.shape, jnp.bfloat16),
-            in_specs=[pl.BlockSpec((LO, toks, chans), lambda i: (0, 0, 0))]
-            + ([] if mixed is None else [pl.BlockSpec(memory_space=pl.ANY)]),
-            out_specs=pl.BlockSpec((1, toks, width), lambda i, req=req: (req, 0, 0)),
-            input_output_aliases={} if mixed is None else {1: 0},
+            input_output_aliases={} if mixed is None else {2: 0},
             compiler_params=params(16),
             name="unpack",
-        )(*([back[req]] if mixed is None else [back[req], mixed]))
+        )(place, *([back[req]] if mixed is None else [back[req], mixed]))
     return mixed, updated.reshape(cache_states.shape)
 
 

time: 167 us -> 162 us (0.970)
  starting transfers between devices: 52.9 us -> 48.8 us
  waiting for transfers between devices: 31.6 us -> 29.3 us
  local copies, waits for them, and re-layouts: 8.27 us -> 10.2 us
    ppermute x6 -> x4, starting transfers between devices: 9.46 us -> 5.01 us  [the longest x3 5 us: on_device(): lax.ppermute(jnp.concatenate([quarter, wanted_by(lax.rem(group + by, grou...]
    ppermute x3, starting transfers between devices: 8.71 us -> 6.54 us  [on_device(): lax.ppermute(leaving, 'hi', shifts(HI, by))]
    pallas_call x4, Pallas kernels: 7.38 us -> 9.52 us  [the longest x2 6.24 us: on_device(): pl.pallas_call(pack_kernel, grid_spec=pltpu.PrefetchScalarGridSpec(num_sc...]
    all_to_all x5, waiting for transfers between devices: 14.7 us -> 12.7 us  [exchange(): return lax.all_to_all(array, axis, split_axis=0, concat_axis=0, tiled=True)]
    pallas_call x1, Pallas kernels: 2.62 us -> 0.71 us  [on_device(): pl.pallas_call(join_kernel, grid_spec=pltpu.PrefetchScalarGridSpec(num_sc...]
    all_to_all x5, starting transfers between devices: 27.9 us -> 29.7 us  [exchange(): return lax.all_to_all(array, axis, split_axis=0, concat_axis=0, tiled=True)]
    ppermute x6 -> x4, waiting for transfers between devices: 5.89 us -> 6.17 us  [the longest x3 6.16 us: on_device(): lax.ppermute(jnp.concatenate([quarter, wanted_by(lax.rem(group + by, grou...]
    unnamed x43 -> x38, local copies, waits for them, and re-layouts: 6.24 us -> 6.39 us
  transfers between devices with their start and end apart: 20 -> 18, of which waited for: 12 -> 11; matrix products, arithmetic and copies ran while one was open for 5% -> 5% of each run, Pallas kernels for 21% -> 22%
where the time goes in v3:
time: 162 us; the launch traced here: 160 us
  Pallas kernels  67.4 us (42%)
  starting transfers between devices  48.8 us (30%)
  waiting for transfers between devices  29.3 us (18%)
  local copies, waits for them, and re-layouts  10.2 us (6%)
  other arithmetic  2.42 us (1%)
    pallas_call x2, Pallas kernels, on_device(): pl.pallas_call(functools.partial(scan_kernel, req), grid_spec=pltpu.Prefe...  32.8 us
    all_to_all x5, starting transfers between devices, exchange(): return lax.all_to_all(array, axis, split_axis=0, concat_axis=0, tiled=True)  29.7 us
    pallas_call x2, Pallas kernels, on_device(): pl.pallas_call(functools.partial(correct_kernel, req), grid_spec=pltpu.Pr...  22.1 us
    all_to_all x5, waiting for transfers between devices, exchange(): return lax.all_to_all(array, axis, split_axis=0, concat_axis=0, tiled=True)  12.7 us
    ppermute x3, waiting for transfers between devices, on_device(): lax.ppermute(leaving, 'hi', shifts(HI, by))  7.75 us
    ppermute x3, starting transfers between devices, on_device(): lax.ppermute(leaving, 'hi', shifts(HI, by))  6.54 us
    unnamed x38, local copies, waits for them, and re-layouts  6.39 us
    pallas_call x2, Pallas kernels, on_device(): pl.pallas_call(pack_kernel, grid_spec=pltpu.PrefetchScalarGridSpec(num_sc...  6.24 us
  transfers between devices with their start and end apart: 18, of which 11 were waited for; matrix products, arithmetic and copies ran while one was open for 5% of the time, Pallas kernels for 22%

profile of v3, /device:TPU:8, one launch (start us, length us, event | category | flops | bytes accessed | tf_op | source)
XLA Modules:
  0.0 159.7 jit_solution(13542161483798816633)
XLA Ops:
  1.3 2.2 %spread.1 = bf16[32,16,256]{2,1,0:T(8,128)(2,1)} custom-call(s32[4]{0:T(128)} %get-tuple-element.62.place_ref, bf16[16,8192]{1,0:T(8,128)(2,1)} %w_ref.1), custom_call_target="tpu_custom_call" | custom-call | tf_op jit(solution)/shard_map/spread/pallas_call | solution.py:281
  3.5 11.3 %all-to-all-start.1 = ((bf16[32,16,256]{2,1,0:T(8,128)(2,1)}), bf16[32,16,256]{2,1,0:T(8,128)(2,1)S(1)}, u32[]{:S(2)}, u32[]{:S(2)}) async-start(bf16[32,16,256]{2,1,0:T(8,128)(2,1)} %spread.1), calls=%async_computation.1 | async-start | bytes 524288 | tf_op jit(solution)/shard_map/all_to_all | solution.py:278
  15.5 1.2 copy.21
  17.9 3.3 %pack.3 = bf16[8,64,1664]{2,1,0:T(8,128)(2,1)} custom-call(s32[4]{0:T(128)} %get-tuple-element.62.place_ref, bf16[2,64,8192]{2,1,0:T(8,128)(2,1)} %x_ref.3, bf16[64,640]{1,0:T(8,128)(2,1)} %maximum_maximum_fusion.refs_0_), custom_call_target="tpu_custom_call" | custom-call | tf_op jit(solution)/shard_map/pack/pallas_call | solution.py:318
  21.1 6.3 %all-to-all-done.1 = bf16[32,16,256]{2,1,0:T(8,128)(2,1)S(1)} async-done(((bf16[32,16,256]{2,1,0:T(8,128)(2,1)}), bf16[32,16,256]{2,1,0:T(8,128)(2,1)S(1)}, u32[]{:S(2)}, u32[]{:S(2)}) %all-to-all-start.1) | async-done | bytes 262176 | tf_op jit(solution)/shard_map/all_to_all | solution.py:278
  27.5 3.6 %all-to-all-start = ((bf16[8,64,1664]{2,1,0:T(8,128)(2,1)}), bf16[8,64,1664]{2,1,0:T(8,128)(2,1)S(1)}, u32[]{:S(2)}, u32[]{:S(2)}) async-start(bf16[8,64,1664]{2,1,0:T(8,128)(2,1)} %pack.3), calls=%async_computation | async-start | bytes 3407872 | tf_op jit(solution)/shard_map/all_to_all | solution.py:278
  31.8 1.7 %collective-permute-start = (bf16[544,256]{1,0:T(8,128)(2,1)S(1)}, bf16[544,256]{1,0:T(8,128)(2,1)S(1)}, u32[]{:S(2)}, u32[]{:S(2)}) collective-permute-start(bf16[544,256]{1,0:T(8,128)(2,1)S(1)} %get-tuple-element.54), channel_id=1, source_target_pairs={{0,64},{64,128},{128,192},{192,0},{1,65},{65,129},{129,193},{193,1... | collective-permute-start | bytes 835592 | tf_op jit(solution)/shard_map/ppermute | solution.py:339
  34.4 2.4 %collective-permute-start.2 = (bf16[544,256]{1,0:T(8,128)(2,1)S(1)}, bf16[544,256]{1,0:T(8,128)(2,1)}, u32[]{:S(2)}, u32[]{:S(2)}) collective-permute-start(bf16[544,256]{1,0:T(8,128)(2,1)S(1)} %get-tuple-element.52), channel_id=1, source_target_pairs={{0,192},{64,0},{128,64},{192,128},{1,193},{65,1},{129,65},{193,129... | collective-permute-start | bytes 835592 | tf_op jit(solution)/shard_map/ppermute | solution.py:339
  36.8 3.0 %pack.2 = bf16[8,64,1024]{2,1,0:T(8,128)(2,1)} custom-call(s32[4]{0:T(128)} %get-tuple-element.62.place_ref, bf16[2,64,8192]{2,1,0:T(8,128)(2,1)} %x_ref.3), custom_call_target="tpu_custom_call" | custom-call | tf_op jit(solution)/shard_map/pack/pallas_call | solution.py:318
  39.8 1.7 %collective-permute-done.refs_1_.refs_2_.refs_19_ = bf16[544,256]{1,0:T(8,128)(2,1)S(1)} collective-permute-done((bf16[544,256]{1,0:T(8,128)(2,1)S(1)}, bf16[544,256]{1,0:T(8,128)(2,1)S(1)}, u32[]{:S(2)}, u32[]{:S(2)}) %collective-permute-start) | collective-permute-done | bytes 278560 | tf_op jit(solution)/shard_map/ppermute | solution.py:339
  41.5 2.9 %collective-permute-done.1.refs_2_.refs_3_.refs_20_ = bf16[544,256]{1,0:T(8,128)(2,1)S(1)} collective-permute-done((bf16[544,256]{1,0:T(8,128)(2,1)S(1)}, bf16[544,256]{1,0:T(8,128)(2,1)S(1)}, u32[]{:S(2)}, u32[]{:S(2)}) %collective-permute-start.1) | collective-permute-done | bytes 278560 | tf_op jit(solution)/shard_map/ppermute | solution.py:339
  45.1 1.6 %collective-permute-done.2.refs_3_.refs_4_.refs_21_ = bf16[544,256]{1,0:T(8,128)(2,1)} collective-permute-done((bf16[544,256]{1,0:T(8,128)(2,1)S(1)}, bf16[544,256]{1,0:T(8,128)(2,1)}, u32[]{:S(2)}, u32[]{:S(2)}) %collective-permute-start.2) | collective-permute-done | bytes 278560 | tf_op jit(solution)/shard_map/ppermute | solution.py:339
  46.7 4.6 %all-to-all-done.got_ref.refs_4_ = bf16[8,64,1664]{2,1,0:T(8,128)(2,1)S(1)} async-done(((bf16[8,64,1664]{2,1,0:T(8,128)(2,1)}), bf16[8,64,1664]{2,1,0:T(8,128)(2,1)S(1)}, u32[]{:S(2)}, u32[]{:S(2)}) %all-to-all-start) | async-done | bytes 1703968 | tf_op jit(solution)/shard_map/all_to_all | solution.py:278
  51.3 3.6 %all-to-all-start.2 = ((bf16[8,64,1024]{2,1,0:T(8,128)(2,1)}), bf16[8,64,1024]{2,1,0:T(8,128)(2,1)S(1)}, u32[]{:S(2)}, u32[]{:S(2)}) async-start(bf16[8,64,1024]{2,1,0:T(8,128)(2,1)} %pack.2), calls=%async_computation.2 | async-start | bytes 2097152 | tf_op jit(solution)/shard_map/all_to_all | solution.py:278
  55.9 16.2 %scan.2 = (f32[4096,128]{1,0:T(8,128)}, f32[4096,128]{1,0:T(8,128)}, f32[136,128]{1,0:T(8,128)}) custom-call(s32[4]{0:T(128)} %get-tuple-element.62.place_ref, s32[8]{0:T(128)} %lengths_ref.7, bf16[8,64,1664]{2,1,0:T(8,128)(2,1)} %copy-done.10, bf16[512,256]{1,0:T(8,128)(2,1)} %bitcast.53, bf16[544,256]{1,0:T(8,128)(2,1)} %copy-done.13, ...), custom_call_target="tpu_custom_call" | custom-call | bytes 54000000 | tf_op jit(solution)/shard_map/scan/pallas_call | solution.py:376
  73.2 16.7 %scan.3 = (bf16[352,128]{1,0:T(8,128)(2,1)}, f32[4096,128]{1,0:T(8,128)}, f32[4096,128]{1,0:T(8,128)}, f32[136,128]{1,0:T(8,128)}) custom-call(s32[4]{0:T(128)} %get-tuple-element.62.place_ref, s32[8]{0:T(128)} %lengths_ref.7, bf16[8,64,1024]{2,1,0:T(8,128)(2,1)} %copy-done.12, bf16[8,64,640]{2,1,0:T(8,128)(2,1)} %collective-permute-done.3.refs_0_.refs_4_, ...), custom_call_target="tpu_custom_call" | custom-call | bytes 54000000 | tf_op jit(solution)/shard_map/scan/pallas_call | solution.py:376
  89.8 1.9 %collective-permute-start.4 = (bf16[352,128]{1,0:T(8,128)(2,1)}, bf16[352,128]{1,0:T(8,128)(2,1)S(1)}, u32[]{:S(2)}, u32[]{:S(2)}) collective-permute-start(bf16[352,128]{1,0:T(8,128)(2,1)} %get-tuple-element.35.refs_0_), channel_id=1, source_target_pairs={{0,16},{16,32},{32,48},{48,0},{1,17},{17,33},{33,49},{49,1},{2,18}... | collective-permute-start | bytes 270344 | tf_op jit(solution)/shard_map/ppermute | solution.py:416
  91.7 2.5 %collective-permute-start.5 = (bf16[352,128]{1,0:T(8,128)(2,1)}, bf16[352,128]{1,0:T(8,128)(2,1)S(1)}, u32[]{:S(2)}, u32[]{:S(2)}) collective-permute-start(bf16[352,128]{1,0:T(8,128)(2,1)} %get-tuple-element.35.refs_0_), channel_id=1, source_target_pairs={{0,32},{16,48},{32,0},{48,16},{1,33},{17,49},{33,1},{49,17},{2,34}... | collective-permute-start | bytes 270344 | tf_op jit(solution)/shard_map/ppermute | solution.py:416
  94.2 2.2 %collective-permute-start.6 = (bf16[352,128]{1,0:T(8,128)(2,1)}, bf16[352,128]{1,0:T(8,128)(2,1)S(1)}, u32[]{:S(2)}, u32[]{:S(2)}) collective-permute-start(bf16[352,128]{1,0:T(8,128)(2,1)} %get-tuple-element.35.refs_0_), channel_id=1, source_target_pairs={{0,48},{16,0},{32,16},{48,32},{1,49},{17,1},{33,17},{49,33},{2,50}... | collective-permute-start | bytes 270344 | tf_op jit(solution)/shard_map/ppermute | solution.py:416
  97.4 4.9 %collective-permute-done.5.refs_2_ = bf16[352,128]{1,0:T(8,128)(2,1)S(1)} collective-permute-done((bf16[352,128]{1,0:T(8,128)(2,1)}, bf16[352,128]{1,0:T(8,128)(2,1)S(1)}, u32[]{:S(2)}, u32[]{:S(2)}) %collective-permute-start.5) | collective-permute-done | bytes 90144 | tf_op jit(solution)/shard_map/ppermute | solution.py:416
  102.3 1.9 %collective-permute-done.6.refs_3_ = bf16[352,128]{1,0:T(8,128)(2,1)S(1)} collective-permute-done((bf16[352,128]{1,0:T(8,128)(2,1)}, bf16[352,128]{1,0:T(8,128)(2,1)S(1)}, u32[]{:S(2)}, u32[]{:S(2)}) %collective-permute-start.6) | collective-permute-done | bytes 90144 | tf_op jit(solution)/shard_map/ppermute | solution.py:416
  107.3 11.1 %correct.3 = bf16[8,64,1024]{2,1,0:T(8,128)(2,1)} custom-call(s32[4]{0:T(128)} %get-tuple-element.62.place_ref, s32[8]{0:T(128)} %lengths_ref.7, f32[4096,128]{1,0:T(8,128)} %get-tuple-element.43.y_ref, f32[4096,128]{1,0:T(8,128)} %get-tuple-element.44.total_ref, f32[2,16,8,128]{3,2,1,0:T(8,128)} %copy-done.2, f32[16,8192]{1,0:T(8,128)} %refs_3_.3, ...), custom_call_target="tpu_custom_call" | custom-call | bytes 32400000 | tf_op jit(solution)/shard_map/correct/pallas_call | solution.py:434
  118.4 6.3 %all-to-all-start.4 = ((bf16[8,64,1024]{2,1,0:T(8,128)(2,1)}), bf16[8,64,1024]{2,1,0:T(8,128)(2,1)S(1)}, u32[]{:S(2)}, u32[]{:S(2)}) async-start(bf16[8,64,1024]{2,1,0:T(8,128)(2,1)} %correct.3), calls=%async_computation.4 | async-start | bytes 2097152 | tf_op jit(solution)/shard_map/all_to_all | solution.py:278
  126.0 1.3 collective-permute-start.9
  127.3 11.1 %correct.2 = bf16[8,64,1024]{2,1,0:T(8,128)(2,1)} custom-call(s32[4]{0:T(128)} %get-tuple-element.62.place_ref, s32[8]{0:T(128)} %lengths_ref.7, f32[4096,128]{1,0:T(8,128)} %get-tuple-element.33.y_ref, f32[4096,128]{1,0:T(8,128)} %get-tuple-element.34.total_ref, f32[2,16,8,128]{3,2,1,0:T(8,128)} %copy-done.2, f32[16,8192]{1,0:T(8,128)} %refs_3_.3, ...), custom_call_target="tpu_custom_call" | custom-call | bytes 32400000 | tf_op jit(solution)/shard_map/correct/pallas_call | solution.py:434
  139.3 4.8 %all-to-all-start.3 = ((bf16[8,64,1024]{2,1,0:T(8,128)(2,1)}), bf16[8,64,1024]{2,1,0:T(8,128)(2,1)S(1)}, u32[]{:S(2)}, u32[]{:S(2)}) async-start(bf16[8,64,1024]{2,1,0:T(8,128)(2,1)} %correct.2), calls=%async_computation.3 | async-start | bytes 2097152 | tf_op jit(solution)/shard_map/all_to_all | solution.py:278
  146.5 1.7 %collective-permute-start.10 = (bf16[2,16,256]{2,1,0:T(8,128)(2,1)S(1)}, bf16[2,16,256]{2,1,0:T(8,128)(2,1)S(1)}, u32[]{:S(2)}, u32[]{:S(2)}) collective-permute-start(bf16[2,16,256]{2,1,0:T(8,128)(2,1)S(1)} %select_select_fusion), channel_id=1, source_target_pairs={{0,64},{64,128},{128,192},{192,0},{1,65},{65,129},{129,193},{193,1... | collective-permute-start | bytes 49160 | tf_op jit(solution)/shard_map/ppermute | solution.py:472
  149.1 2.4 %collective-permute-start.12 = (bf16[2,16,256]{2,1,0:T(8,128)(2,1)S(1)}, bf16[2,16,256]{2,1,0:T(8,128)(2,1)S(1)}, u32[]{:S(2)}, u32[]{:S(2)}) collective-permute-start(bf16[2,16,256]{2,1,0:T(8,128)(2,1)S(1)} %select_select_fusion), channel_id=1, source_target_pairs={{0,192},{64,0},{128,64},{192,128},{1,193},{65,1},{129,65},{193,129... | collective-permute-start | bytes 49160 | tf_op jit(solution)/shard_map/ppermute | solution.py:472
  151.6 1.8 %collective-permute-done.11 = bf16[2,16,256]{2,1,0:T(8,128)(2,1)S(1)} collective-permute-done((bf16[2,16,256]{2,1,0:T(8,128)(2,1)S(1)}, bf16[2,16,256]{2,1,0:T(8,128)(2,1)S(1)}, u32[]{:S(2)}, u32[]{:S(2)}) %collective-permute-start.11) | collective-permute-done | bytes 16416 | tf_op jit(solution)/shard_map/ppermute | solution.py:472
  154.8 1.6 %unpack.2.refs_0_ = bf16[2,64,8192]{2,1,0:T(8,128)(2,1)} custom-call(s32[4]{0:T(128)S(1)} %copy-done.7, bf16[8,64,1024]{2,1,0:T(8,128)(2,1)S(1)} %all-to-all-done.4.back_ref), custom_call_target="tpu_custom_call" | custom-call | tf_op jit(solution)/shard_map/unpack/pallas_call | solution.py:488
  156.4 1.7 %all-to-all-done.3.back_ref = bf16[8,64,1024]{2,1,0:T(8,128)(2,1)S(1)} async-done(((bf16[8,64,1024]{2,1,0:T(8,128)(2,1)}), bf16[8,64,1024]{2,1,0:T(8,128)(2,1)S(1)}, u32[]{:S(2)}, u32[]{:S(2)}) %all-to-all-start.3) | async-done | bytes 1048608 | tf_op jit(solution)/shard_map/all_to_all | solution.py:278
  158.1 1.6 %unpack.3 = bf16[2,64,8192]{2,1,0:T(8,128)(2,1)} custom-call(s32[4]{0:T(128)S(1)} %copy-done.7, bf16[8,64,1024]{2,1,0:T(8,128)(2,1)S(1)} %all-to-all-done.3.back_ref, bf16[2,64,8192]{2,1,0:T(8,128)(2,1)} %unpack.2.refs_0_), custom_call_target="tpu_custom_call", output_to_operand_aliasing={{}: (2, {})} | custom-call | tf_op jit(solution)/shard_map/unpack/pallas_call | solution.py:488
  (81 shorter events, 17.8 us)
Async XLA Ops:
  0.6 16.1 %copy-start = (bf16[2,64,512]{2,1,0:T(8,128)(2,1)S(1)}, bf16[2,64,512]{2,1,0:T(8,128)(2,1)}, u32[]{:S(2)}) copy-start(bf16[2,64,512]{2,1,0:T(8,128)(2,1)} %param.13) | copy-start | bytes 393220
  0.6 16.1 %copy-start.16 = (s32[8]{0:T(128)S(1)}, s32[8]{0:T(128)}, u32[]{:S(2)}) copy-start(s32[8]{0:T(128)} %param.21) | copy-start | bytes 100
  0.7 16.3 %copy-start.15 = (f32[2,64,32]{1,2,0:T(8,128)S(1)}, f32[2,64,32]{1,2,0:T(8,128)}, u32[]{:S(2)}) copy-start(f32[2,64,32]{1,2,0:T(8,128)} %param.14) | copy-start | bytes 49156
  3.5 24.0 %all-to-all-start.1 = ((bf16[32,16,256]{2,1,0:T(8,128)(2,1)}), bf16[32,16,256]{2,1,0:T(8,128)(2,1)S(1)}, u32[]{:S(2)}, u32[]{:S(2)}) async-start(bf16[32,16,256]{2,1,0:T(8,128)(2,1)} %spread.1), calls=%async_computation.1 | async-start | bytes 524288 | tf_op jit(solution)/shard_map/all_to_all | solution.py:278
  27.5 4.3 %copy-start.11 = (bf16[32,16,256]{2,1,0:T(8,128)(2,1)}, bf16[32,16,256]{2,1,0:T(8,128)(2,1)S(1)}, u32[]{:S(2)}) copy-start(bf16[32,16,256]{2,1,0:T(8,128)(2,1)S(1)} %all-to-all-done.1) | copy-start | bytes 786436
  27.5 23.8 %all-to-all-start = ((bf16[8,64,1664]{2,1,0:T(8,128)(2,1)}), bf16[8,64,1664]{2,1,0:T(8,128)(2,1)S(1)}, u32[]{:S(2)}, u32[]{:S(2)}) async-start(bf16[8,64,1664]{2,1,0:T(8,128)(2,1)} %pack.3), calls=%async_computation | async-start | bytes 3407872 | tf_op jit(solution)/shard_map/all_to_all | solution.py:278
  31.8 9.7 %collective-permute-start = (bf16[544,256]{1,0:T(8,128)(2,1)S(1)}, bf16[544,256]{1,0:T(8,128)(2,1)S(1)}, u32[]{:S(2)}, u32[]{:S(2)}) collective-permute-start(bf16[544,256]{1,0:T(8,128)(2,1)S(1)} %get-tuple-element.54), channel_id=1, source_target_pairs={{0,64},{64,128},{128,192},{192,0},{1,65},{65,129},{129,193},{193,1... | collective-permute-start | bytes 835592 | tf_op jit(solution)/shard_map/ppermute | solution.py:339
  33.4 10.9 %collective-permute-start.1 = (bf16[544,256]{1,0:T(8,128)(2,1)S(1)}, bf16[544,256]{1,0:T(8,128)(2,1)S(1)}, u32[]{:S(2)}, u32[]{:S(2)}) collective-permute-start(bf16[544,256]{1,0:T(8,128)(2,1)S(1)} %get-tuple-element.53), channel_id=1, source_target_pairs={{0,128},{64,192},{128,0},{192,64},{1,129},{65,193},{129,1},{193,65... | collective-permute-start | bytes 835592 | tf_op jit(solution)/shard_map/ppermute | solution.py:339
  34.4 12.3 %collective-permute-start.2 = (bf16[544,256]{1,0:T(8,128)(2,1)S(1)}, bf16[544,256]{1,0:T(8,128)(2,1)}, u32[]{:S(2)}, u32[]{:S(2)}) collective-permute-start(bf16[544,256]{1,0:T(8,128)(2,1)S(1)} %get-tuple-element.52), channel_id=1, source_target_pairs={{0,192},{64,0},{128,64},{192,128},{1,193},{65,1},{129,65},{193,129... | collective-permute-start | bytes 835592 | tf_op jit(solution)/shard_map/ppermute | solution.py:339
  41.5 2.9 %copy-start.13 = (bf16[544,256]{1,0:T(8,128)(2,1)}, bf16[544,256]{1,0:T(8,128)(2,1)S(1)}, u32[]{:S(2)}) copy-start(bf16[544,256]{1,0:T(8,128)(2,1)S(1)} %collective-permute-done.refs_1_.refs_2_.refs_19_) | copy-start | bytes 835588
  51.3 4.6 %copy-start.10 = (bf16[8,64,1664]{2,1,0:T(8,128)(2,1)}, bf16[8,64,1664]{2,1,0:T(8,128)(2,1)S(1)}, u32[]{:S(2)}) copy-start(bf16[8,64,1664]{2,1,0:T(8,128)(2,1)S(1)} %all-to-all-done.got_ref.refs_4_) | copy-start | bytes 5111812
  51.3 20.8 %all-to-all-start.2 = ((bf16[8,64,1024]{2,1,0:T(8,128)(2,1)}), bf16[8,64,1024]{2,1,0:T(8,128)(2,1)S(1)}, u32[]{:S(2)}, u32[]{:S(2)}) async-start(bf16[8,64,1024]{2,1,0:T(8,128)(2,1)} %pack.2), calls=%async_computation.2 | async-start | bytes 2097152 | tf_op jit(solution)/shard_map/all_to_all | solution.py:278
  55.9 16.2 %collective-permute-start.3 = (bf16[8,64,640]{2,1,0:T(8,128)(2,1)}, bf16[8,64,640]{2,1,0:T(8,128)(2,1)}, u32[]{:S(2)}, u32[]{:S(2)}) collective-permute-start(bf16[8,64,640]{2,1,0:T(8,128)(2,1)} %slice.3), channel_id=1, source_target_pairs={{0,1},{1,0},{2,3},{3,2},{4,5},{5,4},{6,7},{7,6},{8,9},{9,8},{10,11... | collective-permute-start | bytes 1966088 | tf_op jit(solution)/shard_map/ppermute | solution.py:350
  72.1 1.1 copy-start.12
  73.2 31.0 %copy-start.1 = (f32[16,8192]{1,0:T(8,128)S(1)}, f32[16,8192]{1,0:T(8,128)}, u32[]{:S(2)}) copy-start(f32[16,8192]{1,0:T(8,128)} %refs_3_.3) | copy-start | bytes 1572868
  73.2 31.0 %copy-start.3 = (f32[136,128]{1,0:T(8,128)S(1)}, f32[136,128]{1,0:T(8,128)}, u32[]{:S(2)}) copy-start(f32[136,128]{1,0:T(8,128)} %get-tuple-element.32.refs_17_.refs_4_) | copy-start | bytes 208900
  73.2 31.0 %copy-start.6 = (s32[4]{0:T(128)S(1)}, s32[4]{0:T(128)}, u32[]{:S(2)}) copy-start(s32[4]{0:T(128)} %get-tuple-element.62.place_ref) | copy-start | bytes 52
  89.8 7.5 %collective-permute-start.4 = (bf16[352,128]{1,0:T(8,128)(2,1)}, bf16[352,128]{1,0:T(8,128)(2,1)S(1)}, u32[]{:S(2)}, u32[]{:S(2)}) collective-permute-start(bf16[352,128]{1,0:T(8,128)(2,1)} %get-tuple-element.35.refs_0_), channel_id=1, source_target_pairs={{0,16},{16,32},{32,48},{48,0},{1,17},{17,33},{33,49},{49,1},{2,18}... | collective-permute-start | bytes 270344 | tf_op jit(solution)/shard_map/ppermute | solution.py:416
  91.7 10.5 %collective-permute-start.5 = (bf16[352,128]{1,0:T(8,128)(2,1)}, bf16[352,128]{1,0:T(8,128)(2,1)S(1)}, u32[]{:S(2)}, u32[]{:S(2)}) collective-permute-start(bf16[352,128]{1,0:T(8,128)(2,1)} %get-tuple-element.35.refs_0_), channel_id=1, source_target_pairs={{0,32},{16,48},{32,0},{48,16},{1,33},{17,49},{33,1},{49,17},{2,34}... | collective-permute-start | bytes 270344 | tf_op jit(solution)/shard_map/ppermute | solution.py:416
  94.2 9.9 %collective-permute-start.6 = (bf16[352,128]{1,0:T(8,128)(2,1)}, bf16[352,128]{1,0:T(8,128)(2,1)S(1)}, u32[]{:S(2)}, u32[]{:S(2)}) collective-permute-start(bf16[352,128]{1,0:T(8,128)(2,1)} %get-tuple-element.35.refs_0_), channel_id=1, source_target_pairs={{0,48},{16,0},{32,16},{48,32},{1,49},{17,1},{33,17},{49,33},{2,50}... | collective-permute-start | bytes 270344 | tf_op jit(solution)/shard_map/ppermute | solution.py:416
  104.1 0.9 copy-start.4
  118.4 20.9 %all-to-all-start.4 = ((bf16[8,64,1024]{2,1,0:T(8,128)(2,1)}), bf16[8,64,1024]{2,1,0:T(8,128)(2,1)S(1)}, u32[]{:S(2)}, u32[]{:S(2)}) async-start(bf16[8,64,1024]{2,1,0:T(8,128)(2,1)} %correct.3), calls=%async_computation.4 | async-start | bytes 2097152 | tf_op jit(solution)/shard_map/all_to_all | solution.py:278
  124.7 13.7 %collective-permute-start.7 = (bf16[2,16,256]{2,1,0:T(8,128)(2,1)S(1)}, bf16[2,16,256]{2,1,0:T(8,128)(2,1)S(1)}, u32[]{:S(2)}, u32[]{:S(2)}) collective-permute-start(bf16[2,16,256]{2,1,0:T(8,128)(2,1)S(1)} %get-tuple-element.38), channel_id=1, source_target_pairs={{48,32},{49,33},{50,34},{51,35},{52,36},{53,37},{54,38},{55,39},{5... | collective-permute-start | bytes 49160 | tf_op jit(solution)/shard_map/ppermute | solution.py:467
  125.3 13.1 %collective-permute-start.8 = (bf16[2,16,256]{2,1,0:T(8,128)(2,1)S(1)}, bf16[2,16,256]{2,1,0:T(8,128)(2,1)S(1)}, u32[]{:S(2)}, u32[]{:S(2)}) collective-permute-start(bf16[2,16,256]{2,1,0:T(8,128)(2,1)S(1)} %get-tuple-element.39), channel_id=1, source_target_pairs={{48,16},{49,17},{50,18},{51,19},{52,20},{53,21},{54,22},{55,23},{5... | collective-permute-start | bytes 49160 | tf_op jit(solution)/shard_map/ppermute | solution.py:467
  126.0 13.3 %collective-permute-start.9 = (bf16[2,16,256]{2,1,0:T(8,128)(2,1)S(1)}, bf16[2,16,256]{2,1,0:T(8,128)(2,1)S(1)}, u32[]{:S(2)}, u32[]{:S(2)}) collective-permute-start(bf16[2,16,256]{2,1,0:T(8,128)(2,1)S(1)} %get-tuple-element.40), channel_id=1, source_target_pairs={{48,0},{49,1},{50,2},{51,3},{52,4},{53,5},{54,6},{55,7},{56,8},{57... | collective-permute-start | bytes 49160 | tf_op jit(solution)/shard_map/ppermute | solution.py:467
  138.4 6.0 %copy-start.8 = (s32[8,1]{0,1:T(1,128)S(1)}, s32[8,1]{0,1:T(1,128)}, u32[]{:S(2)}) copy-start(s32[8,1]{0,1:T(1,128)} %param.20) | copy-start | bytes 100
  138.4 6.8 %copy-start.9 = (s32[1,64]{1,0:T(1,128)S(1)}, s32[1,64]{1,0:T(1,128)}, u32[]{:S(2)}) copy-start(s32[1,64]{1,0:T(1,128)} %param.22) | copy-start | bytes 772
  139.3 18.8 %all-to-all-start.3 = ((bf16[8,64,1024]{2,1,0:T(8,128)(2,1)}), bf16[8,64,1024]{2,1,0:T(8,128)(2,1)S(1)}, u32[]{:S(2)}, u32[]{:S(2)}) async-start(bf16[8,64,1024]{2,1,0:T(8,128)(2,1)} %correct.2), calls=%async_computation.3 | async-start | bytes 2097152 | tf_op jit(solution)/shard_map/all_to_all | solution.py:278
  144.1 10.6 %copy-start.7 = (s32[4]{0:T(128)S(1)}, s32[4]{0:T(128)}, u32[]{:S(2)}) copy-start(s32[4]{0:T(128)} %get-tuple-element.62.place_ref) | copy-start | bytes 52
  146.5 5.1 %collective-permute-start.10 = (bf16[2,16,256]{2,1,0:T(8,128)(2,1)S(1)}, bf16[2,16,256]{2,1,0:T(8,128)(2,1)S(1)}, u32[]{:S(2)}, u32[]{:S(2)}) collective-permute-start(bf16[2,16,256]{2,1,0:T(8,128)(2,1)S(1)} %select_select_fusion), channel_id=1, source_target_pairs={{0,64},{64,128},{128,192},{192,0},{1,65},{65,129},{129,193},{193,1... | collective-permute-start | bytes 49160 | tf_op jit(solution)/shard_map/ppermute | solution.py:472
  148.2 5.2 %collective-permute-start.11 = (bf16[2,16,256]{2,1,0:T(8,128)(2,1)S(1)}, bf16[2,16,256]{2,1,0:T(8,128)(2,1)S(1)}, u32[]{:S(2)}, u32[]{:S(2)}) collective-permute-start(bf16[2,16,256]{2,1,0:T(8,128)(2,1)S(1)} %select_select_fusion), channel_id=1, source_target_pairs={{0,128},{64,192},{128,0},{192,64},{1,129},{65,193},{129,1},{193,65... | collective-permute-start | bytes 49160 | tf_op jit(solution)/shard_map/ppermute | solution.py:472
  149.1 4.3 %collective-permute-start.12 = (bf16[2,16,256]{2,1,0:T(8,128)(2,1)S(1)}, bf16[2,16,256]{2,1,0:T(8,128)(2,1)S(1)}, u32[]{:S(2)}, u32[]{:S(2)}) collective-permute-start(bf16[2,16,256]{2,1,0:T(8,128)(2,1)S(1)} %select_select_fusion), channel_id=1, source_target_pairs={{0,192},{64,0},{128,64},{192,128},{1,193},{65,1},{129,65},{193,129... | collective-permute-start | bytes 49160 | tf_op jit(solution)/shard_map/ppermute | solution.py:472
  (3 other events, 2.3 us)

commit v4 on v3

--- a/solution.py
+++ b/solution.py
@@ -21,10 +21,11 @@
     return pl.CostEstimate(flops=0, bytes_accessed=int(us * 3.6e6), transcendentals=0)
 
 
-def spread_kernel(place_ref, w_ref, out_ref):
-    width = w_ref.shape[1] // LO
+def spread_kernel(w_ref, out_ref):
+    piece = w_ref.shape[1] // (HI * LO)
+    first = lax.axis_index("cache") * (LO * piece)
     for lo in range(LO):
-        block = w_ref[:, lo * width : (lo + 1) * width]
+        block = w_ref[:, pl.ds(pl.multiple_of(first + lo * piece, piece), piece)]
         for hi in range(HI):
             out_ref[hi * LO + lo] = block
 
@@ -99,10 +100,9 @@
                 ]
         held_scr[...] = jnp.zeros_like(held_scr)
 
-    first = chans if turn == 0 else 0
     wide_x = got_ref[:, :, :chans].reshape(rows, chans).astype(jnp.float32)
-    dt = share_ref[:, :, first : first + rank].reshape(rows, rank)
-    tail = share_ref[:, :, first + rank :].reshape(rows, LANES)
+    dt = share_ref[:, :, chans : chans + rank].reshape(rows, rank)
+    tail = share_ref[:, :, chans + rank :].reshape(rows, LANES)
     position = (hi * pl.num_programs(0) + step_id) * rows + lax.broadcasted_iota(
         jnp.int32, (rows, 1), 0
     )
@@ -146,7 +146,7 @@
 
     held = tuple(held_scr[n * ROWS : (n + 1) * ROWS, :] for n in range(states))
     total, held = lax.fori_loop(
-        0, rows, per_tok, (held_scr[states * ROWS :, :], held), unroll=16
+        0, rows, per_tok, (held_scr[states * ROWS :, :], held), unroll=32
     )
     for n in range(states):
         held_scr[n * ROWS : (n + 1) * ROWS, :] = held[n]
@@ -178,17 +178,12 @@
     return jnp.concatenate(blocks, axis=0).astype(jnp.bfloat16)
 
 
-def join_kernel(place_ref, *refs):
-    own_ref, arrived_refs, refs = refs[0], refs[1:HI], refs[HI:]
-    reqs = len(refs) - 3 - 2 * HI
-    end_refs, refs = refs[:reqs], refs[reqs:]
-    decay_refs, carry_ref, final_refs = refs[:HI], refs[HI], refs[HI + 1 : 2 * HI + 1]
-    decay_scr, state_scr = refs[2 * HI + 1 :]
-    states = decay_refs[0].shape[0]
+def join(place_ref, sent_refs, end_refs, decay_scr, carry_refs, final_refs, state_scr):
+    states = decay_scr.shape[0] // ROWS
+    reqs = len(end_refs)
     hi = place_ref[0]
-    to_rows(decay_scr, decay_refs, states)
     per_req = (states + 2) * ROWS
-    blocks = [ref[...].astype(jnp.float32) for ref in (own_ref, *arrived_refs)]
+    blocks = [ref[...].astype(jnp.float32) for ref in sent_refs]
     for req in range(reqs):
         for by, block in enumerate(blocks):
             slot = lax.rem(hi - by + HI, HI)
@@ -197,14 +192,14 @@
                 state_scr[pl.ds(2 * slot + j, states, stride=ROWS), :] = block[at : at + states]
         for n in range(states):
             rows = slice(n * ROWS, (n + 1) * ROWS)
-            decay = decay_scr[rows, :] * (-LOG2E)
+            decay = decay_scr[rows, :]
             carry = state_scr[rows, :]
             for by in range(HI - 1, 0, -1):
                 block = blocks[by][req * per_req : (req + 1) * per_req]
                 total = block[states * ROWS : (states + 1) * ROWS] + block[(states + 1) * ROWS :]
                 longer = block[rows] + jnp.exp2(total * decay) * carry
                 carry = jnp.where(hi >= by, longer, carry)
-            carry_ref[req, n] = carry
+            carry_refs[req][rows, :] = carry
             total = end_refs[req][states * ROWS :, :]
             state_scr[rows, :] = end_refs[req][rows, :] + jnp.exp2(total * decay) * carry
         for p in range(HI):
@@ -213,8 +208,14 @@
                 final_refs[p][req, :, j * LANES : (j + 1) * LANES] = value.astype(jnp.bfloat16)
 
 
-def correct_kernel(turn, place_ref, lengths_ref, y_ref, total_ref, carry_ref, *refs):
-    decay_refs, (tail_ref, out_ref, y_scr, c_scr, decay_scr) = refs[:HI], refs[HI:]
+def correct_kernel(turn, reqs, place_ref, lengths_ref, y_ref, total_ref, tail_ref, *refs):
+    decay_refs, refs = refs[:HI], refs[HI:]
+    y_scr, c_scr, decay_scr, carry_scr, state_scr = refs[-5:]
+    if turn == 0:
+        sent_refs, end_refs, refs = refs[:HI], refs[HI : HI + reqs], refs[HI + reqs :]
+        out_ref, carry_refs, final_refs = refs[0], refs[1:reqs], refs[reqs : reqs + HI]
+    else:
+        carry_ref, out_ref = refs[:2]
     parts, toks, _ = out_ref.shape
     states = decay_refs[0].shape[0]
     rows = parts * toks
@@ -224,9 +225,14 @@
     def _():
         to_rows(decay_scr, decay_refs, states)
         decay_scr[...] = decay_scr[...] * (-LOG2E)
+        if turn == 0:
+            carries = (carry_scr, *carry_refs)
+            join(place_ref, sent_refs, end_refs, decay_scr, carries, final_refs, state_scr)
+        else:
+            carry_scr[...] = carry_ref[...]
 
     replicate(tail_ref[...].reshape(rows, LANES), states, states, c_scr, 0, rows, rows)
-    carry = tuple(carry_ref[0, n] for n in range(states))
+    carry = tuple(carry_scr[n * ROWS : (n + 1) * ROWS, :] for n in range(states))
 
     def per_tok(tok, carry):
         at = pl.ds(pl.multiple_of(tok * ROWS, ROWS), ROWS)
@@ -239,7 +245,7 @@
         y_scr[at, :] = out
         return carry
 
-    lax.fori_loop(0, rows, per_tok, carry, unroll=16)
+    lax.fori_loop(0, rows, per_tok, carry, unroll=32)
     position = (place_ref[0] * pl.num_programs(0) + step_id) * rows + lax.broadcasted_iota(
         jnp.int32, (rows, 1), 0
     )
@@ -280,16 +286,13 @@
     mine = dt_weight.shape[0]
     quarter = pl.pallas_call(
         spread_kernel,
-        grid_spec=pltpu.PrefetchScalarGridSpec(
-            num_scalar_prefetch=1,
-            grid=(1,),
-            in_specs=[pl.BlockSpec((mine, width // groups), lambda i, at: (0, at[2]))],
-            out_specs=pl.BlockSpec((HI * LO, mine, piece), lambda i, at: (0, 0, 0)),
-        ),
+        grid=(1,),
+        in_specs=[pl.BlockSpec((mine, width), lambda i: (0, 0))],
+        out_specs=pl.BlockSpec((HI * LO, mine, piece), lambda i: (0, 0, 0)),
         out_shape=jax.ShapeDtypeStruct((HI * LO, mine, piece), jnp.bfloat16),
         compiler_params=params(60),
         name="spread",
-    )(place, dt_weight)
+    )(dt_weight)
     quarter = exchange(quarter, ("hi", "lo")).reshape(rank, piece)
 
     stored = cache_states.reshape(slots, -1)
@@ -347,9 +350,9 @@
     first_got = exchange(first_sent, "lo")
     second_sent, first_got, pieces = lax.optimization_barrier((sent[1], first_got, pieces))
     got = [first_got, exchange(second_sent, "lo")]
-    second_share = lax.ppermute(first_got[:, :, chans:], "head", [(0, 1), (1, 0)])
-
-    steps = 4
+    second_share = lax.ppermute(first_got, "head", [(0, 1), (1, 0)])
+
+    steps = 2
     parts = LO // steps
     rows = parts * toks
     rows_f32 = jax.ShapeDtypeStruct((length * ROWS, LANES), jnp.float32)
@@ -380,7 +383,7 @@
                 grid=(steps,),
                 in_specs=[
                     pl.BlockSpec((parts, toks, columns), lambda i, *at: (i, 0, 0))
-                    for columns in ((chans, share_width) if req else (sent_width,))
+                    for columns in ((chans, sent_width) if req else (sent_width,))
                 ]
                 + [whole(rank, piece)] * HI
                 + own(states)
@@ -414,53 +417,54 @@
         end.append(one_end)
 
     arrived = [lax.ppermute(leaving, "hi", shifts(HI, by)) for by in range(1, HI)]
-    carry, *finals = pl.pallas_call(
-        join_kernel,
-        grid_spec=pltpu.PrefetchScalarGridSpec(
-            num_scalar_prefetch=1,
-            grid=(1,),
-            in_specs=[whole(leave_rows, LANES)] * HI + [whole(end_rows, LANES)] * reqs + own(states),
-            out_specs=[whole(reqs, states, ROWS, LANES)] + [whole(reqs, states, piece)] * HI,
-            scratch_shapes=scratch(states * ROWS, states * ROWS),
-        ),
-        out_shape=[jax.ShapeDtypeStruct((reqs, states, ROWS, LANES), jnp.float32)]
-        + [jax.ShapeDtypeStruct((reqs, states, piece), jnp.bfloat16)] * HI,
-        compiler_params=params(8),
-        name="join",
-    )(place, leaving, *arrived, *end, *[decay_rate] * HI)
-
-    back = []
+    carry_rows = states * ROWS
+    back, carry = [], None
     for req in range(reqs):
-        out = pl.pallas_call(
-            functools.partial(correct_kernel, req),
+        out, *more = pl.pallas_call(
+            functools.partial(correct_kernel, req, reqs),
             grid_spec=pltpu.PrefetchScalarGridSpec(
                 num_scalar_prefetch=2,
                 grid=(steps,),
                 in_specs=[
                     rows_spec,
                     rows_spec,
-                    pl.BlockSpec((1, states, ROWS, LANES), lambda i, *at, req=req: (req, 0, 0, 0)),
+                    pl.BlockSpec(
+                        (parts, toks, LANES), lambda i, *at: (i, 0, (chans + rank) // LANES)
+                    ),
                 ]
                 + own(states)
-                + [
-                    pl.BlockSpec(
-                        (parts, toks, LANES),
-                        lambda i, *at, at_lane=rank + (0 if req else chans): (
-                            i, 0, at_lane // LANES
-                        ),
-                    )
-                ],
-                out_specs=pl.BlockSpec((parts, toks, chans), lambda i, *at: (i, 0, 0)),
-                scratch_shapes=scratch(rows * ROWS, states * rows, states * ROWS),
+                + (
+                    [whole(carry_rows, LANES)]
+                    if req
+                    else [whole(leave_rows, LANES)] * HI + [whole(end_rows, LANES)] * reqs
+                ),
+                out_specs=[pl.BlockSpec((parts, toks, chans), lambda i, *at: (i, 0, 0))]
+                + (
+                    []
+                    if req
+                    else [whole(carry_rows, LANES)] * (reqs - 1)
+                    + [whole(reqs, states, piece)] * HI
+                ),
+                scratch_shapes=scratch(
+                    rows * ROWS, states * rows, carry_rows, carry_rows, carry_rows
+                ),
             ),
-            out_shape=jax.ShapeDtypeStruct((LO, toks, chans), jnp.bfloat16),
+            out_shape=[jax.ShapeDtypeStruct((LO, toks, chans), jnp.bfloat16)]
+            + (
+                []
+                if req
+                else [jax.ShapeDtypeStruct((carry_rows, LANES), jnp.float32)] * (reqs - 1)
+                + [jax.ShapeDtypeStruct((reqs, states, piece), jnp.bfloat16)] * HI
+            ),
             compiler_params=params(60),
             cost_estimate=cost(9),
             name="correct",
         )(
-            place, new_lengths, y[req], total[req], carry, *[decay_rate] * HI,
-            second_share if req else first_got,
+            place, new_lengths, y[req], total[req], second_share if req else first_got,
+            *[decay_rate] * HI, *([carry[req - 1]] if req else [leaving, *arrived, *end]),
         )
+        if req == 0:
+            carry, finals = more[: reqs - 1], more[reqs - 1 :]
         if req == reqs - 1:
             held = finals[HI - 1]
             for to in range(HI - 1):

time: 162 us -> 157 us (0.969)
  local copies, waits for them, and re-layouts: 10.2 us -> 8.03 us
    unnamed x38, local copies, waits for them, and re-layouts: 6.39 us -> 4.51 us
    pallas_call x4 -> x3, Pallas kernels: 25.1 us -> 24.6 us  [the longest x2 22.9 us: on_device(): pl.pallas_call(functools.partial(correct_kernel, req, reqs), grid_spec=pl...]
where the time goes in v4:
time: 157 us; the launch traced here: 155 us
  Pallas kernels  65.8 us (42%)
  starting transfers between devices  49.1 us (31%)
  waiting for transfers between devices  28.4 us (18%)
  local copies, waits for them, and re-layouts  8.03 us (5%)
  other arithmetic  1.85 us (1%)
    pallas_call x2, Pallas kernels, on_device(): pl.pallas_call(functools.partial(scan_kernel, req), grid_spec=pltpu.Prefe...  31.7 us
    all_to_all x5, starting transfers between devices, exchange(): return lax.all_to_all(array, axis, split_axis=0, concat_axis=0, tiled=True)  29.8 us
    pallas_call x2, Pallas kernels, on_device(): pl.pallas_call(functools.partial(correct_kernel, req, reqs), grid_spec=pl...  22.9 us
    all_to_all x5, waiting for transfers between devices, exchange(): return lax.all_to_all(array, axis, split_axis=0, concat_axis=0, tiled=True)  12 us
    ppermute x3, waiting for transfers between devices, on_device(): lax.ppermute(leaving, 'hi', shifts(HI, by))  7.7 us
    ppermute x3, starting transfers between devices, on_device(): lax.ppermute(leaving, 'hi', shifts(HI, by))  6.55 us
    pallas_call x2, Pallas kernels, on_device(): pl.pallas_call(pack_kernel, grid_spec=pltpu.PrefetchScalarGridSpec(num_sc...  6.24 us
    ppermute x3, waiting for transfers between devices, on_device(): lax.ppermute(jnp.concatenate([quarter, wanted_by(lax.rem(group + by, grou...  6.18 us
  transfers between devices with their start and end apart: 18, of which 11 were waited for; matrix products, arithmetic and copies ran while one was open for 5% of the time, Pallas kernels for 22%

profile of v4, /device:TPU:8, one launch (start us, length us, event | category | flops | bytes accessed | tf_op | source)
XLA Modules:
  0.0 154.8 jit_solution(4282366236787434587)
XLA Ops:
  0.7 1.7 %spread.1 = bf16[32,16,256]{2,1,0:T(8,128)(2,1)} custom-call(bf16[16,8192]{1,0:T(8,128)(2,1)} %w_ref.1), custom_call_target="tpu_custom_call" | custom-call | tf_op jit(solution)/shard_map/spread/pallas_call | solution.py:287
  2.4 11.3 %all-to-all-start.1 = ((bf16[32,16,256]{2,1,0:T(8,128)(2,1)}), bf16[32,16,256]{2,1,0:T(8,128)(2,1)S(1)}, u32[]{:S(2)}, u32[]{:S(2)}) async-start(bf16[32,16,256]{2,1,0:T(8,128)(2,1)} %spread.1), calls=%async_computation.1 | async-start | bytes 524288 | tf_op jit(solution)/shard_map/all_to_all | solution.py:284
  14.5 1.2 copy.21
  17.5 3.3 %pack.3 = bf16[8,64,1664]{2,1,0:T(8,128)(2,1)} custom-call(s32[4]{0:T(128)} %pad_add_fusion.place_ref, bf16[2,64,8192]{2,1,0:T(8,128)(2,1)} %x_ref.3, bf16[64,640]{1,0:T(8,128)(2,1)} %maximum_maximum_fusion.refs_0_), custom_call_target="tpu_custom_call" | custom-call | tf_op jit(solution)/shard_map/pack/pallas_call | solution.py:321
  20.8 5.6 %all-to-all-done.1 = bf16[32,16,256]{2,1,0:T(8,128)(2,1)S(1)} async-done(((bf16[32,16,256]{2,1,0:T(8,128)(2,1)}), bf16[32,16,256]{2,1,0:T(8,128)(2,1)S(1)}, u32[]{:S(2)}, u32[]{:S(2)}) %all-to-all-start.1) | async-done | bytes 262176 | tf_op jit(solution)/shard_map/all_to_all | solution.py:284
  26.4 3.6 %all-to-all-start = ((bf16[8,64,1664]{2,1,0:T(8,128)(2,1)}), bf16[8,64,1664]{2,1,0:T(8,128)(2,1)S(1)}, u32[]{:S(2)}, u32[]{:S(2)}) async-start(bf16[8,64,1664]{2,1,0:T(8,128)(2,1)} %pack.3), calls=%async_computation | async-start | bytes 3407872 | tf_op jit(solution)/shard_map/all_to_all | solution.py:284
  30.7 1.7 %collective-permute-start = (bf16[544,256]{1,0:T(8,128)(2,1)S(1)}, bf16[544,256]{1,0:T(8,128)(2,1)S(1)}, u32[]{:S(2)}, u32[]{:S(2)}) collective-permute-start(bf16[544,256]{1,0:T(8,128)(2,1)S(1)} %get-tuple-element.56), channel_id=1, source_target_pairs={{0,64},{64,128},{128,192},{192,0},{1,65},{65,129},{129,193},{193,1... | collective-permute-start | bytes 835592 | tf_op jit(solution)/shard_map/ppermute | solution.py:342
  33.3 2.4 %collective-permute-start.2 = (bf16[544,256]{1,0:T(8,128)(2,1)S(1)}, bf16[544,256]{1,0:T(8,128)(2,1)}, u32[]{:S(2)}, u32[]{:S(2)}) collective-permute-start(bf16[544,256]{1,0:T(8,128)(2,1)S(1)} %get-tuple-element.54), channel_id=1, source_target_pairs={{0,192},{64,0},{128,64},{192,128},{1,193},{65,1},{129,65},{193,129... | collective-permute-start | bytes 835592 | tf_op jit(solution)/shard_map/ppermute | solution.py:342
  35.7 3.0 %pack.2 = bf16[8,64,1024]{2,1,0:T(8,128)(2,1)} custom-call(s32[4]{0:T(128)} %pad_add_fusion.place_ref, bf16[2,64,8192]{2,1,0:T(8,128)(2,1)} %x_ref.3), custom_call_target="tpu_custom_call" | custom-call | tf_op jit(solution)/shard_map/pack/pallas_call | solution.py:321
  38.7 1.7 %collective-permute-done.refs_1_.refs_2_.refs_19_ = bf16[544,256]{1,0:T(8,128)(2,1)S(1)} collective-permute-done((bf16[544,256]{1,0:T(8,128)(2,1)S(1)}, bf16[544,256]{1,0:T(8,128)(2,1)S(1)}, u32[]{:S(2)}, u32[]{:S(2)}) %collective-permute-start) | collective-permute-done | bytes 278560 | tf_op jit(solution)/shard_map/ppermute | solution.py:342
  40.4 2.9 %collective-permute-done.1.refs_2_.refs_3_.refs_20_ = bf16[544,256]{1,0:T(8,128)(2,1)S(1)} collective-permute-done((bf16[544,256]{1,0:T(8,128)(2,1)S(1)}, bf16[544,256]{1,0:T(8,128)(2,1)S(1)}, u32[]{:S(2)}, u32[]{:S(2)}) %collective-permute-start.1) | collective-permute-done | bytes 278560 | tf_op jit(solution)/shard_map/ppermute | solution.py:342
  44.0 1.6 %collective-permute-done.2.refs_3_.refs_4_.refs_21_ = bf16[544,256]{1,0:T(8,128)(2,1)} collective-permute-done((bf16[544,256]{1,0:T(8,128)(2,1)S(1)}, bf16[544,256]{1,0:T(8,128)(2,1)}, u32[]{:S(2)}, u32[]{:S(2)}) %collective-permute-start.2) | collective-permute-done | bytes 278560 | tf_op jit(solution)/shard_map/ppermute | solution.py:342
  45.6 4.6 %all-to-all-done.got_ref.tail_ref = bf16[8,64,1664]{2,1,0:T(8,128)(2,1)S(1)} async-done(((bf16[8,64,1664]{2,1,0:T(8,128)(2,1)}), bf16[8,64,1664]{2,1,0:T(8,128)(2,1)S(1)}, u32[]{:S(2)}, u32[]{:S(2)}) %all-to-all-start) | async-done | bytes 1703968 | tf_op jit(solution)/shard_map/all_to_all | solution.py:284
  50.2 3.6 %all-to-all-start.2 = ((bf16[8,64,1024]{2,1,0:T(8,128)(2,1)}), bf16[8,64,1024]{2,1,0:T(8,128)(2,1)S(1)}, u32[]{:S(2)}, u32[]{:S(2)}) async-start(bf16[8,64,1024]{2,1,0:T(8,128)(2,1)} %pack.2), calls=%async_computation.2 | async-start | bytes 2097152 | tf_op jit(solution)/shard_map/all_to_all | solution.py:284
  53.9 15.7 %scan.2 = (f32[4096,128]{1,0:T(8,128)}, f32[4096,128]{1,0:T(8,128)}, f32[136,128]{1,0:T(8,128)}) custom-call(s32[4]{0:T(128)} %pad_add_fusion.place_ref, s32[8]{0:T(128)} %lengths_ref.7, bf16[8,64,1664]{2,1,0:T(8,128)(2,1)} %copy-done.4, bf16[512,256]{1,0:T(8,128)(2,1)} %bitcast.53, bf16[544,256]{1,0:T(8,128)(2,1)} %copy-done.7, bf16[544,256]{1,0:T(8,128)(2,1)} %copy-done.8, ...), custom_call_target="tpu_custom_call" | custom-call | bytes 54000000 | tf_op jit(solution)/shard_map/scan/pallas_call | solution.py:379
  70.7 16.0 %scan.3 = (bf16[352,128]{1,0:T(8,128)(2,1)}, f32[4096,128]{1,0:T(8,128)}, f32[4096,128]{1,0:T(8,128)}, f32[136,128]{1,0:T(8,128)}) custom-call(s32[4]{0:T(128)} %pad_add_fusion.place_ref, s32[8]{0:T(128)} %lengths_ref.7, bf16[8,64,1024]{2,1,0:T(8,128)(2,1)} %copy-done.5, bf16[8,64,1664]{2,1,0:T(8,128)(2,1)} %collective-permute-done.3.refs_0_.tail_ref, ...), custom_call_target="tpu_custom_call" | custom-call | bytes 54000000 | tf_op jit(solution)/shard_map/scan/pallas_call | solution.py:379
  86.6 1.9 %collective-permute-start.4 = (bf16[352,128]{1,0:T(8,128)(2,1)}, bf16[352,128]{1,0:T(8,128)(2,1)S(1)}, u32[]{:S(2)}, u32[]{:S(2)}) collective-permute-start(bf16[352,128]{1,0:T(8,128)(2,1)} %get-tuple-element.38.refs_4_), channel_id=1, source_target_pairs={{0,16},{16,32},{32,48},{48,0},{1,17},{17,33},{33,49},{49,1},{2,18}... | collective-permute-start | bytes 270344 | tf_op jit(solution)/shard_map/ppermute | solution.py:419
  88.5 2.5 %collective-permute-start.5 = (bf16[352,128]{1,0:T(8,128)(2,1)}, bf16[352,128]{1,0:T(8,128)(2,1)S(1)}, u32[]{:S(2)}, u32[]{:S(2)}) collective-permute-start(bf16[352,128]{1,0:T(8,128)(2,1)} %get-tuple-element.38.refs_4_), channel_id=1, source_target_pairs={{0,32},{16,48},{32,0},{48,16},{1,33},{17,49},{33,1},{49,17},{2,34}... | collective-permute-start | bytes 270344 | tf_op jit(solution)/shard_map/ppermute | solution.py:419
  91.0 2.2 %collective-permute-start.6 = (bf16[352,128]{1,0:T(8,128)(2,1)}, bf16[352,128]{1,0:T(8,128)(2,1)S(1)}, u32[]{:S(2)}, u32[]{:S(2)}) collective-permute-start(bf16[352,128]{1,0:T(8,128)(2,1)} %get-tuple-element.38.refs_4_), channel_id=1, source_target_pairs={{0,48},{16,0},{32,16},{48,32},{1,49},{17,1},{33,17},{49,33},{2,50}... | collective-permute-start | bytes 270344 | tf_op jit(solution)/shard_map/ppermute | solution.py:419
  94.1 4.9 %collective-permute-done.5.refs_6_ = bf16[352,128]{1,0:T(8,128)(2,1)S(1)} collective-permute-done((bf16[352,128]{1,0:T(8,128)(2,1)}, bf16[352,128]{1,0:T(8,128)(2,1)S(1)}, u32[]{:S(2)}, u32[]{:S(2)}) %collective-permute-start.5) | collective-permute-done | bytes 90144 | tf_op jit(solution)/shard_map/ppermute | solution.py:419
  99.0 1.9 %collective-permute-done.6.refs_7_ = bf16[352,128]{1,0:T(8,128)(2,1)S(1)} collective-permute-done((bf16[352,128]{1,0:T(8,128)(2,1)}, bf16[352,128]{1,0:T(8,128)(2,1)S(1)}, u32[]{:S(2)}, u32[]{:S(2)}) %collective-permute-start.6) | collective-permute-done | bytes 90144 | tf_op jit(solution)/shard_map/ppermute | solution.py:419
  101.5 11.7 %correct.2 = (bf16[8,64,1024]{2,1,0:T(8,128)(2,1)}, f32[128,128]{1,0:T(8,128)}, bf16[2,16,256]{2,1,0:T(8,128)(2,1)}, bf16[2,16,256]{2,1,0:T(8,128)(2,1)}, bf16[2...) custom-call(s32[4]{0:T(128)} %pad_add_fusion.place_ref, s32[8]{0:T(128)} %lengths_ref.7, ...), custom_call_target="tpu_custom_call" | custom-call | bytes 32400000 | tf_op jit(solution)/shard_map/correct/pallas_call | solution.py:423
  113.3 6.4 %all-to-all-start.4 = ((bf16[8,64,1024]{2,1,0:T(8,128)(2,1)}), bf16[8,64,1024]{2,1,0:T(8,128)(2,1)S(1)}, u32[]{:S(2)}, u32[]{:S(2)}) async-start(bf16[8,64,1024]{2,1,0:T(8,128)(2,1)} %get-tuple-element.46), calls=%async_computation.4 | async-start | bytes 2097152 | tf_op jit(solution)/shard_map/all_to_all | solution.py:284
  121.1 1.3 collective-permute-start.9
  122.4 11.1 %correct.3 = bf16[8,64,1024]{2,1,0:T(8,128)(2,1)} custom-call(s32[4]{0:T(128)} %pad_add_fusion.place_ref, s32[8]{0:T(128)} %lengths_ref.7, f32[4096,128]{1,0:T(8,128)} %get-tuple-element.34.y_ref, f32[4096,128]{1,0:T(8,128)} %get-tuple-element.35.total_ref, bf16[8,64,1664]{2,1,0:T(8,128)(2,1)} %collective-permute-done.3.refs_0_.tail_ref, ...), custom_call_target="tpu_custom_call" | custom-call | bytes 32400000 | tf_op jit(solution)/shard_map/correct/pallas_call | solution.py:423
  134.3 4.9 %all-to-all-start.3 = ((bf16[8,64,1024]{2,1,0:T(8,128)(2,1)}), bf16[8,64,1024]{2,1,0:T(8,128)(2,1)S(1)}, u32[]{:S(2)}, u32[]{:S(2)}) async-start(bf16[8,64,1024]{2,1,0:T(8,128)(2,1)} %correct.3), calls=%async_computation.3 | async-start | bytes 2097152 | tf_op jit(solution)/shard_map/all_to_all | solution.py:284
  141.6 1.7 %collective-permute-start.10 = (bf16[2,16,256]{2,1,0:T(8,128)(2,1)S(1)}, bf16[2,16,256]{2,1,0:T(8,128)(2,1)S(1)}, u32[]{:S(2)}, u32[]{:S(2)}) collective-permute-start(bf16[2,16,256]{2,1,0:T(8,128)(2,1)S(1)} %select_select_fusion), channel_id=1, source_target_pairs={{0,64},{64,128},{128,192},{192,0},{1,65},{65,129},{129,193},{193,1... | collective-permute-start | bytes 49160 | tf_op jit(solution)/shard_map/ppermute | solution.py:476
  144.2 2.4 %collective-permute-start.12 = (bf16[2,16,256]{2,1,0:T(8,128)(2,1)S(1)}, bf16[2,16,256]{2,1,0:T(8,128)(2,1)S(1)}, u32[]{:S(2)}, u32[]{:S(2)}) collective-permute-start(bf16[2,16,256]{2,1,0:T(8,128)(2,1)S(1)} %select_select_fusion), channel_id=1, source_target_pairs={{0,192},{64,0},{128,64},{192,128},{1,193},{65,1},{129,65},{193,129... | collective-permute-start | bytes 49160 | tf_op jit(solution)/shard_map/ppermute | solution.py:476
  146.7 1.8 %collective-permute-done.11 = bf16[2,16,256]{2,1,0:T(8,128)(2,1)S(1)} collective-permute-done((bf16[2,16,256]{2,1,0:T(8,128)(2,1)S(1)}, bf16[2,16,256]{2,1,0:T(8,128)(2,1)S(1)}, u32[]{:S(2)}, u32[]{:S(2)}) %collective-permute-start.11) | collective-permute-done | bytes 16416 | tf_op jit(solution)/shard_map/ppermute | solution.py:476
  149.9 1.6 %unpack.2.refs_0_ = bf16[2,64,8192]{2,1,0:T(8,128)(2,1)} custom-call(s32[4]{0:T(128)S(1)} %copy-done.1, bf16[8,64,1024]{2,1,0:T(8,128)(2,1)S(1)} %all-to-all-done.4.back_ref), custom_call_target="tpu_custom_call" | custom-call | tf_op jit(solution)/shard_map/unpack/pallas_call | solution.py:492
  151.5 1.7 %all-to-all-done.3.back_ref = bf16[8,64,1024]{2,1,0:T(8,128)(2,1)S(1)} async-done(((bf16[8,64,1024]{2,1,0:T(8,128)(2,1)}), bf16[8,64,1024]{2,1,0:T(8,128)(2,1)S(1)}, u32[]{:S(2)}, u32[]{:S(2)}) %all-to-all-start.3) | async-done | bytes 1048608 | tf_op jit(solution)/shard_map/all_to_all | solution.py:284
  153.2 1.6 %unpack.3 = bf16[2,64,8192]{2,1,0:T(8,128)(2,1)} custom-call(s32[4]{0:T(128)S(1)} %copy-done.1, bf16[8,64,1024]{2,1,0:T(8,128)(2,1)S(1)} %all-to-all-done.3.back_ref, bf16[2,64,8192]{2,1,0:T(8,128)(2,1)} %unpack.2.refs_0_), custom_call_target="tpu_custom_call", output_to_operand_aliasing={{}: (2, {})} | custom-call | tf_op jit(solution)/shard_map/unpack/pallas_call | solution.py:492
  (79 shorter events, 14.3 us)
Async XLA Ops:
  0.6 13.8 %copy-start = (bf16[2,64,512]{2,1,0:T(8,128)(2,1)S(1)}, bf16[2,64,512]{2,1,0:T(8,128)(2,1)}, u32[]{:S(2)}) copy-start(bf16[2,64,512]{2,1,0:T(8,128)(2,1)} %param.13) | copy-start | bytes 393220
  0.6 15.1 %copy-start.2 = (s32[8,1]{0,1:T(1,128)S(1)}, s32[8,1]{0,1:T(1,128)}, u32[]{:S(2)}) copy-start(s32[8,1]{0,1:T(1,128)} %param.20) | copy-start | bytes 100
  0.7 15.1 %copy-start.13 = (s32[8]{0:T(128)S(1)}, s32[8]{0:T(128)}, u32[]{:S(2)}) copy-start(s32[8]{0:T(128)} %param.21) | copy-start | bytes 100
  2.4 24.0 %all-to-all-start.1 = ((bf16[32,16,256]{2,1,0:T(8,128)(2,1)}), bf16[32,16,256]{2,1,0:T(8,128)(2,1)S(1)}, u32[]{:S(2)}, u32[]{:S(2)}) async-start(bf16[32,16,256]{2,1,0:T(8,128)(2,1)} %spread.1), calls=%async_computation.1 | async-start | bytes 524288 | tf_op jit(solution)/shard_map/all_to_all | solution.py:284
  26.4 4.3 %copy-start.6 = (bf16[32,16,256]{2,1,0:T(8,128)(2,1)}, bf16[32,16,256]{2,1,0:T(8,128)(2,1)S(1)}, u32[]{:S(2)}) copy-start(bf16[32,16,256]{2,1,0:T(8,128)(2,1)S(1)} %all-to-all-done.1) | copy-start | bytes 786436
  26.4 23.8 %all-to-all-start = ((bf16[8,64,1664]{2,1,0:T(8,128)(2,1)}), bf16[8,64,1664]{2,1,0:T(8,128)(2,1)S(1)}, u32[]{:S(2)}, u32[]{:S(2)}) async-start(bf16[8,64,1664]{2,1,0:T(8,128)(2,1)} %pack.3), calls=%async_computation | async-start | bytes 3407872 | tf_op jit(solution)/shard_map/all_to_all | solution.py:284
  30.7 9.7 %collective-permute-start = (bf16[544,256]{1,0:T(8,128)(2,1)S(1)}, bf16[544,256]{1,0:T(8,128)(2,1)S(1)}, u32[]{:S(2)}, u32[]{:S(2)}) collective-permute-start(bf16[544,256]{1,0:T(8,128)(2,1)S(1)} %get-tuple-element.56), channel_id=1, source_target_pairs={{0,64},{64,128},{128,192},{192,0},{1,65},{65,129},{129,193},{193,1... | collective-permute-start | bytes 835592 | tf_op jit(solution)/shard_map/ppermute | solution.py:342
  32.4 10.9 %collective-permute-start.1 = (bf16[544,256]{1,0:T(8,128)(2,1)S(1)}, bf16[544,256]{1,0:T(8,128)(2,1)S(1)}, u32[]{:S(2)}, u32[]{:S(2)}) collective-permute-start(bf16[544,256]{1,0:T(8,128)(2,1)S(1)} %get-tuple-element.55), channel_id=1, source_target_pairs={{0,128},{64,192},{128,0},{192,64},{1,129},{65,193},{129,1},{193,65... | collective-permute-start | bytes 835592 | tf_op jit(solution)/shard_map/ppermute | solution.py:342
  33.3 12.3 %collective-permute-start.2 = (bf16[544,256]{1,0:T(8,128)(2,1)S(1)}, bf16[544,256]{1,0:T(8,128)(2,1)}, u32[]{:S(2)}, u32[]{:S(2)}) collective-permute-start(bf16[544,256]{1,0:T(8,128)(2,1)S(1)} %get-tuple-element.54), channel_id=1, source_target_pairs={{0,192},{64,0},{128,64},{192,128},{1,193},{65,1},{129,65},{193,129... | collective-permute-start | bytes 835592 | tf_op jit(solution)/shard_map/ppermute | solution.py:342
  40.4 2.9 %copy-start.7 = (bf16[544,256]{1,0:T(8,128)(2,1)}, bf16[544,256]{1,0:T(8,128)(2,1)S(1)}, u32[]{:S(2)}) copy-start(bf16[544,256]{1,0:T(8,128)(2,1)S(1)} %collective-permute-done.refs_1_.refs_2_.refs_19_) | copy-start | bytes 835588
  50.2 3.7 %copy-start.4 = (bf16[8,64,1664]{2,1,0:T(8,128)(2,1)}, bf16[8,64,1664]{2,1,0:T(8,128)(2,1)S(1)}, u32[]{:S(2)}) copy-start(bf16[8,64,1664]{2,1,0:T(8,128)(2,1)S(1)} %all-to-all-done.got_ref.tail_ref) | copy-start | bytes 5111812
  50.2 19.4 %all-to-all-start.2 = ((bf16[8,64,1024]{2,1,0:T(8,128)(2,1)}), bf16[8,64,1024]{2,1,0:T(8,128)(2,1)S(1)}, u32[]{:S(2)}, u32[]{:S(2)}) async-start(bf16[8,64,1024]{2,1,0:T(8,128)(2,1)} %pack.2), calls=%async_computation.2 | async-start | bytes 2097152 | tf_op jit(solution)/shard_map/all_to_all | solution.py:284
  53.9 15.8 %collective-permute-start.3 = (bf16[8,64,1664]{2,1,0:T(8,128)(2,1)S(1)}, bf16[8,64,1664]{2,1,0:T(8,128)(2,1)}, u32[]{:S(2)}, u32[]{:S(2)}) collective-permute-start(bf16[8,64,1664]{2,1,0:T(8,128)(2,1)S(1)} %all-to-all-done.got_ref.tail_ref), channel_id=1, source_target_pairs={{0,1},{1,0},{2,3},{3,2},{4,5},{5,4},{6,7},{7,6},{8,9},{9,8},{10,11... | collective-permute-start | bytes 5111816 | tf_op jit(solution)/shard_map/ppermute | solution.py:353
  86.6 7.5 %collective-permute-start.4 = (bf16[352,128]{1,0:T(8,128)(2,1)}, bf16[352,128]{1,0:T(8,128)(2,1)S(1)}, u32[]{:S(2)}, u32[]{:S(2)}) collective-permute-start(bf16[352,128]{1,0:T(8,128)(2,1)} %get-tuple-element.38.refs_4_), channel_id=1, source_target_pairs={{0,16},{16,32},{32,48},{48,0},{1,17},{17,33},{33,49},{49,1},{2,18}... | collective-permute-start | bytes 270344 | tf_op jit(solution)/shard_map/ppermute | solution.py:419
  88.5 10.5 %collective-permute-start.5 = (bf16[352,128]{1,0:T(8,128)(2,1)}, bf16[352,128]{1,0:T(8,128)(2,1)S(1)}, u32[]{:S(2)}, u32[]{:S(2)}) collective-permute-start(bf16[352,128]{1,0:T(8,128)(2,1)} %get-tuple-element.38.refs_4_), channel_id=1, source_target_pairs={{0,32},{16,48},{32,0},{48,16},{1,33},{17,49},{33,1},{49,17},{2,34}... | collective-permute-start | bytes 270344 | tf_op jit(solution)/shard_map/ppermute | solution.py:419
  91.0 9.9 %collective-permute-start.6 = (bf16[352,128]{1,0:T(8,128)(2,1)}, bf16[352,128]{1,0:T(8,128)(2,1)S(1)}, u32[]{:S(2)}, u32[]{:S(2)}) collective-permute-start(bf16[352,128]{1,0:T(8,128)(2,1)} %get-tuple-element.38.refs_4_), channel_id=1, source_target_pairs={{0,48},{16,0},{32,16},{48,32},{1,49},{17,1},{33,17},{49,33},{2,50}... | collective-permute-start | bytes 270344 | tf_op jit(solution)/shard_map/ppermute | solution.py:419
  94.1 6.8 %copy-start.9 = (bf16[352,128]{1,0:T(8,128)(2,1)}, bf16[352,128]{1,0:T(8,128)(2,1)S(1)}, u32[]{:S(2)}) copy-start(bf16[352,128]{1,0:T(8,128)(2,1)S(1)} %collective-permute-done.4.refs_5_) | copy-start | bytes 270340
  99.0 1.9 %copy-start.10 = (bf16[352,128]{1,0:T(8,128)(2,1)}, bf16[352,128]{1,0:T(8,128)(2,1)S(1)}, u32[]{:S(2)}) copy-start(bf16[352,128]{1,0:T(8,128)(2,1)S(1)} %collective-permute-done.5.refs_6_) | copy-start | bytes 270340
  113.3 6.4 %copy-start.16 = (bf16[2,16,256]{2,1,0:T(8,128)(2,1)S(1)}, bf16[2,16,256]{2,1,0:T(8,128)(2,1)}, u32[]{:S(2)}) copy-start(bf16[2,16,256]{2,1,0:T(8,128)(2,1)} %get-tuple-element.41) | copy-start | bytes 49156
  113.3 7.1 %copy-start.15 = (bf16[2,16,256]{2,1,0:T(8,128)(2,1)S(1)}, bf16[2,16,256]{2,1,0:T(8,128)(2,1)}, u32[]{:S(2)}) copy-start(bf16[2,16,256]{2,1,0:T(8,128)(2,1)} %get-tuple-element.42) | copy-start | bytes 49156
  113.3 7.8 %copy-start.14 = (bf16[2,16,256]{2,1,0:T(8,128)(2,1)S(1)}, bf16[2,16,256]{2,1,0:T(8,128)(2,1)}, u32[]{:S(2)}) copy-start(bf16[2,16,256]{2,1,0:T(8,128)(2,1)} %get-tuple-element.43) | copy-start | bytes 49156
  113.3 21.0 %all-to-all-start.4 = ((bf16[8,64,1024]{2,1,0:T(8,128)(2,1)}), bf16[8,64,1024]{2,1,0:T(8,128)(2,1)S(1)}, u32[]{:S(2)}, u32[]{:S(2)}) async-start(bf16[8,64,1024]{2,1,0:T(8,128)(2,1)} %get-tuple-element.46), calls=%async_computation.4 | async-start | bytes 2097152 | tf_op jit(solution)/shard_map/all_to_all | solution.py:284
  119.7 13.8 %collective-permute-start.7 = (bf16[2,16,256]{2,1,0:T(8,128)(2,1)S(1)}, bf16[2,16,256]{2,1,0:T(8,128)(2,1)S(1)}, u32[]{:S(2)}, u32[]{:S(2)}) collective-permute-start(bf16[2,16,256]{2,1,0:T(8,128)(2,1)S(1)} %copy-done.16), channel_id=1, source_target_pairs={{48,32},{49,33},{50,34},{51,35},{52,36},{53,37},{54,38},{55,39},{5... | collective-permute-start | bytes 49160 | tf_op jit(solution)/shard_map/ppermute | solution.py:471
  120.4 13.1 %collective-permute-start.8 = (bf16[2,16,256]{2,1,0:T(8,128)(2,1)S(1)}, bf16[2,16,256]{2,1,0:T(8,128)(2,1)S(1)}, u32[]{:S(2)}, u32[]{:S(2)}) collective-permute-start(bf16[2,16,256]{2,1,0:T(8,128)(2,1)S(1)} %copy-done.15), channel_id=1, source_target_pairs={{48,16},{49,17},{50,18},{51,19},{52,20},{53,21},{54,22},{55,23},{5... | collective-permute-start | bytes 49160 | tf_op jit(solution)/shard_map/ppermute | solution.py:471
  121.1 13.2 %collective-permute-start.9 = (bf16[2,16,256]{2,1,0:T(8,128)(2,1)S(1)}, bf16[2,16,256]{2,1,0:T(8,128)(2,1)S(1)}, u32[]{:S(2)}, u32[]{:S(2)}) collective-permute-start(bf16[2,16,256]{2,1,0:T(8,128)(2,1)S(1)} %copy-done.14), channel_id=1, source_target_pairs={{48,0},{49,1},{50,2},{51,3},{52,4},{53,5},{54,6},{55,7},{56,8},{57... | collective-permute-start | bytes 49160 | tf_op jit(solution)/shard_map/ppermute | solution.py:471
  122.4 11.9 %copy-start.12 = (bf16[2,16,256]{2,1,0:T(8,128)(2,1)S(1)}, bf16[2,16,256]{2,1,0:T(8,128)(2,1)}, u32[]{:S(2)}) copy-start(bf16[2,16,256]{2,1,0:T(8,128)(2,1)} %get-tuple-element.44) | copy-start | bytes 49156
  133.5 6.8 %copy-start.3 = (s32[1,64]{1,0:T(1,128)S(1)}, s32[1,64]{1,0:T(1,128)}, u32[]{:S(2)}) copy-start(s32[1,64]{1,0:T(1,128)} %param.22) | copy-start | bytes 772
  134.3 18.9 %all-to-all-start.3 = ((bf16[8,64,1024]{2,1,0:T(8,128)(2,1)}), bf16[8,64,1024]{2,1,0:T(8,128)(2,1)S(1)}, u32[]{:S(2)}, u32[]{:S(2)}) async-start(bf16[8,64,1024]{2,1,0:T(8,128)(2,1)} %correct.3), calls=%async_computation.3 | async-start | bytes 2097152 | tf_op jit(solution)/shard_map/all_to_all | solution.py:284
  139.2 10.6 %copy-start.1 = (s32[4]{0:T(128)S(1)}, s32[4]{0:T(128)}, u32[]{:S(2)}) copy-start(s32[4]{0:T(128)} %pad_add_fusion.place_ref) | copy-start | bytes 52
  141.6 5.1 %collective-permute-start.10 = (bf16[2,16,256]{2,1,0:T(8,128)(2,1)S(1)}, bf16[2,16,256]{2,1,0:T(8,128)(2,1)S(1)}, u32[]{:S(2)}, u32[]{:S(2)}) collective-permute-start(bf16[2,16,256]{2,1,0:T(8,128)(2,1)S(1)} %select_select_fusion), channel_id=1, source_target_pairs={{0,64},{64,128},{128,192},{192,0},{1,65},{65,129},{129,193},{193,1... | collective-permute-start | bytes 49160 | tf_op jit(solution)/shard_map/ppermute | solution.py:476
  143.3 5.2 %collective-permute-start.11 = (bf16[2,16,256]{2,1,0:T(8,128)(2,1)S(1)}, bf16[2,16,256]{2,1,0:T(8,128)(2,1)S(1)}, u32[]{:S(2)}, u32[]{:S(2)}) collective-permute-start(bf16[2,16,256]{2,1,0:T(8,128)(2,1)S(1)} %select_select_fusion), channel_id=1, source_target_pairs={{0,128},{64,192},{128,0},{192,64},{1,129},{65,193},{129,1},{193,65... | collective-permute-start | bytes 49160 | tf_op jit(solution)/shard_map/ppermute | solution.py:476
  144.2 4.3 %collective-permute-start.12 = (bf16[2,16,256]{2,1,0:T(8,128)(2,1)S(1)}, bf16[2,16,256]{2,1,0:T(8,128)(2,1)S(1)}, u32[]{:S(2)}, u32[]{:S(2)}) collective-permute-start(bf16[2,16,256]{2,1,0:T(8,128)(2,1)S(1)} %select_select_fusion), channel_id=1, source_target_pairs={{0,192},{64,0},{128,64},{192,128},{1,193},{65,1},{129,65},{193,129... | collective-permute-start | bytes 49160 | tf_op jit(solution)/shard_map/ppermute | solution.py:476
  (3 other events, 2.3 us)

commit v5 on v4

--- a/solution.py
+++ b/solution.py
@@ -290,7 +290,7 @@
         in_specs=[pl.BlockSpec((mine, width), lambda i: (0, 0))],
         out_specs=pl.BlockSpec((HI * LO, mine, piece), lambda i: (0, 0, 0)),
         out_shape=jax.ShapeDtypeStruct((HI * LO, mine, piece), jnp.bfloat16),
-        compiler_params=params(60),
+        compiler_params=params(63),
         name="spread",
     )(dt_weight)
     quarter = exchange(quarter, ("hi", "lo")).reshape(rank, piece)
@@ -302,6 +302,14 @@
         wanted.astype(jnp.bfloat16), stored, preferred_element_type=jnp.float32
     ).astype(jnp.bfloat16)
     picked = picked.reshape(groups, reqs, states, piece)
+    source_group = lax.rem(group - jnp.arange(groups, dtype=jnp.int32) + groups, groups)
+    turns = lax.rem(jnp.arange(reqs, dtype=jnp.int32) + place[3], reqs)
+    request = (source_group[:, None] * reqs + turns[None, :]).reshape(-1)
+    ids = jnp.arange(count, dtype=jnp.int32)
+    ranks = jnp.sum((owners[:, None] == owners[None, :]) & (ids[None, :] < ids[:, None]), axis=1)
+    target = evict_order[0][ranks]
+    hits = (target[request][:, None] == slot_ids[None, :]) & (owners[request] == group)[:, None]
+
     def of_turn(turn):
         return lambda i, at, *_: (lax.rem(at[3] + turn, 2), 0, 0)
 
@@ -328,7 +336,7 @@
                 out_specs=pl.BlockSpec((LO, toks, columns), lambda i, at: (0, 0, 0)),
             ),
             out_shape=jax.ShapeDtypeStruct((LO, toks, columns), jnp.bfloat16),
-            compiler_params=params(60),
+            compiler_params=params(63),
             name="pack",
         )(place, conv_out, *[share] * (turn == 0))
         for turn, columns in enumerate((sent_width, chans))
@@ -348,7 +356,9 @@
     ]
     own_seed = wanted_by(group)
     first_got = exchange(first_sent, "lo")
-    second_sent, first_got, pieces = lax.optimization_barrier((sent[1], first_got, pieces))
+    second_sent, first_got, pieces, hits = lax.optimization_barrier(
+        (sent[1], first_got, pieces, hits)
+    )
     got = [first_got, exchange(second_sent, "lo")]
     second_share = lax.ppermute(first_got, "head", [(0, 1), (1, 0)])
 
@@ -403,7 +413,7 @@
                 [jax.ShapeDtypeStruct((leave_rows, LANES), jnp.bfloat16)] if last else []
             )
             + [rows_f32, rows_f32, jax.ShapeDtypeStruct((end_rows, LANES), jnp.float32)],
-            compiler_params=params(60),
+            compiler_params=params(63),
             cost_estimate=cost(15),
             name="scan",
         )(
@@ -456,7 +466,7 @@
                 else [jax.ShapeDtypeStruct((carry_rows, LANES), jnp.float32)] * (reqs - 1)
                 + [jax.ShapeDtypeStruct((reqs, states, piece), jnp.bfloat16)] * HI
             ),
-            compiler_params=params(60),
+            compiler_params=params(63),
             cost_estimate=cost(9),
             name="correct",
         )(
@@ -473,36 +483,34 @@
             out, held = lax.optimization_barrier((out, held))
         back.append(exchange(out, "lo"))
 
+    def unpack(turn, mixed):
+        return pl.pallas_call(
+            unpack_kernel,
+            grid_spec=pltpu.PrefetchScalarGridSpec(
+                num_scalar_prefetch=1,
+                grid=(1,),
+                in_specs=[whole(LO, toks, chans)]
+                + [pl.BlockSpec(memory_space=pl.ANY)] * len(mixed),
+                out_specs=pl.BlockSpec((1, toks, width), of_turn(turn)),
+            ),
+            out_shape=jax.ShapeDtypeStruct(conv_out.shape, jnp.bfloat16),
+            input_output_aliases={2: 0} if mixed else {},
+            compiler_params=params(16),
+            name="unpack",
+        )(place, back[turn], *mixed)
+
+    mixed = unpack(0, [])
+    held, mixed = lax.optimization_barrier((held, mixed))
+    for turn in range(1, reqs):
+        mixed = unpack(turn, [mixed])
+
     fresh = [held] + [lax.ppermute(held, "cache", shifts(groups, by)) for by in range(1, groups)]
     fresh = jnp.stack(fresh).reshape(count, -1)
-    source_group = lax.rem(group - jnp.arange(groups, dtype=jnp.int32) + groups, groups)
-    turns = lax.rem(jnp.arange(reqs, dtype=jnp.int32) + place[3], reqs)
-    request = (source_group[:, None] * reqs + turns[None, :]).reshape(-1)
-    ids = jnp.arange(count, dtype=jnp.int32)
-    ranks = jnp.sum((owners[:, None] == owners[None, :]) & (ids[None, :] < ids[:, None]), axis=1)
-    target = evict_order[0][ranks]
-    hits = (target[request][:, None] == slot_ids[None, :]) & (owners[request] == group)[:, None]
     rows = jnp.dot(
         hits.T.astype(jnp.bfloat16), fresh, preferred_element_type=jnp.float32
     ).astype(jnp.bfloat16)
     updated = jnp.where(jnp.any(hits, axis=0)[:, None], rows, stored)
 
-    mixed = None
-    for req in range(reqs):
-        mixed = pl.pallas_call(
-            unpack_kernel,
-            grid_spec=pltpu.PrefetchScalarGridSpec(
-                num_scalar_prefetch=1,
-                grid=(1,),
-                in_specs=[pl.BlockSpec((LO, toks, chans), lambda i, at: (0, 0, 0))]
-                + ([] if mixed is None else [pl.BlockSpec(memory_space=pl.ANY)]),
-                out_specs=pl.BlockSpec((1, toks, width), of_turn(req)),
-            ),
-            out_shape=jax.ShapeDtypeStruct(conv_out.shape, jnp.bfloat16),
-            input_output_aliases={} if mixed is None else {2: 0},
-            compiler_params=params(16),
-            name="unpack",
-        )(place, *([back[req]] if mixed is None else [back[req], mixed]))
     return mixed, updated.reshape(cache_states.shape)
 
 

time: 157 us -> 156 us (level)
    unnamed x38 -> x32, local copies, waits for them, and re-layouts: 4.51 us -> 3.47 us
  transfers between devices with their start and end apart: 18 -> 18, of which waited for: 11 -> 11; matrix products, arithmetic and copies ran while one was open for 5% -> 6% of each run, Pallas kernels for 22% -> 23%
where the time goes in v5:
time: 156 us; the launch traced here: 154 us
  Pallas kernels  65.6 us (42%)
  starting transfers between devices  49.8 us (32%)
  waiting for transfers between devices  27.1 us (17%)
  local copies, waits for them, and re-layouts  7 us (4%)
  other arithmetic  2.71 us (2%)
    pallas_call x2, Pallas kernels, on_device(): pl.pallas_call(functools.partial(scan_kernel, req), grid_spec=pltpu.Prefe...  30.9 us
    all_to_all x5, starting transfers between devices, exchange(): return lax.all_to_all(array, axis, split_axis=0, concat_axis=0, tiled=True)  30.7 us
    pallas_call x2, Pallas kernels, on_device(): pl.pallas_call(functools.partial(correct_kernel, req, reqs), grid_spec=pl...  22.2 us
    all_to_all x5, waiting for transfers between devices, exchange(): return lax.all_to_all(array, axis, split_axis=0, concat_axis=0, tiled=True)  10.8 us
    ppermute x3, waiting for transfers between devices, on_device(): lax.ppermute(leaving, 'hi', shifts(HI, by))  7.67 us
    ppermute x3, starting transfers between devices, on_device(): lax.ppermute(leaving, 'hi', shifts(HI, by))  6.55 us
    pallas_call x2, Pallas kernels, on_device(): pl.pallas_call(pack_kernel, grid_spec=pltpu.PrefetchScalarGridSpec(num_sc...  6.22 us
    ppermute x3, waiting for transfers between devices, on_device(): lax.ppermute(jnp.concatenate([quarter, wanted_by(lax.rem(group + by, grou...  5.65 us
  transfers between devices with their start and end apart: 18, of which 11 were waited for; matrix products, arithmetic and copies ran while one was open for 6% of the time, Pallas kernels for 23%

profile of v5, /device:TPU:8, one launch (start us, length us, event | category | flops | bytes accessed | tf_op | source)
XLA Modules:
  0.0 153.8 jit_solution(17619949887061168227)
XLA Ops:
  0.7 1.7 %spread.1 = bf16[32,16,256]{2,1,0:T(8,128)(2,1)} custom-call(bf16[16,8192]{1,0:T(8,128)(2,1)} %w_ref.1), custom_call_target="tpu_custom_call" | custom-call | tf_op jit(solution)/shard_map/spread/pallas_call | solution.py:287
  2.4 11.3 %all-to-all-start.1 = ((bf16[32,16,256]{2,1,0:T(8,128)(2,1)}), bf16[32,16,256]{2,1,0:T(8,128)(2,1)S(1)}, u32[]{:S(2)}, u32[]{:S(2)}) async-start(bf16[32,16,256]{2,1,0:T(8,128)(2,1)} %spread.1), calls=%async_computation.1 | async-start | bytes 524288 | tf_op jit(solution)/shard_map/all_to_all | solution.py:284
  14.5 1.2 copy.21
  18.1 3.3 %pack.3 = bf16[8,64,1664]{2,1,0:T(8,128)(2,1)} custom-call(s32[4]{0:T(128)} %pad_add_fusion.place_ref, bf16[2,64,8192]{2,1,0:T(8,128)(2,1)} %x_ref.3, bf16[64,640]{1,0:T(8,128)(2,1)} %maximum_maximum_fusion.refs_0_), custom_call_target="tpu_custom_call" | custom-call | tf_op jit(solution)/shard_map/pack/pallas_call | solution.py:329
  21.4 5.0 %all-to-all-done.1 = bf16[32,16,256]{2,1,0:T(8,128)(2,1)S(1)} async-done(((bf16[32,16,256]{2,1,0:T(8,128)(2,1)}), bf16[32,16,256]{2,1,0:T(8,128)(2,1)S(1)}, u32[]{:S(2)}, u32[]{:S(2)}) %all-to-all-start.1) | async-done | bytes 262176 | tf_op jit(solution)/shard_map/all_to_all | solution.py:284
  26.4 4.3 %all-to-all-start = ((bf16[8,64,1664]{2,1,0:T(8,128)(2,1)}), bf16[8,64,1664]{2,1,0:T(8,128)(2,1)}, u32[]{:S(2)}, u32[]{:S(2)}) async-start(bf16[8,64,1664]{2,1,0:T(8,128)(2,1)} %pack.3), calls=%async_computation | async-start | bytes 3407872 | tf_op jit(solution)/shard_map/all_to_all | solution.py:284
  33.4 1.6 %collective-permute-start = (bf16[544,256]{1,0:T(8,128)(2,1)}, bf16[544,256]{1,0:T(8,128)(2,1)}, u32[]{:S(2)}, u32[]{:S(2)}) collective-permute-start(bf16[544,256]{1,0:T(8,128)(2,1)} %get-tuple-element.62), channel_id=1, source_target_pairs={{0,64},{64,128},{128,192},{192,0},{1,65},{65,129},{129,193},{193,1... | collective-permute-start | bytes 835592 | tf_op jit(solution)/shard_map/ppermute | solution.py:350
  35.9 2.4 %collective-permute-start.2 = (bf16[544,256]{1,0:T(8,128)(2,1)}, bf16[544,256]{1,0:T(8,128)(2,1)}, u32[]{:S(2)}, u32[]{:S(2)}) collective-permute-start(bf16[544,256]{1,0:T(8,128)(2,1)} %get-tuple-element.60), channel_id=1, source_target_pairs={{0,192},{64,0},{128,64},{192,128},{1,193},{65,1},{129,65},{193,129... | collective-permute-start | bytes 835592 | tf_op jit(solution)/shard_map/ppermute | solution.py:350
  38.3 3.0 %pack.2 = bf16[8,64,1024]{2,1,0:T(8,128)(2,1)} custom-call(s32[4]{0:T(128)} %pad_add_fusion.place_ref, bf16[2,64,8192]{2,1,0:T(8,128)(2,1)} %x_ref.3), custom_call_target="tpu_custom_call" | custom-call | tf_op jit(solution)/shard_map/pack/pallas_call | solution.py:329
  43.3 2.9 %collective-permute-done.1.refs_2_.refs_3_.refs_20_ = bf16[544,256]{1,0:T(8,128)(2,1)} collective-permute-done((bf16[544,256]{1,0:T(8,128)(2,1)}, bf16[544,256]{1,0:T(8,128)(2,1)}, u32[]{:S(2)}, u32[]{:S(2)}) %collective-permute-start.1) | collective-permute-done | bytes 278560 | tf_op jit(solution)/shard_map/ppermute | solution.py:350
  46.2 2.1 %collective-permute-done.2.refs_3_.refs_4_.refs_21_ = bf16[544,256]{1,0:T(8,128)(2,1)} collective-permute-done((bf16[544,256]{1,0:T(8,128)(2,1)}, bf16[544,256]{1,0:T(8,128)(2,1)}, u32[]{:S(2)}, u32[]{:S(2)}) %collective-permute-start.2) | collective-permute-done | bytes 278560 | tf_op jit(solution)/shard_map/ppermute | solution.py:350
  48.3 2.7 %all-to-all-done.got_ref.tail_ref = bf16[8,64,1664]{2,1,0:T(8,128)(2,1)} async-done(((bf16[8,64,1664]{2,1,0:T(8,128)(2,1)}), bf16[8,64,1664]{2,1,0:T(8,128)(2,1)}, u32[]{:S(2)}, u32[]{:S(2)}) %all-to-all-start) | async-done | bytes 1703968 | tf_op jit(solution)/shard_map/all_to_all | solution.py:284
  51.0 4.3 %all-to-all-start.2 = ((bf16[8,64,1024]{2,1,0:T(8,128)(2,1)}), bf16[8,64,1024]{2,1,0:T(8,128)(2,1)}, u32[]{:S(2)}, u32[]{:S(2)}) async-start(bf16[8,64,1024]{2,1,0:T(8,128)(2,1)} %pack.2), calls=%async_computation.2 | async-start | bytes 2097152 | tf_op jit(solution)/shard_map/all_to_all | solution.py:284
  55.4 15.4 %scan.2 = (f32[4096,128]{1,0:T(8,128)}, f32[4096,128]{1,0:T(8,128)}, f32[136,128]{1,0:T(8,128)}) custom-call(s32[4]{0:T(128)} %pad_add_fusion.place_ref, s32[8]{0:T(128)} %lengths_ref.7, bf16[8,64,1664]{2,1,0:T(8,128)(2,1)} %all-to-all-done.got_ref.tail_ref, bf16[512,256]{1,0:T(8,128)(2,1)} %bitcast.54, ...), custom_call_target="tpu_custom_call" | custom-call | bytes 54000000 | tf_op jit(solution)/shard_map/scan/pallas_call | solution.py:389
  70.8 15.6 %scan.3 = (bf16[352,128]{1,0:T(8,128)(2,1)}, f32[4096,128]{1,0:T(8,128)}, f32[4096,128]{1,0:T(8,128)}, f32[136,128]{1,0:T(8,128)}) custom-call(s32[4]{0:T(128)} %pad_add_fusion.place_ref, s32[8]{0:T(128)} %lengths_ref.7, bf16[8,64,1024]{2,1,0:T(8,128)(2,1)} %all-to-all-done.2.got_ref, bf16[8,64,1664]{2,1,0:T(8,128)(2,1)} %collective-permute-done.3.refs_0_.tail_ref, ...), custom_call_target="tpu_custom_call" | custom-call | bytes 54000000 | tf_op jit(solution)/shard_map/scan/pallas_call | solution.py:389
  86.4 1.9 %collective-permute-start.4 = (bf16[352,128]{1,0:T(8,128)(2,1)}, bf16[352,128]{1,0:T(8,128)(2,1)S(1)}, u32[]{:S(2)}, u32[]{:S(2)}) collective-permute-start(bf16[352,128]{1,0:T(8,128)(2,1)} %get-tuple-element.41.refs_4_), channel_id=1, source_target_pairs={{0,16},{16,32},{32,48},{48,0},{1,17},{17,33},{33,49},{49,1},{2,18}... | collective-permute-start | bytes 270344 | tf_op jit(solution)/shard_map/ppermute | solution.py:429
  88.2 2.5 %collective-permute-start.5 = (bf16[352,128]{1,0:T(8,128)(2,1)}, bf16[352,128]{1,0:T(8,128)(2,1)S(1)}, u32[]{:S(2)}, u32[]{:S(2)}) collective-permute-start(bf16[352,128]{1,0:T(8,128)(2,1)} %get-tuple-element.41.refs_4_), channel_id=1, source_target_pairs={{0,32},{16,48},{32,0},{48,16},{1,33},{17,49},{33,1},{49,17},{2,34}... | collective-permute-start | bytes 270344 | tf_op jit(solution)/shard_map/ppermute | solution.py:429
  90.7 2.2 %collective-permute-start.6 = (bf16[352,128]{1,0:T(8,128)(2,1)}, bf16[352,128]{1,0:T(8,128)(2,1)S(1)}, u32[]{:S(2)}, u32[]{:S(2)}) collective-permute-start(bf16[352,128]{1,0:T(8,128)(2,1)} %get-tuple-element.41.refs_4_), channel_id=1, source_target_pairs={{0,48},{16,0},{32,16},{48,32},{1,49},{17,1},{33,17},{49,33},{2,50}... | collective-permute-start | bytes 270344 | tf_op jit(solution)/shard_map/ppermute | solution.py:429
  93.8 4.9 %collective-permute-done.5.refs_6_ = bf16[352,128]{1,0:T(8,128)(2,1)S(1)} collective-permute-done((bf16[352,128]{1,0:T(8,128)(2,1)}, bf16[352,128]{1,0:T(8,128)(2,1)S(1)}, u32[]{:S(2)}, u32[]{:S(2)}) %collective-permute-start.5) | collective-permute-done | bytes 90144 | tf_op jit(solution)/shard_map/ppermute | solution.py:429
  98.8 1.8 %collective-permute-done.6.refs_7_ = bf16[352,128]{1,0:T(8,128)(2,1)S(1)} collective-permute-done((bf16[352,128]{1,0:T(8,128)(2,1)}, bf16[352,128]{1,0:T(8,128)(2,1)S(1)}, u32[]{:S(2)}, u32[]{:S(2)}) %collective-permute-start.6) | collective-permute-done | bytes 90144 | tf_op jit(solution)/shard_map/ppermute | solution.py:429
  101.2 11.4 %correct.2 = (bf16[8,64,1024]{2,1,0:T(8,128)(2,1)}, f32[128,128]{1,0:T(8,128)}, bf16[2,16,256]{2,1,0:T(8,128)(2,1)}, bf16[2,16,256]{2,1,0:T(8,128)(2,1)}, bf16[2...) custom-call(s32[4]{0:T(128)} %pad_add_fusion.place_ref, s32[8]{0:T(128)} %lengths_ref.7, ...), custom_call_target="tpu_custom_call" | custom-call | bytes 32400000 | tf_op jit(solution)/shard_map/correct/pallas_call | solution.py:433
  112.7 6.3 %all-to-all-start.4 = ((bf16[8,64,1024]{2,1,0:T(8,128)(2,1)}), bf16[8,64,1024]{2,1,0:T(8,128)(2,1)}, u32[]{:S(2)}, u32[]{:S(2)}) async-start(bf16[8,64,1024]{2,1,0:T(8,128)(2,1)} %get-tuple-element.50), calls=%async_computation.4 | async-start | bytes 2097152 | tf_op jit(solution)/shard_map/all_to_all | solution.py:284
  120.3 1.3 collective-permute-start.9
  121.6 10.8 %correct.3 = bf16[8,64,1024]{2,1,0:T(8,128)(2,1)} custom-call(s32[4]{0:T(128)} %pad_add_fusion.place_ref, s32[8]{0:T(128)} %lengths_ref.7, f32[4096,128]{1,0:T(8,128)} %get-tuple-element.37.y_ref, f32[4096,128]{1,0:T(8,128)} %get-tuple-element.38.total_ref, bf16[8,64,1664]{2,1,0:T(8,128)(2,1)} %collective-permute-done.3.refs_0_.tail_ref, ...), custom_call_target="tpu_custom_call" | custom-call | bytes 32400000 | tf_op jit(solution)/shard_map/correct/pallas_call | solution.py:433
  132.4 1.1 collective-permute-done.9
  133.5 4.6 %all-to-all-start.3 = ((bf16[8,64,1024]{2,1,0:T(8,128)(2,1)}), bf16[8,64,1024]{2,1,0:T(8,128)(2,1)S(1)}, u32[]{:S(2)}, u32[]{:S(2)}) async-start(bf16[8,64,1024]{2,1,0:T(8,128)(2,1)} %correct.3), calls=%async_computation.3 | async-start | bytes 2097152 | tf_op jit(solution)/shard_map/all_to_all | solution.py:284
  138.1 2.9 %unpack.2.refs_0_ = bf16[2,64,8192]{2,1,0:T(8,128)(2,1)} custom-call(s32[4]{0:T(128)S(1)} %copy-done.1, bf16[8,64,1024]{2,1,0:T(8,128)(2,1)} %all-to-all-done.4.back_ref), custom_call_target="tpu_custom_call" | custom-call | tf_op jit(solution)/shard_map/unpack/pallas_call | solution.py:487
  141.0 1.6 %collective-permute-start.10 = (bf16[2,16,256]{2,1,0:T(8,128)(2,1)S(1)}, bf16[2,16,256]{2,1,0:T(8,128)(2,1)S(1)}, u32[]{:S(2)}, u32[]{:S(2)}) collective-permute-start(bf16[2,16,256]{2,1,0:T(8,128)(2,1)S(1)} %select_select_fusion), channel_id=1, source_target_pairs={{0,64},{64,128},{128,192},{192,0},{1,65},{65,129},{129,193},{193,1... | collective-permute-start | bytes 49160 | tf_op jit(solution)/shard_map/ppermute | solution.py:507
  143.5 2.4 %collective-permute-start.12 = (bf16[2,16,256]{2,1,0:T(8,128)(2,1)S(1)}, bf16[2,16,256]{2,1,0:T(8,128)(2,1)S(1)}, u32[]{:S(2)}, u32[]{:S(2)}) collective-permute-start(bf16[2,16,256]{2,1,0:T(8,128)(2,1)S(1)} %select_select_fusion), channel_id=1, source_target_pairs={{0,192},{64,0},{128,64},{192,128},{1,193},{65,1},{129,65},{193,129... | collective-permute-start | bytes 49160 | tf_op jit(solution)/shard_map/ppermute | solution.py:507
  146.0 1.9 %collective-permute-done.11 = bf16[2,16,256]{2,1,0:T(8,128)(2,1)S(1)} collective-permute-done((bf16[2,16,256]{2,1,0:T(8,128)(2,1)S(1)}, bf16[2,16,256]{2,1,0:T(8,128)(2,1)S(1)}, u32[]{:S(2)}, u32[]{:S(2)}) %collective-permute-start.11) | collective-permute-done | bytes 16416 | tf_op jit(solution)/shard_map/ppermute | solution.py:507
  149.1 3.0 %all-to-all-done.3.back_ref = bf16[8,64,1024]{2,1,0:T(8,128)(2,1)S(1)} async-done(((bf16[8,64,1024]{2,1,0:T(8,128)(2,1)}), bf16[8,64,1024]{2,1,0:T(8,128)(2,1)S(1)}, u32[]{:S(2)}, u32[]{:S(2)}) %all-to-all-start.3) | async-done | bytes 1048608 | tf_op jit(solution)/shard_map/all_to_all | solution.py:284
  152.2 1.6 %unpack.3 = bf16[2,64,8192]{2,1,0:T(8,128)(2,1)} custom-call(s32[4]{0:T(128)S(1)} %copy-done.1, bf16[8,64,1024]{2,1,0:T(8,128)(2,1)S(1)} %all-to-all-done.3.back_ref, bf16[2,64,8192]{2,1,0:T(8,128)(2,1)} %unpack.2.refs_0_), custom_call_target="tpu_custom_call", output_to_operand_aliasing={{}: (2, {})} | custom-call | tf_op jit(solution)/shard_map/unpack/pallas_call | solution.py:487
  (74 shorter events, 13.9 us)
Async XLA Ops:
  0.6 13.8 %copy-start = (bf16[2,64,512]{2,1,0:T(8,128)(2,1)S(1)}, bf16[2,64,512]{2,1,0:T(8,128)(2,1)}, u32[]{:S(2)}) copy-start(bf16[2,64,512]{2,1,0:T(8,128)(2,1)} %param.13) | copy-start | bytes 393220
  0.6 15.1 %copy-start.2 = (s32[8,1]{0,1:T(1,128)S(1)}, s32[8,1]{0,1:T(1,128)}, u32[]{:S(2)}) copy-start(s32[8,1]{0,1:T(1,128)} %param.20) | copy-start | bytes 100
  0.7 15.1 %copy-start.10 = (s32[8]{0:T(128)S(1)}, s32[8]{0:T(128)}, u32[]{:S(2)}) copy-start(s32[8]{0:T(128)} %param.21) | copy-start | bytes 100
  2.4 24.0 %all-to-all-start.1 = ((bf16[32,16,256]{2,1,0:T(8,128)(2,1)}), bf16[32,16,256]{2,1,0:T(8,128)(2,1)S(1)}, u32[]{:S(2)}, u32[]{:S(2)}) async-start(bf16[32,16,256]{2,1,0:T(8,128)(2,1)} %spread.1), calls=%async_computation.1 | async-start | bytes 524288 | tf_op jit(solution)/shard_map/all_to_all | solution.py:284
  21.4 10.4 %copy-start.5 = (bf16[1,8,16,256]{3,2,1,0:T(8,128)(2,1)S(1)}, bf16[1,8,16,256]{3,2,1,0:T(8,128)(2,1)}, u32[]{:S(2)}) copy-start(bf16[1,8,16,256]{3,2,1,0:T(8,128)(2,1)} %copy.22) | copy-start | bytes 196612
  26.4 7.0 %copy-start.4 = (bf16[32,16,256]{2,1,0:T(8,128)(2,1)}, bf16[32,16,256]{2,1,0:T(8,128)(2,1)S(1)}, u32[]{:S(2)}) copy-start(bf16[32,16,256]{2,1,0:T(8,128)(2,1)S(1)} %all-to-all-done.1) | copy-start | bytes 786436
  26.4 24.6 %all-to-all-start = ((bf16[8,64,1664]{2,1,0:T(8,128)(2,1)}), bf16[8,64,1664]{2,1,0:T(8,128)(2,1)}, u32[]{:S(2)}, u32[]{:S(2)}) async-start(bf16[8,64,1664]{2,1,0:T(8,128)(2,1)} %pack.3), calls=%async_computation | async-start | bytes 3407872 | tf_op jit(solution)/shard_map/all_to_all | solution.py:284
  32.4 8.9 %copy-start.3 = (s32[1,64]{1,0:T(1,128)S(1)}, s32[1,64]{1,0:T(1,128)}, u32[]{:S(2)}) copy-start(s32[1,64]{1,0:T(1,128)} %param.22) | copy-start | bytes 772
  33.4 9.9 %collective-permute-start = (bf16[544,256]{1,0:T(8,128)(2,1)}, bf16[544,256]{1,0:T(8,128)(2,1)}, u32[]{:S(2)}, u32[]{:S(2)}) collective-permute-start(bf16[544,256]{1,0:T(8,128)(2,1)} %get-tuple-element.62), channel_id=1, source_target_pairs={{0,64},{64,128},{128,192},{192,0},{1,65},{65,129},{129,193},{193,1... | collective-permute-start | bytes 835592 | tf_op jit(solution)/shard_map/ppermute | solution.py:350
  35.0 11.2 %collective-permute-start.1 = (bf16[544,256]{1,0:T(8,128)(2,1)}, bf16[544,256]{1,0:T(8,128)(2,1)}, u32[]{:S(2)}, u32[]{:S(2)}) collective-permute-start(bf16[544,256]{1,0:T(8,128)(2,1)} %get-tuple-element.61), channel_id=1, source_target_pairs={{0,128},{64,192},{128,0},{192,64},{1,129},{65,193},{129,1},{193,65... | collective-permute-start | bytes 835592 | tf_op jit(solution)/shard_map/ppermute | solution.py:350
  35.9 12.4 %collective-permute-start.2 = (bf16[544,256]{1,0:T(8,128)(2,1)}, bf16[544,256]{1,0:T(8,128)(2,1)}, u32[]{:S(2)}, u32[]{:S(2)}) collective-permute-start(bf16[544,256]{1,0:T(8,128)(2,1)} %get-tuple-element.60), channel_id=1, source_target_pairs={{0,192},{64,0},{128,64},{192,128},{1,193},{65,1},{129,65},{193,129... | collective-permute-start | bytes 835592 | tf_op jit(solution)/shard_map/ppermute | solution.py:350
  51.0 19.7 %all-to-all-start.2 = ((bf16[8,64,1024]{2,1,0:T(8,128)(2,1)}), bf16[8,64,1024]{2,1,0:T(8,128)(2,1)}, u32[]{:S(2)}, u32[]{:S(2)}) async-start(bf16[8,64,1024]{2,1,0:T(8,128)(2,1)} %pack.2), calls=%async_computation.2 | async-start | bytes 2097152 | tf_op jit(solution)/shard_map/all_to_all | solution.py:284
  55.3 15.5 %collective-permute-start.3 = (bf16[8,64,1664]{2,1,0:T(8,128)(2,1)}, bf16[8,64,1664]{2,1,0:T(8,128)(2,1)}, u32[]{:S(2)}, u32[]{:S(2)}) collective-permute-start(bf16[8,64,1664]{2,1,0:T(8,128)(2,1)} %all-to-all-done.got_ref.tail_ref), channel_id=1, source_target_pairs={{0,1},{1,0},{2,3},{3,2},{4,5},{5,4},{6,7},{7,6},{8,9},{9,8},{10,11... | collective-permute-start | bytes 5111816 | tf_op jit(solution)/shard_map/ppermute | solution.py:363
  86.4 7.5 %collective-permute-start.4 = (bf16[352,128]{1,0:T(8,128)(2,1)}, bf16[352,128]{1,0:T(8,128)(2,1)S(1)}, u32[]{:S(2)}, u32[]{:S(2)}) collective-permute-start(bf16[352,128]{1,0:T(8,128)(2,1)} %get-tuple-element.41.refs_4_), channel_id=1, source_target_pairs={{0,16},{16,32},{32,48},{48,0},{1,17},{17,33},{33,49},{49,1},{2,18}... | collective-permute-start | bytes 270344 | tf_op jit(solution)/shard_map/ppermute | solution.py:429
  88.2 10.5 %collective-permute-start.5 = (bf16[352,128]{1,0:T(8,128)(2,1)}, bf16[352,128]{1,0:T(8,128)(2,1)S(1)}, u32[]{:S(2)}, u32[]{:S(2)}) collective-permute-start(bf16[352,128]{1,0:T(8,128)(2,1)} %get-tuple-element.41.refs_4_), channel_id=1, source_target_pairs={{0,32},{16,48},{32,0},{48,16},{1,33},{17,49},{33,1},{49,17},{2,34}... | collective-permute-start | bytes 270344 | tf_op jit(solution)/shard_map/ppermute | solution.py:429
  90.7 9.9 %collective-permute-start.6 = (bf16[352,128]{1,0:T(8,128)(2,1)}, bf16[352,128]{1,0:T(8,128)(2,1)S(1)}, u32[]{:S(2)}, u32[]{:S(2)}) collective-permute-start(bf16[352,128]{1,0:T(8,128)(2,1)} %get-tuple-element.41.refs_4_), channel_id=1, source_target_pairs={{0,48},{16,0},{32,16},{48,32},{1,49},{17,1},{33,17},{49,33},{2,50}... | collective-permute-start | bytes 270344 | tf_op jit(solution)/shard_map/ppermute | solution.py:429
  93.8 6.8 %copy-start.6 = (bf16[352,128]{1,0:T(8,128)(2,1)}, bf16[352,128]{1,0:T(8,128)(2,1)S(1)}, u32[]{:S(2)}) copy-start(bf16[352,128]{1,0:T(8,128)(2,1)S(1)} %collective-permute-done.4.refs_5_) | copy-start | bytes 270340
  98.8 1.9 %copy-start.7 = (bf16[352,128]{1,0:T(8,128)(2,1)}, bf16[352,128]{1,0:T(8,128)(2,1)S(1)}, u32[]{:S(2)}) copy-start(bf16[352,128]{1,0:T(8,128)(2,1)S(1)} %collective-permute-done.5.refs_6_) | copy-start | bytes 270340
  100.6 0.6 copy-start.8
  112.6 6.3 %copy-start.13 = (bf16[2,16,256]{2,1,0:T(8,128)(2,1)S(1)}, bf16[2,16,256]{2,1,0:T(8,128)(2,1)}, u32[]{:S(2)}) copy-start(bf16[2,16,256]{2,1,0:T(8,128)(2,1)} %get-tuple-element.44) | copy-start | bytes 49156
  112.7 7.0 %copy-start.12 = (bf16[2,16,256]{2,1,0:T(8,128)(2,1)S(1)}, bf16[2,16,256]{2,1,0:T(8,128)(2,1)}, u32[]{:S(2)}) copy-start(bf16[2,16,256]{2,1,0:T(8,128)(2,1)} %get-tuple-element.45) | copy-start | bytes 49156
  112.7 7.6 %copy-start.11 = (bf16[2,16,256]{2,1,0:T(8,128)(2,1)S(1)}, bf16[2,16,256]{2,1,0:T(8,128)(2,1)}, u32[]{:S(2)}) copy-start(bf16[2,16,256]{2,1,0:T(8,128)(2,1)} %get-tuple-element.46) | copy-start | bytes 49156
  112.7 20.9 %all-to-all-start.4 = ((bf16[8,64,1024]{2,1,0:T(8,128)(2,1)}), bf16[8,64,1024]{2,1,0:T(8,128)(2,1)}, u32[]{:S(2)}, u32[]{:S(2)}) async-start(bf16[8,64,1024]{2,1,0:T(8,128)(2,1)} %get-tuple-element.50), calls=%async_computation.4 | async-start | bytes 2097152 | tf_op jit(solution)/shard_map/all_to_all | solution.py:284
  118.9 13.5 %collective-permute-start.7 = (bf16[2,16,256]{2,1,0:T(8,128)(2,1)S(1)}, bf16[2,16,256]{2,1,0:T(8,128)(2,1)S(1)}, u32[]{:S(2)}, u32[]{:S(2)}) collective-permute-start(bf16[2,16,256]{2,1,0:T(8,128)(2,1)S(1)} %copy-done.13), channel_id=1, source_target_pairs={{48,32},{49,33},{50,34},{51,35},{52,36},{53,37},{54,38},{55,39},{5... | collective-permute-start | bytes 49160 | tf_op jit(solution)/shard_map/ppermute | solution.py:481
  119.6 12.8 %collective-permute-start.8 = (bf16[2,16,256]{2,1,0:T(8,128)(2,1)S(1)}, bf16[2,16,256]{2,1,0:T(8,128)(2,1)S(1)}, u32[]{:S(2)}, u32[]{:S(2)}) collective-permute-start(bf16[2,16,256]{2,1,0:T(8,128)(2,1)S(1)} %copy-done.12), channel_id=1, source_target_pairs={{48,16},{49,17},{50,18},{51,19},{52,20},{53,21},{54,22},{55,23},{5... | collective-permute-start | bytes 49160 | tf_op jit(solution)/shard_map/ppermute | solution.py:481
  120.3 13.2 %collective-permute-start.9 = (bf16[2,16,256]{2,1,0:T(8,128)(2,1)S(1)}, bf16[2,16,256]{2,1,0:T(8,128)(2,1)S(1)}, u32[]{:S(2)}, u32[]{:S(2)}) collective-permute-start(bf16[2,16,256]{2,1,0:T(8,128)(2,1)S(1)} %copy-done.11), channel_id=1, source_target_pairs={{48,0},{49,1},{50,2},{51,3},{52,4},{53,5},{54,6},{55,7},{56,8},{57... | collective-permute-start | bytes 49160 | tf_op jit(solution)/shard_map/ppermute | solution.py:481
  121.6 11.9 %copy-start.9 = (bf16[2,16,256]{2,1,0:T(8,128)(2,1)S(1)}, bf16[2,16,256]{2,1,0:T(8,128)(2,1)}, u32[]{:S(2)}) copy-start(bf16[2,16,256]{2,1,0:T(8,128)(2,1)} %get-tuple-element.47) | copy-start | bytes 49156
  132.4 5.8 %copy-start.1 = (s32[4]{0:T(128)S(1)}, s32[4]{0:T(128)}, u32[]{:S(2)}) copy-start(s32[4]{0:T(128)} %pad_add_fusion.place_ref) | copy-start | bytes 52
  133.5 18.6 %all-to-all-start.3 = ((bf16[8,64,1024]{2,1,0:T(8,128)(2,1)}), bf16[8,64,1024]{2,1,0:T(8,128)(2,1)S(1)}, u32[]{:S(2)}, u32[]{:S(2)}) async-start(bf16[8,64,1024]{2,1,0:T(8,128)(2,1)} %correct.3), calls=%async_computation.3 | async-start | bytes 2097152 | tf_op jit(solution)/shard_map/all_to_all | solution.py:284
  141.0 5.0 %collective-permute-start.10 = (bf16[2,16,256]{2,1,0:T(8,128)(2,1)S(1)}, bf16[2,16,256]{2,1,0:T(8,128)(2,1)S(1)}, u32[]{:S(2)}, u32[]{:S(2)}) collective-permute-start(bf16[2,16,256]{2,1,0:T(8,128)(2,1)S(1)} %select_select_fusion), channel_id=1, source_target_pairs={{0,64},{64,128},{128,192},{192,0},{1,65},{65,129},{129,193},{193,1... | collective-permute-start | bytes 49160 | tf_op jit(solution)/shard_map/ppermute | solution.py:507
  142.6 5.2 %collective-permute-start.11 = (bf16[2,16,256]{2,1,0:T(8,128)(2,1)S(1)}, bf16[2,16,256]{2,1,0:T(8,128)(2,1)S(1)}, u32[]{:S(2)}, u32[]{:S(2)}) collective-permute-start(bf16[2,16,256]{2,1,0:T(8,128)(2,1)S(1)} %select_select_fusion), channel_id=1, source_target_pairs={{0,128},{64,192},{128,0},{192,64},{1,129},{65,193},{129,1},{193,65... | collective-permute-start | bytes 49160 | tf_op jit(solution)/shard_map/ppermute | solution.py:507
  143.5 4.3 %collective-permute-start.12 = (bf16[2,16,256]{2,1,0:T(8,128)(2,1)S(1)}, bf16[2,16,256]{2,1,0:T(8,128)(2,1)S(1)}, u32[]{:S(2)}, u32[]{:S(2)}) collective-permute-start(bf16[2,16,256]{2,1,0:T(8,128)(2,1)S(1)} %select_select_fusion), channel_id=1, source_target_pairs={{0,192},{64,0},{128,64},{192,128},{1,193},{65,1},{129,65},{193,129... | collective-permute-start | bytes 49160 | tf_op jit(solution)/shard_map/ppermute | solution.py:507

commit v6 on v5

--- a/solution.py
+++ b/solution.py
@@ -178,13 +178,24 @@
     return jnp.concatenate(blocks, axis=0).astype(jnp.bfloat16)
 
 
-def join(place_ref, sent_refs, end_refs, decay_scr, carry_refs, final_refs, state_scr):
+def join(place_ref, sent_refs, decay_scr, carry_refs, final_ref, state_scr):
     states = decay_scr.shape[0] // ROWS
-    reqs = len(end_refs)
+    reqs = len(carry_refs)
     hi = place_ref[0]
     per_req = (states + 2) * ROWS
     blocks = [ref[...].astype(jnp.float32) for ref in sent_refs]
+
+    def of_shard(shard, values):
+        distance = lax.rem(hi - shard + HI, HI)
+        value = values[0]
+        for by in range(1, HI):
+            value = jnp.where(distance == by, values[by], value)
+        return value
+
     for req in range(reqs):
+        ends = [block[req * per_req : (req + 1) * per_req] for block in blocks]
+        totals = [end[states * ROWS : (states + 1) * ROWS] + end[(states + 1) * ROWS :] for end in ends]
+        in_order = [of_shard(shard, totals) for shard in range(HI)]
         for by, block in enumerate(blocks):
             slot = lax.rem(hi - by + HI, HI)
             for j in range(2):
@@ -193,27 +204,26 @@
         for n in range(states):
             rows = slice(n * ROWS, (n + 1) * ROWS)
             decay = decay_scr[rows, :]
-            carry = state_scr[rows, :]
+            carry = final = state_scr[rows, :]
             for by in range(HI - 1, 0, -1):
-                block = blocks[by][req * per_req : (req + 1) * per_req]
-                total = block[states * ROWS : (states + 1) * ROWS] + block[(states + 1) * ROWS :]
-                longer = block[rows] + jnp.exp2(total * decay) * carry
+                longer = ends[by][rows] + jnp.exp2(totals[by] * decay) * carry
                 carry = jnp.where(hi >= by, longer, carry)
             carry_refs[req][rows, :] = carry
-            total = end_refs[req][states * ROWS :, :]
-            state_scr[rows, :] = end_refs[req][rows, :] + jnp.exp2(total * decay) * carry
-        for p in range(HI):
-            for j in range(2):
-                value = state_scr[pl.ds(2 * p + j, states, stride=ROWS), :]
-                final_refs[p][req, :, j * LANES : (j + 1) * LANES] = value.astype(jnp.bfloat16)
+            for shard in range(HI):
+                end = of_shard(shard, [end[rows] for end in ends])
+                final = end + jnp.exp2(in_order[shard] * decay) * final
+            state_scr[rows, :] = final
+        for j in range(2):
+            value = state_scr[pl.ds(2 * hi + j, states, stride=ROWS), :]
+            final_ref[req, :, j * LANES : (j + 1) * LANES] = value.astype(jnp.bfloat16)
 
 
 def correct_kernel(turn, reqs, place_ref, lengths_ref, y_ref, total_ref, tail_ref, *refs):
     decay_refs, refs = refs[:HI], refs[HI:]
     y_scr, c_scr, decay_scr, carry_scr, state_scr = refs[-5:]
     if turn == 0:
-        sent_refs, end_refs, refs = refs[:HI], refs[HI : HI + reqs], refs[HI + reqs :]
-        out_ref, carry_refs, final_refs = refs[0], refs[1:reqs], refs[reqs : reqs + HI]
+        sent_refs, refs = refs[:HI], refs[HI:]
+        out_ref, carry_refs, final_ref = refs[0], refs[1:reqs], refs[reqs]
     else:
         carry_ref, out_ref = refs[:2]
     parts, toks, _ = out_ref.shape
@@ -227,7 +237,7 @@
         decay_scr[...] = decay_scr[...] * (-LOG2E)
         if turn == 0:
             carries = (carry_scr, *carry_refs)
-            join(place_ref, sent_refs, end_refs, decay_scr, carries, final_refs, state_scr)
+            join(place_ref, sent_refs, decay_scr, carries, final_ref, state_scr)
         else:
             carry_scr[...] = carry_ref[...]
 
@@ -446,14 +456,14 @@
                 + (
                     [whole(carry_rows, LANES)]
                     if req
-                    else [whole(leave_rows, LANES)] * HI + [whole(end_rows, LANES)] * reqs
+                    else [whole(leave_rows, LANES)] * HI
                 ),
                 out_specs=[pl.BlockSpec((parts, toks, chans), lambda i, *at: (i, 0, 0))]
                 + (
                     []
                     if req
                     else [whole(carry_rows, LANES)] * (reqs - 1)
-                    + [whole(reqs, states, piece)] * HI
+                    + [whole(reqs, states, piece)]
                 ),
                 scratch_shapes=scratch(
                     rows * ROWS, states * rows, carry_rows, carry_rows, carry_rows
@@ -464,23 +474,17 @@
                 []
                 if req
                 else [jax.ShapeDtypeStruct((carry_rows, LANES), jnp.float32)] * (reqs - 1)
-                + [jax.ShapeDtypeStruct((reqs, states, piece), jnp.bfloat16)] * HI
+                + [jax.ShapeDtypeStruct((reqs, states, piece), jnp.bfloat16)]
             ),
             compiler_params=params(63),
             cost_estimate=cost(9),
             name="correct",
         )(
             place, new_lengths, y[req], total[req], second_share if req else first_got,
-            *[decay_rate] * HI, *([carry[req - 1]] if req else [leaving, *arrived, *end]),
+            *[decay_rate] * HI, *([carry[req - 1]] if req else [leaving, *arrived]),
         )
         if req == 0:
-            carry, finals = more[: reqs - 1], more[reqs - 1 :]
-        if req == reqs - 1:
-            held = finals[HI - 1]
-            for to in range(HI - 1):
-                moved = lax.ppermute(finals[to], "hi", [(HI - 1, to)])
-                held = jnp.where(hi == to, moved, held)
-            out, held = lax.optimization_barrier((out, held))
+            carry, held = more[: reqs - 1], more[reqs - 1]
         back.append(exchange(out, "lo"))
 
     def unpack(turn, mixed):
@@ -501,8 +505,6 @@
 
     mixed = unpack(0, [])
     held, mixed = lax.optimization_barrier((held, mixed))
-    for turn in range(1, reqs):
-        mixed = unpack(turn, [mixed])
 
     fresh = [held] + [lax.ppermute(held, "cache", shifts(groups, by)) for by in range(1, groups)]
     fresh = jnp.stack(fresh).reshape(count, -1)
@@ -511,7 +513,11 @@
     ).astype(jnp.bfloat16)
     updated = jnp.where(jnp.any(hits, axis=0)[:, None], rows, stored)
 
-    return mixed, updated.reshape(cache_states.shape)
+    updated = updated.reshape(cache_states.shape)
+    back[-1], updated = lax.optimization_barrier((back[-1], updated))
+    for turn in range(1, reqs):
+        mixed = unpack(turn, [mixed])
+    return mixed, updated
 
 
 def solution(mesh):

time: 156 us -> 155 us (level)
  waiting for transfers between devices: 27.1 us -> 30.8 us
  starting transfers between devices: 49.8 us -> 46.2 us
    all_to_all x5, waiting for transfers between devices: 10.8 us -> 15.6 us  [exchange(): return lax.all_to_all(array, axis, split_axis=0, concat_axis=0, tiled=True)]
    ppermute x3 -> x0, starting transfers between devices: 2.62 us -> none  [on_device(): moved = lax.ppermute(finals[to], 'hi', [(HI - 1, to)])]
    unnamed x32 -> x26, local copies, waits for them, and re-layouts: 3.47 us -> 3.45 us
  transfers between devices with their start and end apart: 18 -> 15, of which waited for: 11 -> 11; matrix products, arithmetic and copies ran while one was open for 6% -> 6% of each run, Pallas kernels for 23% -> 23%
where the time goes in v6:
time: 155 us; the launch traced here: 153 us
  Pallas kernels  65.3 us (42%)
  starting transfers between devices  46.2 us (30%)
  waiting for transfers between devices  30.8 us (20%)
  local copies, waits for them, and re-layouts  6.98 us (5%)
  other arithmetic  2.76 us (2%)
    pallas_call x2, Pallas kernels, on_device(): pl.pallas_call(functools.partial(scan_kernel, req), grid_spec=pltpu.Prefe...  30.9 us
    all_to_all x5, starting transfers between devices, exchange(): return lax.all_to_all(array, axis, split_axis=0, concat_axis=0, tiled=True)  29.6 us
    pallas_call x2, Pallas kernels, on_device(): pl.pallas_call(functools.partial(correct_kernel, req, reqs), grid_spec=pl...  21.9 us
    all_to_all x5, waiting for transfers between devices, exchange(): return lax.all_to_all(array, axis, split_axis=0, concat_axis=0, tiled=True)  15.6 us
    ppermute x3, waiting for transfers between devices, on_device(): lax.ppermute(leaving, 'hi', shifts(HI, by))  7.67 us
    ppermute x3, starting transfers between devices, on_device(): lax.ppermute(leaving, 'hi', shifts(HI, by))  6.57 us
    pallas_call x2, Pallas kernels, on_device(): pl.pallas_call(pack_kernel, grid_spec=pltpu.PrefetchScalarGridSpec(num_sc...  6.23 us
    ppermute x3, waiting for transfers between devices, on_device(): lax.ppermute(jnp.concatenate([quarter, wanted_by(lax.rem(group + by, grou...  5.64 us
  transfers between devices with their start and end apart: 15, of which 11 were waited for; matrix products, arithmetic and copies ran while one was open for 6% of the time, Pallas kernels for 23%

profile of v6, /device:TPU:8, one launch (start us, length us, event | category | flops | bytes accessed | tf_op | source)
XLA Modules:
  0.0 153.4 jit_solution(13084236415155282764)
XLA Ops:
  0.7 1.7 %spread.1 = bf16[32,16,256]{2,1,0:T(8,128)(2,1)} custom-call(bf16[16,8192]{1,0:T(8,128)(2,1)} %w_ref.1), custom_call_target="tpu_custom_call" | custom-call | tf_op jit(solution)/shard_map/spread/pallas_call | solution.py:297
  2.4 11.3 %all-to-all-start.1 = ((bf16[32,16,256]{2,1,0:T(8,128)(2,1)}), bf16[32,16,256]{2,1,0:T(8,128)(2,1)S(1)}, u32[]{:S(2)}, u32[]{:S(2)}) async-start(bf16[32,16,256]{2,1,0:T(8,128)(2,1)} %spread.1), calls=%async_computation.1 | async-start | bytes 524288 | tf_op jit(solution)/shard_map/all_to_all | solution.py:294
  14.5 1.2 copy.21
  18.2 3.3 %pack.3 = bf16[8,64,1664]{2,1,0:T(8,128)(2,1)} custom-call(s32[4]{0:T(128)} %pad_add_fusion.place_ref, bf16[2,64,8192]{2,1,0:T(8,128)(2,1)} %x_ref.3, bf16[64,640]{1,0:T(8,128)(2,1)} %maximum_maximum_fusion.refs_0_), custom_call_target="tpu_custom_call" | custom-call | tf_op jit(solution)/shard_map/pack/pallas_call | solution.py:339
  21.4 5.0 %all-to-all-done.1 = bf16[32,16,256]{2,1,0:T(8,128)(2,1)S(1)} async-done(((bf16[32,16,256]{2,1,0:T(8,128)(2,1)}), bf16[32,16,256]{2,1,0:T(8,128)(2,1)S(1)}, u32[]{:S(2)}, u32[]{:S(2)}) %all-to-all-start.1) | async-done | bytes 262176 | tf_op jit(solution)/shard_map/all_to_all | solution.py:294
  26.4 4.3 %all-to-all-start = ((bf16[8,64,1664]{2,1,0:T(8,128)(2,1)}), bf16[8,64,1664]{2,1,0:T(8,128)(2,1)}, u32[]{:S(2)}, u32[]{:S(2)}) async-start(bf16[8,64,1664]{2,1,0:T(8,128)(2,1)} %pack.3), calls=%async_computation | async-start | bytes 3407872 | tf_op jit(solution)/shard_map/all_to_all | solution.py:294
  32.4 1.0 pad_maximum_fusion.2
  33.4 1.6 %collective-permute-start = (bf16[544,256]{1,0:T(8,128)(2,1)}, bf16[544,256]{1,0:T(8,128)(2,1)}, u32[]{:S(2)}, u32[]{:S(2)}) collective-permute-start(bf16[544,256]{1,0:T(8,128)(2,1)} %get-tuple-element.54), channel_id=1, source_target_pairs={{0,64},{64,128},{128,192},{192,0},{1,65},{65,129},{129,193},{193,1... | collective-permute-start | bytes 835592 | tf_op jit(solution)/shard_map/ppermute | solution.py:360
  35.9 2.4 %collective-permute-start.2 = (bf16[544,256]{1,0:T(8,128)(2,1)}, bf16[544,256]{1,0:T(8,128)(2,1)}, u32[]{:S(2)}, u32[]{:S(2)}) collective-permute-start(bf16[544,256]{1,0:T(8,128)(2,1)} %get-tuple-element.52), channel_id=1, source_target_pairs={{0,192},{64,0},{128,64},{192,128},{1,193},{65,1},{129,65},{193,129... | collective-permute-start | bytes 835592 | tf_op jit(solution)/shard_map/ppermute | solution.py:360
  38.3 3.0 %pack.2 = bf16[8,64,1024]{2,1,0:T(8,128)(2,1)} custom-call(s32[4]{0:T(128)} %pad_add_fusion.place_ref, bf16[2,64,8192]{2,1,0:T(8,128)(2,1)} %x_ref.3), custom_call_target="tpu_custom_call" | custom-call | tf_op jit(solution)/shard_map/pack/pallas_call | solution.py:339
  43.3 2.9 %collective-permute-done.1.refs_2_.refs_3_.refs_20_ = bf16[544,256]{1,0:T(8,128)(2,1)} collective-permute-done((bf16[544,256]{1,0:T(8,128)(2,1)}, bf16[544,256]{1,0:T(8,128)(2,1)}, u32[]{:S(2)}, u32[]{:S(2)}) %collective-permute-start.1) | collective-permute-done | bytes 278560 | tf_op jit(solution)/shard_map/ppermute | solution.py:360
  46.2 2.1 %collective-permute-done.2.refs_3_.refs_4_.refs_21_ = bf16[544,256]{1,0:T(8,128)(2,1)} collective-permute-done((bf16[544,256]{1,0:T(8,128)(2,1)}, bf16[544,256]{1,0:T(8,128)(2,1)}, u32[]{:S(2)}, u32[]{:S(2)}) %collective-permute-start.2) | collective-permute-done | bytes 278560 | tf_op jit(solution)/shard_map/ppermute | solution.py:360
  48.3 2.7 %all-to-all-done.got_ref.tail_ref = bf16[8,64,1664]{2,1,0:T(8,128)(2,1)} async-done(((bf16[8,64,1664]{2,1,0:T(8,128)(2,1)}), bf16[8,64,1664]{2,1,0:T(8,128)(2,1)}, u32[]{:S(2)}, u32[]{:S(2)}) %all-to-all-start) | async-done | bytes 1703968 | tf_op jit(solution)/shard_map/all_to_all | solution.py:294
  51.1 4.3 %all-to-all-start.2 = ((bf16[8,64,1024]{2,1,0:T(8,128)(2,1)}), bf16[8,64,1024]{2,1,0:T(8,128)(2,1)}, u32[]{:S(2)}, u32[]{:S(2)}) async-start(bf16[8,64,1024]{2,1,0:T(8,128)(2,1)} %pack.2), calls=%async_computation.2 | async-start | bytes 2097152 | tf_op jit(solution)/shard_map/all_to_all | solution.py:294
  55.4 15.3 %scan.2 = (f32[4096,128]{1,0:T(8,128)}, f32[4096,128]{1,0:T(8,128)}, f32[136,128]{1,0:T(8,128)}) custom-call(s32[4]{0:T(128)} %pad_add_fusion.place_ref, s32[8]{0:T(128)} %lengths_ref.7, bf16[8,64,1664]{2,1,0:T(8,128)(2,1)} %all-to-all-done.got_ref.tail_ref, bf16[512,256]{1,0:T(8,128)(2,1)} %bitcast.53, ...), custom_call_target="tpu_custom_call" | custom-call | bytes 54000000 | tf_op jit(solution)/shard_map/scan/pallas_call | solution.py:399
  70.8 15.6 %scan.3 = (bf16[352,128]{1,0:T(8,128)(2,1)}, f32[4096,128]{1,0:T(8,128)}, f32[4096,128]{1,0:T(8,128)}, f32[136,128]{1,0:T(8,128)}) custom-call(s32[4]{0:T(128)} %pad_add_fusion.place_ref, s32[8]{0:T(128)} %lengths_ref.7, bf16[8,64,1024]{2,1,0:T(8,128)(2,1)} %all-to-all-done.2.got_ref, bf16[8,64,1664]{2,1,0:T(8,128)(2,1)} %collective-permute-done.3.refs_0_.tail_ref, ...), custom_call_target="tpu_custom_call" | custom-call | bytes 54000000 | tf_op jit(solution)/shard_map/scan/pallas_call | solution.py:399
  86.4 1.9 %collective-permute-start.4 = (bf16[352,128]{1,0:T(8,128)(2,1)}, bf16[352,128]{1,0:T(8,128)(2,1)S(1)}, u32[]{:S(2)}, u32[]{:S(2)}) collective-permute-start(bf16[352,128]{1,0:T(8,128)(2,1)} %get-tuple-element.37.refs_4_), channel_id=1, source_target_pairs={{0,16},{16,32},{32,48},{48,0},{1,17},{17,33},{33,49},{49,1},{2,18}... | collective-permute-start | bytes 270344 | tf_op jit(solution)/shard_map/ppermute | solution.py:439
  88.3 2.5 %collective-permute-start.5 = (bf16[352,128]{1,0:T(8,128)(2,1)}, bf16[352,128]{1,0:T(8,128)(2,1)S(1)}, u32[]{:S(2)}, u32[]{:S(2)}) collective-permute-start(bf16[352,128]{1,0:T(8,128)(2,1)} %get-tuple-element.37.refs_4_), channel_id=1, source_target_pairs={{0,32},{16,48},{32,0},{48,16},{1,33},{17,49},{33,1},{49,17},{2,34}... | collective-permute-start | bytes 270344 | tf_op jit(solution)/shard_map/ppermute | solution.py:439
  90.8 2.2 %collective-permute-start.6 = (bf16[352,128]{1,0:T(8,128)(2,1)}, bf16[352,128]{1,0:T(8,128)(2,1)S(1)}, u32[]{:S(2)}, u32[]{:S(2)}) collective-permute-start(bf16[352,128]{1,0:T(8,128)(2,1)} %get-tuple-element.37.refs_4_), channel_id=1, source_target_pairs={{0,48},{16,0},{32,16},{48,32},{1,49},{17,1},{33,17},{49,33},{2,50}... | collective-permute-start | bytes 270344 | tf_op jit(solution)/shard_map/ppermute | solution.py:439
  93.9 4.9 %collective-permute-done.5.refs_6_ = bf16[352,128]{1,0:T(8,128)(2,1)S(1)} collective-permute-done((bf16[352,128]{1,0:T(8,128)(2,1)}, bf16[352,128]{1,0:T(8,128)(2,1)S(1)}, u32[]{:S(2)}, u32[]{:S(2)}) %collective-permute-start.5) | collective-permute-done | bytes 90144 | tf_op jit(solution)/shard_map/ppermute | solution.py:439
  98.8 1.8 %collective-permute-done.6.refs_7_ = bf16[352,128]{1,0:T(8,128)(2,1)S(1)} collective-permute-done((bf16[352,128]{1,0:T(8,128)(2,1)}, bf16[352,128]{1,0:T(8,128)(2,1)S(1)}, u32[]{:S(2)}, u32[]{:S(2)}) %collective-permute-start.6) | collective-permute-done | bytes 90144 | tf_op jit(solution)/shard_map/ppermute | solution.py:439
  101.2 11.1 %correct.2 = (bf16[8,64,1024]{2,1,0:T(8,128)(2,1)}, f32[128,128]{1,0:T(8,128)}, bf16[2,16,256]{2,1,0:T(8,128)(2,1)}) custom-call(s32[4]{0:T(128)} %pad_add_fusion.place_ref, s32[8]{0:T(128)} %lengths_ref.7, f32[4096,128]{1,0:T(8,128)} %get-tuple-element.35.y_ref, f32[4096,128]{1,0:T(8,128)} %get-tuple-element.36.total_ref, ...), custom_call_target="tpu_custom_call" | custom-call | bytes 32400000 | tf_op jit(solution)/shard_map/correct/pallas_call | solution.py:443
  112.4 6.1 %all-to-all-start.4 = ((bf16[8,64,1024]{2,1,0:T(8,128)(2,1)}), bf16[8,64,1024]{2,1,0:T(8,128)(2,1)}, u32[]{:S(2)}, u32[]{:S(2)}) async-start(bf16[8,64,1024]{2,1,0:T(8,128)(2,1)} %get-tuple-element.41), calls=%async_computation.4 | async-start | bytes 2097152 | tf_op jit(solution)/shard_map/all_to_all | solution.py:294
  118.5 10.7 %correct.3 = bf16[8,64,1024]{2,1,0:T(8,128)(2,1)} custom-call(s32[4]{0:T(128)} %pad_add_fusion.place_ref, s32[8]{0:T(128)} %lengths_ref.7, f32[4096,128]{1,0:T(8,128)} %get-tuple-element.33.y_ref, f32[4096,128]{1,0:T(8,128)} %get-tuple-element.34.total_ref, bf16[8,64,1664]{2,1,0:T(8,128)(2,1)} %collective-permute-done.3.refs_0_.tail_ref, ...), custom_call_target="tpu_custom_call" | custom-call | bytes 32400000 | tf_op jit(solution)/shard_map/correct/pallas_call | solution.py:443
  129.2 3.9 %all-to-all-done.4.back_ref = bf16[8,64,1024]{2,1,0:T(8,128)(2,1)} async-done(((bf16[8,64,1024]{2,1,0:T(8,128)(2,1)}), bf16[8,64,1024]{2,1,0:T(8,128)(2,1)}, u32[]{:S(2)}, u32[]{:S(2)}) %all-to-all-start.4) | async-done | bytes 1048608 | tf_op jit(solution)/shard_map/all_to_all | solution.py:294
  133.1 3.6 %all-to-all-start.3 = ((bf16[8,64,1024]{2,1,0:T(8,128)(2,1)}), bf16[8,64,1024]{2,1,0:T(8,128)(2,1)S(1)}, u32[]{:S(2)}, u32[]{:S(2)}) async-start(bf16[8,64,1024]{2,1,0:T(8,128)(2,1)} %correct.3), calls=%async_computation.3 | async-start | bytes 2097152 | tf_op jit(solution)/shard_map/all_to_all | solution.py:294
  136.7 2.9 %unpack.2.refs_0_ = bf16[2,64,8192]{2,1,0:T(8,128)(2,1)} custom-call(s32[4]{0:T(128)S(1)} %copy-done.1, bf16[8,64,1024]{2,1,0:T(8,128)(2,1)} %all-to-all-done.4.back_ref), custom_call_target="tpu_custom_call" | custom-call | tf_op jit(solution)/shard_map/unpack/pallas_call | solution.py:491
  139.6 1.6 %collective-permute-start.7 = (bf16[2,16,256]{2,1,0:T(8,128)(2,1)S(1)}, bf16[2,16,256]{2,1,0:T(8,128)(2,1)S(1)}, u32[]{:S(2)}, u32[]{:S(2)}) collective-permute-start(bf16[2,16,256]{2,1,0:T(8,128)(2,1)S(1)} %copy-done.9), channel_id=1, source_target_pairs={{0,64},{64,128},{128,192},{192,0},{1,65},{65,129},{129,193},{193,1... | collective-permute-start | bytes 49160 | tf_op jit(solution)/shard_map/ppermute | solution.py:509
  142.1 2.4 %collective-permute-start.9 = (bf16[2,16,256]{2,1,0:T(8,128)(2,1)S(1)}, bf16[2,16,256]{2,1,0:T(8,128)(2,1)S(1)}, u32[]{:S(2)}, u32[]{:S(2)}) collective-permute-start(bf16[2,16,256]{2,1,0:T(8,128)(2,1)S(1)} %copy-done.9), channel_id=1, source_target_pairs={{0,192},{64,0},{128,64},{192,128},{1,193},{65,1},{129,65},{193,129... | collective-permute-start | bytes 49160 | tf_op jit(solution)/shard_map/ppermute | solution.py:509
  144.6 1.9 %collective-permute-done.8 = bf16[2,16,256]{2,1,0:T(8,128)(2,1)S(1)} collective-permute-done((bf16[2,16,256]{2,1,0:T(8,128)(2,1)S(1)}, bf16[2,16,256]{2,1,0:T(8,128)(2,1)S(1)}, u32[]{:S(2)}, u32[]{:S(2)}) %collective-permute-start.8) | collective-permute-done | bytes 16416 | tf_op jit(solution)/shard_map/ppermute | solution.py:509
  147.7 4.0 %all-to-all-done.3.back_ref = bf16[8,64,1024]{2,1,0:T(8,128)(2,1)S(1)} async-done(((bf16[8,64,1024]{2,1,0:T(8,128)(2,1)}), bf16[8,64,1024]{2,1,0:T(8,128)(2,1)S(1)}, u32[]{:S(2)}, u32[]{:S(2)}) %all-to-all-start.3) | async-done | bytes 1048608 | tf_op jit(solution)/shard_map/all_to_all | solution.py:294
  151.7 1.6 %unpack.3 = bf16[2,64,8192]{2,1,0:T(8,128)(2,1)} custom-call(s32[4]{0:T(128)S(1)} %copy-done.1, bf16[8,64,1024]{2,1,0:T(8,128)(2,1)S(1)} %all-to-all-done.3.back_ref, bf16[2,64,8192]{2,1,0:T(8,128)(2,1)} %unpack.2.refs_0_), custom_call_target="tpu_custom_call", output_to_operand_aliasing={{}: (2, {})} | custom-call | tf_op jit(solution)/shard_map/unpack/pallas_call | solution.py:491
  (61 shorter events, 11.7 us)
Async XLA Ops:
  0.6 13.8 %copy-start = (bf16[2,64,512]{2,1,0:T(8,128)(2,1)S(1)}, bf16[2,64,512]{2,1,0:T(8,128)(2,1)}, u32[]{:S(2)}) copy-start(bf16[2,64,512]{2,1,0:T(8,128)(2,1)} %param.13) | copy-start | bytes 393220
  0.6 15.1 %copy-start.2 = (s32[8,1]{0,1:T(1,128)S(1)}, s32[8,1]{0,1:T(1,128)}, u32[]{:S(2)}) copy-start(s32[8,1]{0,1:T(1,128)} %param.20) | copy-start | bytes 100
  0.7 15.1 %copy-start.10 = (s32[8]{0:T(128)S(1)}, s32[8]{0:T(128)}, u32[]{:S(2)}) copy-start(s32[8]{0:T(128)} %param.21) | copy-start | bytes 100
  2.4 24.0 %all-to-all-start.1 = ((bf16[32,16,256]{2,1,0:T(8,128)(2,1)}), bf16[32,16,256]{2,1,0:T(8,128)(2,1)S(1)}, u32[]{:S(2)}, u32[]{:S(2)}) async-start(bf16[32,16,256]{2,1,0:T(8,128)(2,1)} %spread.1), calls=%async_computation.1 | async-start | bytes 524288 | tf_op jit(solution)/shard_map/all_to_all | solution.py:294
  21.4 10.4 %copy-start.5 = (bf16[1,8,16,256]{3,2,1,0:T(8,128)(2,1)S(1)}, bf16[1,8,16,256]{3,2,1,0:T(8,128)(2,1)}, u32[]{:S(2)}) copy-start(bf16[1,8,16,256]{3,2,1,0:T(8,128)(2,1)} %copy.22) | copy-start | bytes 196612
  26.4 7.0 %copy-start.4 = (bf16[32,16,256]{2,1,0:T(8,128)(2,1)}, bf16[32,16,256]{2,1,0:T(8,128)(2,1)S(1)}, u32[]{:S(2)}) copy-start(bf16[32,16,256]{2,1,0:T(8,128)(2,1)S(1)} %all-to-all-done.1) | copy-start | bytes 786436
  26.4 24.6 %all-to-all-start = ((bf16[8,64,1664]{2,1,0:T(8,128)(2,1)}), bf16[8,64,1664]{2,1,0:T(8,128)(2,1)}, u32[]{:S(2)}, u32[]{:S(2)}) async-start(bf16[8,64,1664]{2,1,0:T(8,128)(2,1)} %pack.3), calls=%async_computation | async-start | bytes 3407872 | tf_op jit(solution)/shard_map/all_to_all | solution.py:294
  32.4 8.9 %copy-start.3 = (s32[1,64]{1,0:T(1,128)S(1)}, s32[1,64]{1,0:T(1,128)}, u32[]{:S(2)}) copy-start(s32[1,64]{1,0:T(1,128)} %param.22) | copy-start | bytes 772
  33.4 9.9 %collective-permute-start = (bf16[544,256]{1,0:T(8,128)(2,1)}, bf16[544,256]{1,0:T(8,128)(2,1)}, u32[]{:S(2)}, u32[]{:S(2)}) collective-permute-start(bf16[544,256]{1,0:T(8,128)(2,1)} %get-tuple-element.54), channel_id=1, source_target_pairs={{0,64},{64,128},{128,192},{192,0},{1,65},{65,129},{129,193},{193,1... | collective-permute-start | bytes 835592 | tf_op jit(solution)/shard_map/ppermute | solution.py:360
  35.0 11.2 %collective-permute-start.1 = (bf16[544,256]{1,0:T(8,128)(2,1)}, bf16[544,256]{1,0:T(8,128)(2,1)}, u32[]{:S(2)}, u32[]{:S(2)}) collective-permute-start(bf16[544,256]{1,0:T(8,128)(2,1)} %get-tuple-element.53), channel_id=1, source_target_pairs={{0,128},{64,192},{128,0},{192,64},{1,129},{65,193},{129,1},{193,65... | collective-permute-start | bytes 835592 | tf_op jit(solution)/shard_map/ppermute | solution.py:360
  35.9 12.4 %collective-permute-start.2 = (bf16[544,256]{1,0:T(8,128)(2,1)}, bf16[544,256]{1,0:T(8,128)(2,1)}, u32[]{:S(2)}, u32[]{:S(2)}) collective-permute-start(bf16[544,256]{1,0:T(8,128)(2,1)} %get-tuple-element.52), channel_id=1, source_target_pairs={{0,192},{64,0},{128,64},{192,128},{1,193},{65,1},{129,65},{193,129... | collective-permute-start | bytes 835592 | tf_op jit(solution)/shard_map/ppermute | solution.py:360
  51.1 19.7 %all-to-all-start.2 = ((bf16[8,64,1024]{2,1,0:T(8,128)(2,1)}), bf16[8,64,1024]{2,1,0:T(8,128)(2,1)}, u32[]{:S(2)}, u32[]{:S(2)}) async-start(bf16[8,64,1024]{2,1,0:T(8,128)(2,1)} %pack.2), calls=%async_computation.2 | async-start | bytes 2097152 | tf_op jit(solution)/shard_map/all_to_all | solution.py:294
  55.3 15.4 %collective-permute-start.3 = (bf16[8,64,1664]{2,1,0:T(8,128)(2,1)}, bf16[8,64,1664]{2,1,0:T(8,128)(2,1)}, u32[]{:S(2)}, u32[]{:S(2)}) collective-permute-start(bf16[8,64,1664]{2,1,0:T(8,128)(2,1)} %all-to-all-done.got_ref.tail_ref), channel_id=1, source_target_pairs={{0,1},{1,0},{2,3},{3,2},{4,5},{5,4},{6,7},{7,6},{8,9},{9,8},{10,11... | collective-permute-start | bytes 5111816 | tf_op jit(solution)/shard_map/ppermute | solution.py:373
  86.4 7.5 %collective-permute-start.4 = (bf16[352,128]{1,0:T(8,128)(2,1)}, bf16[352,128]{1,0:T(8,128)(2,1)S(1)}, u32[]{:S(2)}, u32[]{:S(2)}) collective-permute-start(bf16[352,128]{1,0:T(8,128)(2,1)} %get-tuple-element.37.refs_4_), channel_id=1, source_target_pairs={{0,16},{16,32},{32,48},{48,0},{1,17},{17,33},{33,49},{49,1},{2,18}... | collective-permute-start | bytes 270344 | tf_op jit(solution)/shard_map/ppermute | solution.py:439
  88.3 10.5 %collective-permute-start.5 = (bf16[352,128]{1,0:T(8,128)(2,1)}, bf16[352,128]{1,0:T(8,128)(2,1)S(1)}, u32[]{:S(2)}, u32[]{:S(2)}) collective-permute-start(bf16[352,128]{1,0:T(8,128)(2,1)} %get-tuple-element.37.refs_4_), channel_id=1, source_target_pairs={{0,32},{16,48},{32,0},{48,16},{1,33},{17,49},{33,1},{49,17},{2,34}... | collective-permute-start | bytes 270344 | tf_op jit(solution)/shard_map/ppermute | solution.py:439
  90.8 9.8 %collective-permute-start.6 = (bf16[352,128]{1,0:T(8,128)(2,1)}, bf16[352,128]{1,0:T(8,128)(2,1)S(1)}, u32[]{:S(2)}, u32[]{:S(2)}) collective-permute-start(bf16[352,128]{1,0:T(8,128)(2,1)} %get-tuple-element.37.refs_4_), channel_id=1, source_target_pairs={{0,48},{16,0},{32,16},{48,32},{1,49},{17,1},{33,17},{49,33},{2,50}... | collective-permute-start | bytes 270344 | tf_op jit(solution)/shard_map/ppermute | solution.py:439
  93.9 6.8 %copy-start.6 = (bf16[352,128]{1,0:T(8,128)(2,1)}, bf16[352,128]{1,0:T(8,128)(2,1)S(1)}, u32[]{:S(2)}) copy-start(bf16[352,128]{1,0:T(8,128)(2,1)S(1)} %collective-permute-done.4.refs_5_) | copy-start | bytes 270340
  98.8 1.8 %copy-start.7 = (bf16[352,128]{1,0:T(8,128)(2,1)}, bf16[352,128]{1,0:T(8,128)(2,1)S(1)}, u32[]{:S(2)}) copy-start(bf16[352,128]{1,0:T(8,128)(2,1)S(1)} %collective-permute-done.5.refs_6_) | copy-start | bytes 270340
  100.6 0.6 copy-start.8
  112.4 20.7 %all-to-all-start.4 = ((bf16[8,64,1024]{2,1,0:T(8,128)(2,1)}), bf16[8,64,1024]{2,1,0:T(8,128)(2,1)}, u32[]{:S(2)}, u32[]{:S(2)}) async-start(bf16[8,64,1024]{2,1,0:T(8,128)(2,1)} %get-tuple-element.41), calls=%async_computation.4 | async-start | bytes 2097152 | tf_op jit(solution)/shard_map/all_to_all | solution.py:294
  129.2 7.5 %copy-start.1 = (s32[4]{0:T(128)S(1)}, s32[4]{0:T(128)}, u32[]{:S(2)}) copy-start(s32[4]{0:T(128)} %pad_add_fusion.place_ref) | copy-start | bytes 52
  133.1 18.6 %all-to-all-start.3 = ((bf16[8,64,1024]{2,1,0:T(8,128)(2,1)}), bf16[8,64,1024]{2,1,0:T(8,128)(2,1)S(1)}, u32[]{:S(2)}, u32[]{:S(2)}) async-start(bf16[8,64,1024]{2,1,0:T(8,128)(2,1)} %correct.3), calls=%async_computation.3 | async-start | bytes 2097152 | tf_op jit(solution)/shard_map/all_to_all | solution.py:294
  136.7 2.9 %copy-start.9 = (bf16[2,16,256]{2,1,0:T(8,128)(2,1)S(1)}, bf16[2,16,256]{2,1,0:T(8,128)(2,1)}, u32[]{:S(2)}) copy-start(bf16[2,16,256]{2,1,0:T(8,128)(2,1)} %get-tuple-element.42) | copy-start | bytes 49156
  139.6 5.0 %collective-permute-start.7 = (bf16[2,16,256]{2,1,0:T(8,128)(2,1)S(1)}, bf16[2,16,256]{2,1,0:T(8,128)(2,1)S(1)}, u32[]{:S(2)}, u32[]{:S(2)}) collective-permute-start(bf16[2,16,256]{2,1,0:T(8,128)(2,1)S(1)} %copy-done.9), channel_id=1, source_target_pairs={{0,64},{64,128},{128,192},{192,0},{1,65},{65,129},{129,193},{193,1... | collective-permute-start | bytes 49160 | tf_op jit(solution)/shard_map/ppermute | solution.py:509
  141.2 5.2 %collective-permute-start.8 = (bf16[2,16,256]{2,1,0:T(8,128)(2,1)S(1)}, bf16[2,16,256]{2,1,0:T(8,128)(2,1)S(1)}, u32[]{:S(2)}, u32[]{:S(2)}) collective-permute-start(bf16[2,16,256]{2,1,0:T(8,128)(2,1)S(1)} %copy-done.9), channel_id=1, source_target_pairs={{0,128},{64,192},{128,0},{192,64},{1,129},{65,193},{129,1},{193,65... | collective-permute-start | bytes 49160 | tf_op jit(solution)/shard_map/ppermute | solution.py:509
  142.1 4.3 %collective-permute-start.9 = (bf16[2,16,256]{2,1,0:T(8,128)(2,1)S(1)}, bf16[2,16,256]{2,1,0:T(8,128)(2,1)S(1)}, u32[]{:S(2)}, u32[]{:S(2)}) collective-permute-start(bf16[2,16,256]{2,1,0:T(8,128)(2,1)S(1)} %copy-done.9), channel_id=1, source_target_pairs={{0,192},{64,0},{128,64},{192,128},{1,193},{65,1},{129,65},{193,129... | collective-permute-start | bytes 49160 | tf_op jit(solution)/shard_map/ppermute | solution.py:509

commit v7 on v6

--- a/solution.py
+++ b/solution.py
@@ -178,9 +178,8 @@
     return jnp.concatenate(blocks, axis=0).astype(jnp.bfloat16)
 
 
-def join(place_ref, sent_refs, decay_scr, carry_refs, final_ref, state_scr):
+def join(place_ref, reqs, turn, sent_refs, decay_scr, carry_scr, final_ref, state_scr):
     states = decay_scr.shape[0] // ROWS
-    reqs = len(carry_refs)
     hi = place_ref[0]
     per_req = (states + 2) * ROWS
     blocks = [ref[...].astype(jnp.float32) for ref in sent_refs]
@@ -192,7 +191,7 @@
             value = jnp.where(distance == by, values[by], value)
         return value
 
-    for req in range(reqs):
+    for req in range(reqs) if final_ref is not None else [turn]:
         ends = [block[req * per_req : (req + 1) * per_req] for block in blocks]
         totals = [end[states * ROWS : (states + 1) * ROWS] + end[(states + 1) * ROWS :] for end in ends]
         in_order = [of_shard(shard, totals) for shard in range(HI)]
@@ -205,27 +204,32 @@
             rows = slice(n * ROWS, (n + 1) * ROWS)
             decay = decay_scr[rows, :]
             carry = final = state_scr[rows, :]
-            for by in range(HI - 1, 0, -1):
-                longer = ends[by][rows] + jnp.exp2(totals[by] * decay) * carry
-                carry = jnp.where(hi >= by, longer, carry)
-            carry_refs[req][rows, :] = carry
+            if req == turn:
+                for by in range(HI - 1, 0, -1):
+                    longer = ends[by][rows] + jnp.exp2(totals[by] * decay) * carry
+                    carry = jnp.where(hi >= by, longer, carry)
+                carry_scr[rows, :] = carry
+            if final_ref is None:
+                continue
             for shard in range(HI):
                 end = of_shard(shard, [end[rows] for end in ends])
                 final = end + jnp.exp2(in_order[shard] * decay) * final
             state_scr[rows, :] = final
-        for j in range(2):
+        for j in range(2 if final_ref is not None else 0):
             value = state_scr[pl.ds(2 * hi + j, states, stride=ROWS), :]
             final_ref[req, :, j * LANES : (j + 1) * LANES] = value.astype(jnp.bfloat16)
+
+
+def columns_kernel(states, tail_ref, out_ref):
+    rows = tail_ref.shape[0] * tail_ref.shape[1]
+    replicate(tail_ref[...].reshape(rows, LANES), states, states, out_ref, 0, rows, rows)
 
 
 def correct_kernel(turn, reqs, place_ref, lengths_ref, y_ref, total_ref, tail_ref, *refs):
     decay_refs, refs = refs[:HI], refs[HI:]
     y_scr, c_scr, decay_scr, carry_scr, state_scr = refs[-5:]
-    if turn == 0:
-        sent_refs, refs = refs[:HI], refs[HI:]
-        out_ref, carry_refs, final_ref = refs[0], refs[1:reqs], refs[reqs]
-    else:
-        carry_ref, out_ref = refs[:2]
+    sent_refs, out_ref = refs[:HI], refs[HI]
+    final_ref = refs[HI + 1] if turn == reqs - 1 else None
     parts, toks, _ = out_ref.shape
     states = decay_refs[0].shape[0]
     rows = parts * toks
@@ -235,13 +239,12 @@
     def _():
         to_rows(decay_scr, decay_refs, states)
         decay_scr[...] = decay_scr[...] * (-LOG2E)
-        if turn == 0:
-            carries = (carry_scr, *carry_refs)
-            join(place_ref, sent_refs, decay_scr, carries, final_ref, state_scr)
-        else:
-            carry_scr[...] = carry_ref[...]
-
-    replicate(tail_ref[...].reshape(rows, LANES), states, states, c_scr, 0, rows, rows)
+        join(place_ref, reqs, turn, sent_refs, decay_scr, carry_scr, final_ref, state_scr)
+
+    if turn == 0:
+        c_scr = tail_ref
+    else:
+        replicate(tail_ref[...].reshape(rows, LANES), states, states, c_scr, 0, rows, rows)
     carry = tuple(carry_scr[n * ROWS : (n + 1) * ROWS, :] for n in range(states))
 
     def per_tok(tok, carry):
@@ -436,9 +439,22 @@
         total.append(one_total)
         end.append(one_end)
 
+    carry_rows = states * ROWS
+    late_got, leaving = lax.optimization_barrier((first_got, leaving))
     arrived = [lax.ppermute(leaving, "hi", shifts(HI, by)) for by in range(1, HI)]
-    carry_rows = states * ROWS
-    back, carry = [], None
+    tail_spec = pl.BlockSpec((parts, toks, LANES), lambda i, *at: (i, 0, (chans + rank) // LANES))
+    columns_spec = pl.BlockSpec((states * rows, LANES), lambda i, *at: (i, 0))
+    columns = pl.pallas_call(
+        functools.partial(columns_kernel, states),
+        grid=(steps,),
+        in_specs=[tail_spec],
+        out_specs=columns_spec,
+        out_shape=jax.ShapeDtypeStruct((steps * states * rows, LANES), jnp.float32),
+        compiler_params=params(63),
+        cost_estimate=cost(4),
+        name="columns",
+    )(late_got)
+    back = []
     for req in range(reqs):
         out, *more = pl.pallas_call(
             functools.partial(correct_kernel, req, reqs),
@@ -448,43 +464,26 @@
                 in_specs=[
                     rows_spec,
                     rows_spec,
-                    pl.BlockSpec(
-                        (parts, toks, LANES), lambda i, *at: (i, 0, (chans + rank) // LANES)
-                    ),
+                    tail_spec if req else columns_spec,
                 ]
                 + own(states)
-                + (
-                    [whole(carry_rows, LANES)]
-                    if req
-                    else [whole(leave_rows, LANES)] * HI
-                ),
+                + [whole(leave_rows, LANES)] * HI,
                 out_specs=[pl.BlockSpec((parts, toks, chans), lambda i, *at: (i, 0, 0))]
-                + (
-                    []
-                    if req
-                    else [whole(carry_rows, LANES)] * (reqs - 1)
-                    + [whole(reqs, states, piece)]
-                ),
+                + [whole(reqs, states, piece)] * (req == reqs - 1),
                 scratch_shapes=scratch(
                     rows * ROWS, states * rows, carry_rows, carry_rows, carry_rows
                 ),
             ),
             out_shape=[jax.ShapeDtypeStruct((LO, toks, chans), jnp.bfloat16)]
-            + (
-                []
-                if req
-                else [jax.ShapeDtypeStruct((carry_rows, LANES), jnp.float32)] * (reqs - 1)
-                + [jax.ShapeDtypeStruct((reqs, states, piece), jnp.bfloat16)]
-            ),
+            + [jax.ShapeDtypeStruct((reqs, states, piece), jnp.bfloat16)] * (req == reqs - 1),
             compiler_params=params(63),
             cost_estimate=cost(9),
             name="correct",
         )(
-            place, new_lengths, y[req], total[req], second_share if req else first_got,
-            *[decay_rate] * HI, *([carry[req - 1]] if req else [leaving, *arrived]),
+            place, new_lengths, y[req], total[req], second_share if req else columns,
+            *[decay_rate] * HI, leaving, *arrived,
         )
-        if req == 0:
-            carry, held = more[: reqs - 1], more[reqs - 1]
+        held = more[0] if more else None
         back.append(exchange(out, "lo"))
 
     def unpack(turn, mixed):
@@ -492,10 +491,12 @@
             unpack_kernel,
             grid_spec=pltpu.PrefetchScalarGridSpec(
                 num_scalar_prefetch=1,
-                grid=(1,),
-                in_specs=[whole(LO, toks, chans)]
+                grid=(2,),
+                in_specs=[pl.BlockSpec((LO, toks // 2, chans), lambda i, at: (0, i, 0))]
                 + [pl.BlockSpec(memory_space=pl.ANY)] * len(mixed),
-                out_specs=pl.BlockSpec((1, toks, width), of_turn(turn)),
+                out_specs=pl.BlockSpec(
+                    (1, toks // 2, width), lambda i, at: (lax.rem(at[3] + turn, 2), i, 0)
+                ),
             ),
             out_shape=jax.ShapeDtypeStruct(conv_out.shape, jnp.bfloat16),
             input_output_aliases={2: 0} if mixed else {},

time: 155 us -> 154 us (level)
  waiting for transfers between devices: 30.8 us -> 27.5 us
  Pallas kernels: 65.3 us -> 68.2 us
    pallas_call x0 -> x1, Pallas kernels: none -> 3.29 us  [on_device(): pl.pallas_call(functools.partial(columns_kernel, states), grid=(steps,),...]
    ppermute x3, waiting for transfers between devices: 7.67 us -> 4.41 us  [on_device(): lax.ppermute(leaving, 'hi', shifts(HI, by))]
  transfers between devices with their start and end apart: 15 -> 15, of which waited for: 11 -> 11; matrix products, arithmetic and copies ran while one was open for 6% -> 6% of each run, Pallas kernels for 23% -> 25%
where the time goes in v7:
time: 154 us; the launch traced here: 153 us
  Pallas kernels  68.2 us (44%)
  starting transfers between devices  46 us (30%)
  waiting for transfers between devices  27.5 us (18%)
  local copies, waits for them, and re-layouts  6.98 us (5%)
  other arithmetic  2.77 us (2%)
    pallas_call x2, Pallas kernels, on_device(): pl.pallas_call(functools.partial(scan_kernel, req), grid_spec=pltpu.Prefe...  31.1 us
    all_to_all x5, starting transfers between devices, exchange(): return lax.all_to_all(array, axis, split_axis=0, concat_axis=0, tiled=True)  29.6 us
    pallas_call x2, Pallas kernels, on_device(): pl.pallas_call(functools.partial(correct_kernel, req, reqs), grid_spec=pl...  21.6 us
    all_to_all x5, waiting for transfers between devices, exchange(): return lax.all_to_all(array, axis, split_axis=0, concat_axis=0, tiled=True)  15.6 us
    ppermute x3, starting transfers between devices, on_device(): lax.ppermute(leaving, 'hi', shifts(HI, by))  6.54 us
    pallas_call x2, Pallas kernels, on_device(): pl.pallas_call(pack_kernel, grid_spec=pltpu.PrefetchScalarGridSpec(num_sc...  6.23 us
    ppermute x3, waiting for transfers between devices, on_device(): lax.ppermute(jnp.concatenate([quarter, wanted_by(lax.rem(group + by, grou...  5.64 us
    ppermute x3, starting transfers between devices, on_device(): lax.ppermute(jnp.concatenate([quarter, wanted_by(lax.rem(group + by, grou...  4.93 us
  transfers between devices with their start and end apart: 15, of which 11 were waited for; matrix products, arithmetic and copies ran while one was open for 6% of the time, Pallas kernels for 25%

profile of v7, /device:TPU:8, one launch (start us, length us, event | category | flops | bytes accessed | tf_op | source)
XLA Modules:
  0.0 152.9 jit_solution(5307142392781156107)
XLA Ops:
  0.7 1.7 %spread.1 = bf16[32,16,256]{2,1,0:T(8,128)(2,1)} custom-call(bf16[16,8192]{1,0:T(8,128)(2,1)} %w_ref.1), custom_call_target="tpu_custom_call" | custom-call | tf_op jit(solution)/shard_map/spread/pallas_call | solution.py:300
  2.4 11.3 %all-to-all-start.1 = ((bf16[32,16,256]{2,1,0:T(8,128)(2,1)}), bf16[32,16,256]{2,1,0:T(8,128)(2,1)S(1)}, u32[]{:S(2)}, u32[]{:S(2)}) async-start(bf16[32,16,256]{2,1,0:T(8,128)(2,1)} %spread.1), calls=%async_computation.1 | async-start | bytes 524288 | tf_op jit(solution)/shard_map/all_to_all | solution.py:297
  14.5 1.2 copy.21
  18.2 3.3 %pack.3 = bf16[8,64,1664]{2,1,0:T(8,128)(2,1)} custom-call(s32[4]{0:T(128)} %pad_add_fusion.place_ref, bf16[2,64,8192]{2,1,0:T(8,128)(2,1)} %x_ref.3, bf16[64,640]{1,0:T(8,128)(2,1)} %maximum_maximum_fusion.refs_0_), custom_call_target="tpu_custom_call" | custom-call | tf_op jit(solution)/shard_map/pack/pallas_call | solution.py:342
  21.4 5.0 %all-to-all-done.1 = bf16[32,16,256]{2,1,0:T(8,128)(2,1)S(1)} async-done(((bf16[32,16,256]{2,1,0:T(8,128)(2,1)}), bf16[32,16,256]{2,1,0:T(8,128)(2,1)S(1)}, u32[]{:S(2)}, u32[]{:S(2)}) %all-to-all-start.1) | async-done | bytes 262176 | tf_op jit(solution)/shard_map/all_to_all | solution.py:297
  26.4 4.3 %all-to-all-start = ((bf16[8,64,1664]{2,1,0:T(8,128)(2,1)}), bf16[8,64,1664]{2,1,0:T(8,128)(2,1)}, u32[]{:S(2)}, u32[]{:S(2)}) async-start(bf16[8,64,1664]{2,1,0:T(8,128)(2,1)} %pack.3), calls=%async_computation | async-start | bytes 3407872 | tf_op jit(solution)/shard_map/all_to_all | solution.py:297
  33.4 1.6 %collective-permute-start = (bf16[544,256]{1,0:T(8,128)(2,1)}, bf16[544,256]{1,0:T(8,128)(2,1)}, u32[]{:S(2)}, u32[]{:S(2)}) collective-permute-start(bf16[544,256]{1,0:T(8,128)(2,1)} %get-tuple-element.56), channel_id=1, source_target_pairs={{0,64},{64,128},{128,192},{192,0},{1,65},{65,129},{129,193},{193,1... | collective-permute-start | bytes 835592 | tf_op jit(solution)/shard_map/ppermute | solution.py:363
  34.9 0.9 collective-permute-start.1
  35.9 2.4 %collective-permute-start.2 = (bf16[544,256]{1,0:T(8,128)(2,1)}, bf16[544,256]{1,0:T(8,128)(2,1)}, u32[]{:S(2)}, u32[]{:S(2)}) collective-permute-start(bf16[544,256]{1,0:T(8,128)(2,1)} %get-tuple-element.54), channel_id=1, source_target_pairs={{0,192},{64,0},{128,64},{192,128},{1,193},{65,1},{129,65},{193,129... | collective-permute-start | bytes 835592 | tf_op jit(solution)/shard_map/ppermute | solution.py:363
  38.3 3.0 %pack.2 = bf16[8,64,1024]{2,1,0:T(8,128)(2,1)} custom-call(s32[4]{0:T(128)} %pad_add_fusion.place_ref, bf16[2,64,8192]{2,1,0:T(8,128)(2,1)} %x_ref.3), custom_call_target="tpu_custom_call" | custom-call | tf_op jit(solution)/shard_map/pack/pallas_call | solution.py:342
  43.3 2.9 %collective-permute-done.1.refs_2_.refs_3_.refs_20_ = bf16[544,256]{1,0:T(8,128)(2,1)} collective-permute-done((bf16[544,256]{1,0:T(8,128)(2,1)}, bf16[544,256]{1,0:T(8,128)(2,1)}, u32[]{:S(2)}, u32[]{:S(2)}) %collective-permute-start.1) | collective-permute-done | bytes 278560 | tf_op jit(solution)/shard_map/ppermute | solution.py:363
  46.2 2.1 %collective-permute-done.2.refs_3_.refs_4_.refs_21_ = bf16[544,256]{1,0:T(8,128)(2,1)} collective-permute-done((bf16[544,256]{1,0:T(8,128)(2,1)}, bf16[544,256]{1,0:T(8,128)(2,1)}, u32[]{:S(2)}, u32[]{:S(2)}) %collective-permute-start.2) | collective-permute-done | bytes 278560 | tf_op jit(solution)/shard_map/ppermute | solution.py:363
  48.3 2.8 %all-to-all-done.got_ref.tail_ref = bf16[8,64,1664]{2,1,0:T(8,128)(2,1)} async-done(((bf16[8,64,1664]{2,1,0:T(8,128)(2,1)}), bf16[8,64,1664]{2,1,0:T(8,128)(2,1)}, u32[]{:S(2)}, u32[]{:S(2)}) %all-to-all-start) | async-done | bytes 1703968 | tf_op jit(solution)/shard_map/all_to_all | solution.py:297
  51.0 4.2 %all-to-all-start.2 = ((bf16[8,64,1024]{2,1,0:T(8,128)(2,1)}), bf16[8,64,1024]{2,1,0:T(8,128)(2,1)}, u32[]{:S(2)}, u32[]{:S(2)}) async-start(bf16[8,64,1024]{2,1,0:T(8,128)(2,1)} %pack.2), calls=%async_computation.2 | async-start | bytes 2097152 | tf_op jit(solution)/shard_map/all_to_all | solution.py:297
  55.4 15.4 %scan.2 = (f32[4096,128]{1,0:T(8,128)}, f32[4096,128]{1,0:T(8,128)}, f32[136,128]{1,0:T(8,128)}) custom-call(s32[4]{0:T(128)} %pad_add_fusion.place_ref, s32[8]{0:T(128)} %lengths_ref.7, bf16[8,64,1664]{2,1,0:T(8,128)(2,1)} %all-to-all-done.got_ref.tail_ref, bf16[512,256]{1,0:T(8,128)(2,1)} %bitcast.53, ...), custom_call_target="tpu_custom_call" | custom-call | bytes 54000000 | tf_op jit(solution)/shard_map/scan/pallas_call | solution.py:402
  70.8 15.7 %scan.3 = (bf16[352,128]{1,0:T(8,128)(2,1)}, f32[4096,128]{1,0:T(8,128)}, f32[4096,128]{1,0:T(8,128)}, f32[136,128]{1,0:T(8,128)}) custom-call(s32[4]{0:T(128)} %pad_add_fusion.place_ref, s32[8]{0:T(128)} %lengths_ref.7, bf16[8,64,1024]{2,1,0:T(8,128)(2,1)} %all-to-all-done.2.got_ref, bf16[8,64,1664]{2,1,0:T(8,128)(2,1)} %collective-permute-done.3.refs_0_.tail_ref, ...), custom_call_target="tpu_custom_call" | custom-call | bytes 54000000 | tf_op jit(solution)/shard_map/scan/pallas_call | solution.py:402
  86.5 1.9 %collective-permute-start.4 = (bf16[352,128]{1,0:T(8,128)(2,1)}, bf16[352,128]{1,0:T(8,128)(2,1)S(1)}, u32[]{:S(2)}, u32[]{:S(2)}) collective-permute-start(bf16[352,128]{1,0:T(8,128)(2,1)} %get-tuple-element.37.refs_4_), channel_id=1, source_target_pairs={{0,16},{16,32},{32,48},{48,0},{1,17},{17,33},{33,49},{49,1},{2,18}... | collective-permute-start | bytes 270344 | tf_op jit(solution)/shard_map/ppermute | solution.py:444
  88.4 2.5 %collective-permute-start.5 = (bf16[352,128]{1,0:T(8,128)(2,1)}, bf16[352,128]{1,0:T(8,128)(2,1)S(1)}, u32[]{:S(2)}, u32[]{:S(2)}) collective-permute-start(bf16[352,128]{1,0:T(8,128)(2,1)} %get-tuple-element.37.refs_4_), channel_id=1, source_target_pairs={{0,32},{16,48},{32,0},{48,16},{1,33},{17,49},{33,1},{49,17},{2,34}... | collective-permute-start | bytes 270344 | tf_op jit(solution)/shard_map/ppermute | solution.py:444
  90.8 2.2 %collective-permute-start.6 = (bf16[352,128]{1,0:T(8,128)(2,1)}, bf16[352,128]{1,0:T(8,128)(2,1)S(1)}, u32[]{:S(2)}, u32[]{:S(2)}) collective-permute-start(bf16[352,128]{1,0:T(8,128)(2,1)} %get-tuple-element.37.refs_4_), channel_id=1, source_target_pairs={{0,48},{16,0},{32,16},{48,32},{1,49},{17,1},{33,17},{49,33},{2,50}... | collective-permute-start | bytes 270344 | tf_op jit(solution)/shard_map/ppermute | solution.py:444
  93.0 3.3 %columns.1.tail_ref = f32[8192,128]{1,0:T(8,128)} custom-call(bf16[8,64,1664]{2,1,0:T(8,128)(2,1)} %all-to-all-done.got_ref.tail_ref), custom_call_target="tpu_custom_call" | custom-call | bytes 14400000 | tf_op jit(solution)/shard_map/columns/pallas_call | solution.py:447
  96.3 2.5 %collective-permute-done.5.refs_6_ = bf16[352,128]{1,0:T(8,128)(2,1)S(1)} collective-permute-done((bf16[352,128]{1,0:T(8,128)(2,1)}, bf16[352,128]{1,0:T(8,128)(2,1)S(1)}, u32[]{:S(2)}, u32[]{:S(2)}) %collective-permute-start.5) | collective-permute-done | bytes 90144 | tf_op jit(solution)/shard_map/ppermute | solution.py:444
  98.9 1.9 %collective-permute-done.6.refs_7_ = bf16[352,128]{1,0:T(8,128)(2,1)S(1)} collective-permute-done((bf16[352,128]{1,0:T(8,128)(2,1)}, bf16[352,128]{1,0:T(8,128)(2,1)S(1)}, u32[]{:S(2)}, u32[]{:S(2)}) %collective-permute-start.6) | collective-permute-done | bytes 90144 | tf_op jit(solution)/shard_map/ppermute | solution.py:444
  101.4 10.5 %correct.3 = bf16[8,64,1024]{2,1,0:T(8,128)(2,1)} custom-call(s32[4]{0:T(128)} %pad_add_fusion.place_ref, s32[8]{0:T(128)} %lengths_ref.7, f32[4096,128]{1,0:T(8,128)} %get-tuple-element.41.y_ref, f32[4096,128]{1,0:T(8,128)} %get-tuple-element.42.total_ref, f32[8192,128]{1,0:T(8,128)} %columns.1.tail_ref, f32[16,8192]{1,0:T(8,128)} %refs_3_.3, ...), custom_call_target="tpu_custom_call" | custom-call | bytes 32400000 | tf_op jit(solution)/shard_map/correct/pallas_call | solution.py:459
  111.9 6.1 %all-to-all-start.4 = ((bf16[8,64,1024]{2,1,0:T(8,128)(2,1)}), bf16[8,64,1024]{2,1,0:T(8,128)(2,1)}, u32[]{:S(2)}, u32[]{:S(2)}) async-start(bf16[8,64,1024]{2,1,0:T(8,128)(2,1)} %correct.3), calls=%async_computation.4 | async-start | bytes 2097152 | tf_op jit(solution)/shard_map/all_to_all | solution.py:297
  118.0 11.1 %correct.2 = (bf16[8,64,1024]{2,1,0:T(8,128)(2,1)}, bf16[2,16,256]{2,1,0:T(8,128)(2,1)}) custom-call(s32[4]{0:T(128)} %pad_add_fusion.place_ref, s32[8]{0:T(128)} %lengths_ref.7, f32[4096,128]{1,0:T(8,128)} %get-tuple-element.34.y_ref, f32[4096,128]{1,0:T(8,128)} %get-tuple-element.35.total_ref, ...), custom_call_target="tpu_custom_call" | custom-call | bytes 32400000 | tf_op jit(solution)/shard_map/correct/pallas_call | solution.py:459
  129.1 3.5 %all-to-all-done.4.back_ref = bf16[8,64,1024]{2,1,0:T(8,128)(2,1)} async-done(((bf16[8,64,1024]{2,1,0:T(8,128)(2,1)}), bf16[8,64,1024]{2,1,0:T(8,128)(2,1)}, u32[]{:S(2)}, u32[]{:S(2)}) %all-to-all-start.4) | async-done | bytes 1048608 | tf_op jit(solution)/shard_map/all_to_all | solution.py:297
  132.6 3.6 %all-to-all-start.3 = ((bf16[8,64,1024]{2,1,0:T(8,128)(2,1)}), bf16[8,64,1024]{2,1,0:T(8,128)(2,1)S(1)}, u32[]{:S(2)}, u32[]{:S(2)}) async-start(bf16[8,64,1024]{2,1,0:T(8,128)(2,1)} %get-tuple-element.38), calls=%async_computation.3 | async-start | bytes 2097152 | tf_op jit(solution)/shard_map/all_to_all | solution.py:297
  136.2 2.6 %unpack.2.refs_0_ = bf16[2,64,8192]{2,1,0:T(8,128)(2,1)} custom-call(s32[4]{0:T(128)S(1)} %copy-done.1, bf16[8,64,1024]{2,1,0:T(8,128)(2,1)} %all-to-all-done.4.back_ref), custom_call_target="tpu_custom_call" | custom-call | tf_op jit(solution)/shard_map/unpack/pallas_call | solution.py:490
  139.3 2.4 %collective-permute-start.8 = (bf16[2,16,256]{2,1,0:T(8,128)(2,1)S(1)}, bf16[2,16,256]{2,1,0:T(8,128)(2,1)S(1)}, u32[]{:S(2)}, u32[]{:S(2)}) collective-permute-start(bf16[2,16,256]{2,1,0:T(8,128)(2,1)S(1)} %copy-done.9), channel_id=1, source_target_pairs={{0,128},{64,192},{128,0},{192,64},{1,129},{65,193},{129,1},{193,65... | collective-permute-start | bytes 49160 | tf_op jit(solution)/shard_map/ppermute | solution.py:510
  141.7 1.9 %collective-permute-start.7 = (bf16[2,16,256]{2,1,0:T(8,128)(2,1)S(1)}, bf16[2,16,256]{2,1,0:T(8,128)(2,1)S(1)}, u32[]{:S(2)}, u32[]{:S(2)}) collective-permute-start(bf16[2,16,256]{2,1,0:T(8,128)(2,1)S(1)} %copy-done.9), channel_id=1, source_target_pairs={{0,64},{64,128},{128,192},{192,0},{1,65},{65,129},{129,193},{193,1... | collective-permute-start | bytes 49160 | tf_op jit(solution)/shard_map/ppermute | solution.py:510
  146.8 4.4 %all-to-all-done.3.back_ref = bf16[8,64,1024]{2,1,0:T(8,128)(2,1)S(1)} async-done(((bf16[8,64,1024]{2,1,0:T(8,128)(2,1)}), bf16[8,64,1024]{2,1,0:T(8,128)(2,1)S(1)}, u32[]{:S(2)}, u32[]{:S(2)}) %all-to-all-start.3) | async-done | bytes 1048608 | tf_op jit(solution)/shard_map/all_to_all | solution.py:297
  151.2 1.7 %unpack.3 = bf16[2,64,8192]{2,1,0:T(8,128)(2,1)} custom-call(s32[4]{0:T(128)S(1)} %copy-done.1, bf16[8,64,1024]{2,1,0:T(8,128)(2,1)S(1)} %all-to-all-done.3.back_ref, bf16[2,64,8192]{2,1,0:T(8,128)(2,1)} %unpack.2.refs_0_), custom_call_target="tpu_custom_call", output_to_operand_aliasing={{}: (2, {})} | custom-call | tf_op jit(solution)/shard_map/unpack/pallas_call | solution.py:490
  (62 shorter events, 12.1 us)
Async XLA Ops:
  0.6 13.8 %copy-start = (bf16[2,64,512]{2,1,0:T(8,128)(2,1)S(1)}, bf16[2,64,512]{2,1,0:T(8,128)(2,1)}, u32[]{:S(2)}) copy-start(bf16[2,64,512]{2,1,0:T(8,128)(2,1)} %param.13) | copy-start | bytes 393220
  0.6 15.0 %copy-start.2 = (s32[8,1]{0,1:T(1,128)S(1)}, s32[8,1]{0,1:T(1,128)}, u32[]{:S(2)}) copy-start(s32[8,1]{0,1:T(1,128)} %param.20) | copy-start | bytes 100
  0.7 15.1 %copy-start.10 = (s32[8]{0:T(128)S(1)}, s32[8]{0:T(128)}, u32[]{:S(2)}) copy-start(s32[8]{0:T(128)} %param.21) | copy-start | bytes 100
  2.4 24.0 %all-to-all-start.1 = ((bf16[32,16,256]{2,1,0:T(8,128)(2,1)}), bf16[32,16,256]{2,1,0:T(8,128)(2,1)S(1)}, u32[]{:S(2)}, u32[]{:S(2)}) async-start(bf16[32,16,256]{2,1,0:T(8,128)(2,1)} %spread.1), calls=%async_computation.1 | async-start | bytes 524288 | tf_op jit(solution)/shard_map/all_to_all | solution.py:297
  21.4 10.4 %copy-start.8 = (bf16[1,8,16,256]{3,2,1,0:T(8,128)(2,1)S(1)}, bf16[1,8,16,256]{3,2,1,0:T(8,128)(2,1)}, u32[]{:S(2)}) copy-start(bf16[1,8,16,256]{3,2,1,0:T(8,128)(2,1)} %copy.22) | copy-start | bytes 196612
  26.4 7.0 %copy-start.4 = (bf16[32,16,256]{2,1,0:T(8,128)(2,1)}, bf16[32,16,256]{2,1,0:T(8,128)(2,1)S(1)}, u32[]{:S(2)}) copy-start(bf16[32,16,256]{2,1,0:T(8,128)(2,1)S(1)} %all-to-all-done.1) | copy-start | bytes 786436
  26.4 24.6 %all-to-all-start = ((bf16[8,64,1664]{2,1,0:T(8,128)(2,1)}), bf16[8,64,1664]{2,1,0:T(8,128)(2,1)}, u32[]{:S(2)}, u32[]{:S(2)}) async-start(bf16[8,64,1664]{2,1,0:T(8,128)(2,1)} %pack.3), calls=%async_computation | async-start | bytes 3407872 | tf_op jit(solution)/shard_map/all_to_all | solution.py:297
  32.4 8.9 %copy-start.3 = (s32[1,64]{1,0:T(1,128)S(1)}, s32[1,64]{1,0:T(1,128)}, u32[]{:S(2)}) copy-start(s32[1,64]{1,0:T(1,128)} %param.22) | copy-start | bytes 772
  33.4 9.9 %collective-permute-start = (bf16[544,256]{1,0:T(8,128)(2,1)}, bf16[544,256]{1,0:T(8,128)(2,1)}, u32[]{:S(2)}, u32[]{:S(2)}) collective-permute-start(bf16[544,256]{1,0:T(8,128)(2,1)} %get-tuple-element.56), channel_id=1, source_target_pairs={{0,64},{64,128},{128,192},{192,0},{1,65},{65,129},{129,193},{193,1... | collective-permute-start | bytes 835592 | tf_op jit(solution)/shard_map/ppermute | solution.py:363
  34.9 11.2 %collective-permute-start.1 = (bf16[544,256]{1,0:T(8,128)(2,1)}, bf16[544,256]{1,0:T(8,128)(2,1)}, u32[]{:S(2)}, u32[]{:S(2)}) collective-permute-start(bf16[544,256]{1,0:T(8,128)(2,1)} %get-tuple-element.55), channel_id=1, source_target_pairs={{0,128},{64,192},{128,0},{192,64},{1,129},{65,193},{129,1},{193,65... | collective-permute-start | bytes 835592 | tf_op jit(solution)/shard_map/ppermute | solution.py:363
  35.9 12.4 %collective-permute-start.2 = (bf16[544,256]{1,0:T(8,128)(2,1)}, bf16[544,256]{1,0:T(8,128)(2,1)}, u32[]{:S(2)}, u32[]{:S(2)}) collective-permute-start(bf16[544,256]{1,0:T(8,128)(2,1)} %get-tuple-element.54), channel_id=1, source_target_pairs={{0,192},{64,0},{128,64},{192,128},{1,193},{65,1},{129,65},{193,129... | collective-permute-start | bytes 835592 | tf_op jit(solution)/shard_map/ppermute | solution.py:363
  51.0 19.7 %all-to-all-start.2 = ((bf16[8,64,1024]{2,1,0:T(8,128)(2,1)}), bf16[8,64,1024]{2,1,0:T(8,128)(2,1)}, u32[]{:S(2)}, u32[]{:S(2)}) async-start(bf16[8,64,1024]{2,1,0:T(8,128)(2,1)} %pack.2), calls=%async_computation.2 | async-start | bytes 2097152 | tf_op jit(solution)/shard_map/all_to_all | solution.py:297
  55.3 15.5 %collective-permute-start.3 = (bf16[8,64,1664]{2,1,0:T(8,128)(2,1)}, bf16[8,64,1664]{2,1,0:T(8,128)(2,1)}, u32[]{:S(2)}, u32[]{:S(2)}) collective-permute-start(bf16[8,64,1664]{2,1,0:T(8,128)(2,1)} %all-to-all-done.got_ref.tail_ref), channel_id=1, source_target_pairs={{0,1},{1,0},{2,3},{3,2},{4,5},{5,4},{6,7},{7,6},{8,9},{9,8},{10,11... | collective-permute-start | bytes 5111816 | tf_op jit(solution)/shard_map/ppermute | solution.py:376
  86.5 9.8 %collective-permute-start.4 = (bf16[352,128]{1,0:T(8,128)(2,1)}, bf16[352,128]{1,0:T(8,128)(2,1)S(1)}, u32[]{:S(2)}, u32[]{:S(2)}) collective-permute-start(bf16[352,128]{1,0:T(8,128)(2,1)} %get-tuple-element.37.refs_4_), channel_id=1, source_target_pairs={{0,16},{16,32},{32,48},{48,0},{1,17},{17,33},{33,49},{49,1},{2,18}... | collective-permute-start | bytes 270344 | tf_op jit(solution)/shard_map/ppermute | solution.py:444
  88.4 10.5 %collective-permute-start.5 = (bf16[352,128]{1,0:T(8,128)(2,1)}, bf16[352,128]{1,0:T(8,128)(2,1)S(1)}, u32[]{:S(2)}, u32[]{:S(2)}) collective-permute-start(bf16[352,128]{1,0:T(8,128)(2,1)} %get-tuple-element.37.refs_4_), channel_id=1, source_target_pairs={{0,32},{16,48},{32,0},{48,16},{1,33},{17,49},{33,1},{49,17},{2,34}... | collective-permute-start | bytes 270344 | tf_op jit(solution)/shard_map/ppermute | solution.py:444
  90.8 9.9 %collective-permute-start.6 = (bf16[352,128]{1,0:T(8,128)(2,1)}, bf16[352,128]{1,0:T(8,128)(2,1)S(1)}, u32[]{:S(2)}, u32[]{:S(2)}) collective-permute-start(bf16[352,128]{1,0:T(8,128)(2,1)} %get-tuple-element.37.refs_4_), channel_id=1, source_target_pairs={{0,48},{16,0},{32,16},{48,32},{1,49},{17,1},{33,17},{49,33},{2,50}... | collective-permute-start | bytes 270344 | tf_op jit(solution)/shard_map/ppermute | solution.py:444
  96.3 4.4 %copy-start.5 = (bf16[352,128]{1,0:T(8,128)(2,1)}, bf16[352,128]{1,0:T(8,128)(2,1)S(1)}, u32[]{:S(2)}) copy-start(bf16[352,128]{1,0:T(8,128)(2,1)S(1)} %collective-permute-done.4.refs_5_) | copy-start | bytes 270340
  98.9 1.9 %copy-start.6 = (bf16[352,128]{1,0:T(8,128)(2,1)}, bf16[352,128]{1,0:T(8,128)(2,1)S(1)}, u32[]{:S(2)}) copy-start(bf16[352,128]{1,0:T(8,128)(2,1)S(1)} %collective-permute-done.5.refs_6_) | copy-start | bytes 270340
  100.7 0.6 copy-start.7
  111.9 20.7 %all-to-all-start.4 = ((bf16[8,64,1024]{2,1,0:T(8,128)(2,1)}), bf16[8,64,1024]{2,1,0:T(8,128)(2,1)}, u32[]{:S(2)}, u32[]{:S(2)}) async-start(bf16[8,64,1024]{2,1,0:T(8,128)(2,1)} %correct.3), calls=%async_computation.4 | async-start | bytes 2097152 | tf_op jit(solution)/shard_map/all_to_all | solution.py:297
  129.1 7.1 %copy-start.1 = (s32[4]{0:T(128)S(1)}, s32[4]{0:T(128)}, u32[]{:S(2)}) copy-start(s32[4]{0:T(128)} %pad_add_fusion.place_ref) | copy-start | bytes 52
  132.6 18.6 %all-to-all-start.3 = ((bf16[8,64,1024]{2,1,0:T(8,128)(2,1)}), bf16[8,64,1024]{2,1,0:T(8,128)(2,1)S(1)}, u32[]{:S(2)}, u32[]{:S(2)}) async-start(bf16[8,64,1024]{2,1,0:T(8,128)(2,1)} %get-tuple-element.38), calls=%async_computation.3 | async-start | bytes 2097152 | tf_op jit(solution)/shard_map/all_to_all | solution.py:297
  136.2 2.6 %copy-start.9 = (bf16[2,16,256]{2,1,0:T(8,128)(2,1)S(1)}, bf16[2,16,256]{2,1,0:T(8,128)(2,1)}, u32[]{:S(2)}) copy-start(bf16[2,16,256]{2,1,0:T(8,128)(2,1)} %get-tuple-element.44) | copy-start | bytes 49156
  138.9 4.8 %collective-permute-start.9 = (bf16[2,16,256]{2,1,0:T(8,128)(2,1)S(1)}, bf16[2,16,256]{2,1,0:T(8,128)(2,1)S(1)}, u32[]{:S(2)}, u32[]{:S(2)}) collective-permute-start(bf16[2,16,256]{2,1,0:T(8,128)(2,1)S(1)} %copy-done.9), channel_id=1, source_target_pairs={{0,192},{64,0},{128,64},{192,128},{1,193},{65,1},{129,65},{193,129... | collective-permute-start | bytes 49160 | tf_op jit(solution)/shard_map/ppermute | solution.py:510
  139.3 5.2 %collective-permute-start.8 = (bf16[2,16,256]{2,1,0:T(8,128)(2,1)S(1)}, bf16[2,16,256]{2,1,0:T(8,128)(2,1)S(1)}, u32[]{:S(2)}, u32[]{:S(2)}) collective-permute-start(bf16[2,16,256]{2,1,0:T(8,128)(2,1)S(1)} %copy-done.9), channel_id=1, source_target_pairs={{0,128},{64,192},{128,0},{192,64},{1,129},{65,193},{129,1},{193,65... | collective-permute-start | bytes 49160 | tf_op jit(solution)/shard_map/ppermute | solution.py:510
  141.7 3.7 %collective-permute-start.7 = (bf16[2,16,256]{2,1,0:T(8,128)(2,1)S(1)}, bf16[2,16,256]{2,1,0:T(8,128)(2,1)S(1)}, u32[]{:S(2)}, u32[]{:S(2)}) collective-permute-start(bf16[2,16,256]{2,1,0:T(8,128)(2,1)S(1)} %copy-done.9), channel_id=1, source_target_pairs={{0,64},{64,128},{128,192},{192,0},{1,65},{65,129},{129,193},{193,1... | collective-permute-start | bytes 49160 | tf_op jit(solution)/shard_map/ppermute | solution.py:510
